TPU v7x, 32 devices: a whole 2x2x4 slice. The times are simulated.
32 devices in a mesh: dp: 4 (over y, x), tensor: 8 (over z, core).
Axes of the slice: x: 2, y: 2, z: 4, core: 2. Of those that a mesh axis runs over, the one named last changes fastest.
Arguments:
- enc_tokens: bfloat16 [32, 128, 1024], P(('dp', 'tensor')), may hold values from -6 to 6
- src_lengths: int32 [32], replicated, may hold values from 1 to 128, as said below
- enc_gain: float32 [1024], replicated, may hold values from 0.1 to 1.9
- enc_query: bfloat16 [1024, 8192], P(None, 'tensor'), may hold values from -0.1875 to 0.1875
- enc_key: bfloat16 [1024, 8192], P(None, 'tensor'), may hold values from -0.1875 to 0.1875
- enc_value: bfloat16 [1024, 8192], P(None, 'tensor'), may hold values from -0.1875 to 0.1875
- enc_output: bfloat16 [8192, 1024], P('tensor'), may hold values from -0.0625 to 0.0625
- enc_bias: float32 [64, 33], P('tensor'), may hold values from -3 to 260
- mem_gain: float32 [1024], replicated, may hold values from 0.1 to 1.9
- dec_tokens: bfloat16 [32, 64, 1024], P(('dp', 'tensor')), may hold values from -6 to 6
- tgt_lengths: int32 [32], P(('dp', 'tensor')), may hold values from 1 to 64
- lang_tags: int32 [32], P('dp'), may hold values from 0 to 7
- lang_table: bfloat16 [8, 1024], replicated, may hold values from -6 to 6
- cross_gain: float32 [1024], replicated, may hold values from 0.1 to 1.9
- cross_query: bfloat16 [1024, 8192], P(None, 'tensor'), may hold values from -0.1875 to 0.1875
- cross_key: bfloat16 [1024, 8192], P(None, 'tensor'), may hold values from -0.1875 to 0.1875
- cross_value: bfloat16 [1024, 8192], P(None, 'tensor'), may hold values from -0.1875 to 0.1875
- cross_output: bfloat16 [8192, 1024], P('tensor'), may hold values from -0.0625 to 0.0625
- ffn_gain: float32 [1024], replicated, may hold values from 0.1 to 1.9
- ffn_in: bfloat16 [1024, 32768], P(None, 'tensor'), may hold values from -0.1875 to 0.1875
- ffn_out: bfloat16 [32768, 1024], P('tensor'), may hold values from -0.03125 to 0.03125
Outputs:
- enc_memory: bfloat16 [32, 128, 1024], P(('dp', 'tensor'))
- dec_out: bfloat16 [32, 64, 1024], P(('dp', 'tensor'))
Inputs may be any that keep to these rules, and one draw needn't show every extreme that they name: `src_lengths`: never falling along the batch; the first is 1 and the last is 128.
All inputs are finite; a program needn't handle non-finite values.
Results may differ from a plain program's by a relative error of at most 0.014.
Values may be sent and summed in bfloat16 or wider, within the bound.
No kernel may reach another device: no remote copies, remote signals or barrier semaphores. Data moves between devices by JAX's collectives and lax.ppermute only.
A program may use at most 128 MiB of HBM per device.

v0:
```python
import functools

import jax
import jax.numpy as jnp
from jax import lax
from jax.experimental import pallas as pl
from jax.experimental.pallas import tpu as pltpu
from jax.sharding import PartitionSpec as P

HD = 128
MAXREL = 16
NB = 33
LANG_ROWS = 16
TIE_OWN = True
TIE_NEAR = False
EPSILON = 1e-06
NEG_FILL = -1e30
FFN_STEP = 512
OUT_STEP = 256
VMEM_LIMIT = 16 * 1024 * 1024

IN_VMEM = pl.BlockSpec(memory_space=pltpu.VMEM)
IN_HBM = pl.BlockSpec(memory_space=pltpu.HBM)
IN_SMEM = pl.BlockSpec(memory_space=pltpu.SMEM)
BF16 = jnp.bfloat16
F32 = jnp.float32


def rms_norm(values, norm_gain):
    mean_sq = jnp.mean(values * values, axis=-1, keepdims=True)
    return values * lax.rsqrt(mean_sq + EPSILON) * norm_gain


def after(value, *earlier):
    return lax.optimization_barrier((value,) + earlier)[0]


def in_hbm(*arrays):
    return [pltpu.with_memory_space_constraint(array, pltpu.HBM) for array in arrays]


def load_body(count, *refs):
    sources = refs[:count + 1]
    targets, bias = refs[count + 2:2 * count + 2], refs[2 * count + 2]
    table, sems = refs[2 * count + 3:]
    copies = [
        pltpu.make_async_copy(source, target, sems.at[i])
        for i, (source, target) in enumerate(zip(sources, [*targets, table]))
    ]
    for copy in copies[::-1]:
        copy.start()
    copies.pop().wait()
    heads, query_len, key_len = bias.shape
    shape = (query_len, key_len)
    offset = lax.broadcasted_iota(jnp.int32, shape, 1) - lax.broadcasted_iota(jnp.int32, shape, 0)
    bucket = jnp.clip(offset, -MAXREL, MAXREL) + MAXREL
    for h in range(heads):
        grid = jnp.full(shape, table[h, 0], F32)
        for n in range(1, NB):
            grid = jnp.where(bucket == n, table[h, n], grid)
        bias[h] = grid
    for copy in copies:
        copy.wait()


def load(weights, bias_table, query_len, key_len, earlier):
    count = len(weights)
    heads = bias_table.shape[0]
    size = sum(w.size * w.dtype.itemsize for w in weights)
    return pl.pallas_call(
        functools.partial(load_body, count),
        in_specs=[IN_HBM] * (count + 1) + [IN_VMEM],
        out_specs=[IN_VMEM] * (count + 1),
        out_shape=[jax.ShapeDtypeStruct(w.shape, w.dtype) for w in weights]
        + [jax.ShapeDtypeStruct((heads, query_len, key_len), F32)],
        scratch_shapes=[
            pltpu.SMEM(bias_table.shape, bias_table.dtype),
            pltpu.SemaphoreType.DMA((count + 1,)),
        ],
        compiler_params=pltpu.CompilerParams(vmem_limit_bytes=VMEM_LIMIT),
        cost_estimate=pl.CostEstimate(flops=0, bytes_accessed=2 * size, transcendentals=0),
        name="load",
    )(*in_hbm(*weights, bias_table), earlier)


def dot(a, b):
    return jnp.dot(a, b, preferred_element_type=F32)


def softmax_contexts(query, key, value, bias, masks, parts):
    query_len, key_len = query.shape[0] // parts, key.shape[0] // parts
    ones = jnp.ones((key_len, HD), BF16)
    units = [(i, h) for i in range(parts) for h in range(query.shape[1] // HD)]

    def take(rows, length, unit):
        i, h = unit
        return rows[i * length:(i + 1) * length, h * HD:(h + 1) * HD]

    scores = [
        lax.dot_general(
            take(query, query_len, unit), take(key, key_len, unit), (((1,), (1,)), ((), ())),
            preferred_element_type=F32,
        )
        for unit in units
    ]
    scores = [score * HD ** (-0.5) for score in scores]
    if bias is not None:
        scores = [score + bias[h] for (_, h), score in zip(units, scores)]
    scores = [jnp.where(masks[i], score, NEG_FILL) for (i, _), score in zip(units, scores)]
    row_max = [jnp.max(score, axis=-1, keepdims=True) for score in scores]
    exponent = [jnp.exp(score - top).astype(BF16) for score, top in zip(scores, row_max)]
    summed = [
        dot(part, jnp.concatenate([take(value, key_len, unit), ones], axis=1))
        for unit, part in zip(units, exponent)
    ]
    context = [(total[:, :HD] / total[:, HD:]).astype(BF16) for total in summed]
    heads = len(units) // parts
    return jnp.concatenate(
        [jnp.concatenate(context[i * heads:(i + 1) * heads], axis=1) for i in range(parts)], axis=0
    )


def attention_body(has_bias, parts, first_slot, size, *refs):
    refs = list(refs)
    lengths = refs.pop(0)
    key_parts = [refs.pop(0) for _ in range(parts)]
    queries_in = [] if has_bias else [refs.pop(0), refs.pop(0)]
    wq, wk, wv, wo = [refs.pop(0) for _ in range(4)]
    bias = refs.pop(0) if has_bias else None
    outs = refs
    key_len, query_len = key_parts[0].shape[0], outs[0].shape[0]
    key_rows = jnp.concatenate([ref[...] for ref in key_parts], axis=0)
    query_rows = key_rows
    first = lax.axis_index("dp") * size
    here = lax.axis_index("tensor")
    if not has_bias:
        query_rows = jnp.concatenate(
            [queries_in[i][first_slot // 2] for i in range(parts)], axis=0
        )
    key_index = lax.broadcasted_iota(jnp.int32, (query_len, key_len), 1)
    masks = [key_index < lengths[first + (here ^ (first_slot + i))] for i in range(parts)]
    keys = dot(key_rows, wk[...]).astype(BF16)
    values = dot(key_rows, wv[...]).astype(BF16)
    queries = dot(query_rows, wq[...]).astype(BF16)
    context = softmax_contexts(queries, keys, values, bias, masks, parts)
    term = dot(context, wo[...]).astype(BF16)
    for i in range(parts):
        outs[i][...] = term[i * query_len:(i + 1) * query_len]


def attention(lengths, first_slot, key_parts, queries_in, wq, wk, wv, wo, bias):
    parts = len(key_parts)
    key_len, width = key_parts[0].shape
    query_len = queries_in[0].shape[1] if queries_in else key_len
    columns = wq.shape[1]
    has_bias = bias is not None
    operands = list(key_parts)
    if queries_in:
        operands += queries_in
    operands += [wq, wk, wv, wo]
    if has_bias:
        operands += [bias]
    rows_q, rows_k = parts * query_len, parts * key_len
    return pl.pallas_call(
        functools.partial(
            attention_body, has_bias, parts, first_slot, lax.axis_size("tensor")
        ),
        in_specs=[IN_SMEM] + [IN_VMEM] * len(operands),
        out_specs=[IN_VMEM] * parts,
        out_shape=[jax.ShapeDtypeStruct((query_len, width), BF16)] * parts,
        compiler_params=pltpu.CompilerParams(vmem_limit_bytes=VMEM_LIMIT),
        cost_estimate=pl.CostEstimate(
            flops=4 * width * columns * (rows_q + rows_k) + 4 * rows_q * key_len * columns,
            bytes_accessed=4 * width * (rows_q + rows_k),
            transcendentals=0,
        ),
        name="enc_attention" if has_bias else "cross_attention",
    )(lengths, *operands)


def ffn_body(parts, *refs):
    row_parts = refs[:parts]
    w_in, w_out = refs[parts:parts + 2]
    outs = refs[parts + 2:2 * parts + 2]
    (activated,) = refs[2 * parts + 2:]
    part_len = row_parts[0].shape[0]
    rows = jnp.concatenate([ref[...] for ref in row_parts], axis=0)
    block = min(FFN_STEP, w_in.shape[1])
    for start in range(0, w_in.shape[1], block):
        cols = slice(start, start + block)
        activated[:, cols] = jnp.maximum(dot(rows, w_in[:, cols]), 0.0).astype(BF16)
    block = min(OUT_STEP, w_out.shape[1])
    for start in range(0, w_out.shape[1], block):
        cols = slice(start, start + block)
        term = dot(activated[...], w_out[:, cols]).astype(BF16)
        for i in range(parts):
            outs[i][:, cols] = term[i * part_len:(i + 1) * part_len]


def ffn(row_parts, w_in, w_out):
    parts = len(row_parts)
    part_len, width = row_parts[0].shape
    hidden = w_in.shape[1]
    rows = parts * part_len
    return pl.pallas_call(
        functools.partial(ffn_body, parts),
        in_specs=[IN_VMEM] * (parts + 2),
        out_specs=[IN_VMEM] * parts,
        out_shape=[jax.ShapeDtypeStruct((part_len, width), BF16)] * parts,
        scratch_shapes=[pltpu.VMEM((rows, hidden), BF16)],
        compiler_params=pltpu.CompilerParams(vmem_limit_bytes=VMEM_LIMIT),
        cost_estimate=pl.CostEstimate(
            flops=4 * rows * width * hidden,
            bytes_accessed=4 * rows * width,
            transcendentals=0,
        ),
        name="feed_forward",
    )(*row_parts, w_in, w_out)


def swap(value, bits):
    size = lax.axis_size("tensor")
    return lax.ppermute(value, "tensor", [(i, i ^ bits) for i in range(size)])


def spread(block):
    size = lax.axis_size("tensor")
    slots = {0: block}
    bit = size // 2
    while bit > 1:
        for k in sorted(slots):
            slots[k ^ bit] = swap(slots[k], bit)
        bit //= 2
    own = jnp.stack([slots[2 * k] for k in range(size // 2)])
    return own, swap(own, 1), [slots[size // 2], slots[size // 4]]


def bf16_sum(*terms):
    total = terms[0].astype(F32)
    for term in terms[1:]:
        total = total + term.astype(F32)
    return total.astype(BF16)


def exchange(block, run, before_last=()):
    size = lax.axis_size("tensor")
    last = size // 2 - 1
    outs = {0: run(0, [block, swap(block, 1)])}
    addends = [outs[0][0], swap(outs[0][1], 1)]
    slots = {0: block}
    bit = size // 2
    while bit > 1:
        for k in sorted(slots):
            slots[k ^ bit] = swap(slots[k], bit)
        bit //= 2
        if bit > 1:
            for k in sorted(slots):
                if k:
                    slots[k] = after(slots[k], outs[0][0])
    near, held = {}, [addends[1]] if TIE_OWN else [outs[0][0]]
    for k in [*range(2, last, 2), *range(1, last + 1, 2)]:
        first = slots[2 * k]
        if k == last:
            held += before_last
        if k in near and TIE_NEAR:
            held.append(near[k])
        outs[k] = run(k, [after(first, *held), swap(after(first, *held) if k == last else first, 1)])
        held = [outs[k][0]]
        terms = [outs[k][0], swap(outs[k][1], 1)]
        if k in near:
            terms.append(near[k])
        partial_sum = bf16_sum(*terms)
        if k % 2:
            addends.append(swap(partial_sum, 2 * k))
        else:
            near[k + 1] = swap(partial_sum, 2)
    return addends


def prologue_body(tokens, gain, dec_rows, table, tags, ends, normed, sent, *scratch):
    buffers, sems = scratch[:6], scratch[6]
    copies = [
        pltpu.make_async_copy(source, target, sems.at[i])
        for i, (source, target) in enumerate(
            zip((tokens, gain, dec_rows, table, tags, ends), buffers)
        )
    ]
    for copy in copies:
        copy.start()
    for copy in copies:
        copy.wait()
    normed[...] = rms_norm(buffers[0][...].astype(F32), buffers[1][...]).astype(BF16)
    count = dec_rows.shape[0]
    sent[:count, :] = buffers[2][...]
    langs, width = table.shape
    tag = buffers[4][lax.axis_index("tensor")]
    chosen = lax.broadcasted_iota(jnp.int32, (langs, width), 0) == tag
    row = jnp.sum(jnp.where(chosen, buffers[3][...].astype(F32), 0.0), axis=0, keepdims=True)
    shape = (sent.shape[0] - count, width)
    end = jnp.full(shape, buffers[5][0], jnp.int32).astype(F32)
    is_row = lax.broadcasted_iota(jnp.int32, shape, 0) == 0
    sent[count:, :] = jnp.where(is_row, jnp.broadcast_to(row, shape), end).astype(BF16)


def prologue(tokens, gain, dec_rows, table, tags, ends):
    (rows, width), count = tokens.shape, dec_rows.shape[0]
    operands = [tokens, gain[None, :], dec_rows, table, tags, ends]
    return pl.pallas_call(
        prologue_body,
        in_specs=[IN_HBM] * 6,
        out_specs=[IN_VMEM] * 2,
        out_shape=[
            jax.ShapeDtypeStruct((rows, width), BF16),
            jax.ShapeDtypeStruct((count + LANG_ROWS, width), BF16),
        ],
        scratch_shapes=[pltpu.VMEM(x.shape, x.dtype) for x in operands[:4]]
        + [pltpu.SMEM(x.shape, x.dtype) for x in operands[4:]]
        + [pltpu.SemaphoreType.DMA((6,))],
        compiler_params=pltpu.CompilerParams(vmem_limit_bytes=VMEM_LIMIT),
        name="prologue",
    )(*in_hbm(*operands[:4]), *operands[4:])


def norm_body(count, copies, *refs):
    addends = refs[:count]
    gain = refs[count]
    outs = refs[count + 1:]
    total = addends[0][...].astype(F32)
    for ref in addends[1:]:
        total = total + ref[...].astype(F32)
    normed = rms_norm(total, gain[...]).astype(BF16)
    for ref in outs[:copies]:
        ref[...] = normed
    for ref in outs[copies:]:
        ref[...] = total


def norm_sum(addends, gain, copies, with_sum):
    rows, width = addends[0].shape
    out_shape = [jax.ShapeDtypeStruct((rows, width), BF16)] * copies
    if with_sum:
        out_shape.append(jax.ShapeDtypeStruct((rows, width), F32))
    return pl.pallas_call(
        functools.partial(norm_body, len(addends), copies),
        out_shape=out_shape,
        compiler_params=pltpu.CompilerParams(vmem_limit_bytes=VMEM_LIMIT),
        cost_estimate=pl.CostEstimate(
            flops=8 * rows * width,
            bytes_accessed=2 * rows * width * (len(addends) + 3),
            transcendentals=rows,
        ),
        name="sum_norm",
    )(*addends, gain[None, :])


def masked_body(count, *refs):
    addends, ends, out = refs[:count], refs[count], refs[count + 1]
    total = addends[0][...].astype(F32)
    for ref in addends[1:]:
        total = total + ref[...].astype(F32)
    row = lax.broadcasted_iota(jnp.int32, total.shape, 0).astype(F32)
    keep = row < ends[:, :1].astype(F32)
    out[...] = jnp.where(keep, total, 0.0).astype(BF16)


def masked_sum(addends, ends):
    rows, width = addends[0].shape
    return pl.pallas_call(
        functools.partial(masked_body, len(addends)),
        out_shape=jax.ShapeDtypeStruct((rows, width), BF16),
        compiler_params=pltpu.CompilerParams(vmem_limit_bytes=VMEM_LIMIT),
        name="masked_sum",
    )(*addends, ends)


def on_device(
    enc_tokens,
    src_lengths,
    enc_gain,
    enc_query,
    enc_key,
    enc_value,
    enc_output,
    enc_bias,
    mem_gain,
    dec_tokens,
    tgt_lengths,
    lang_tags,
    lang_table,
    cross_gain,
    cross_query,
    cross_key,
    cross_value,
    cross_output,
    ffn_gain,
    ffn_in,
    ffn_out,
):
    groups = lax.axis_size("dp")
    size = lax.axis_size("tensor")
    per_pair = size // groups
    src_len = enc_tokens.shape[1]
    target_len = dec_tokens.shape[1]

    to_source = []
    for row in range(groups * size):
        j, m = row // size, row % size
        to_source.append((row, (m // per_pair) * size + (m % per_pair) * groups + j))
    to_home = [(b, a) for a, b in to_source]

    enc_normed, sent = prologue(
        enc_tokens[0], enc_gain, dec_tokens[0], lang_table, lang_tags, tgt_lengths
    )
    *enc_weights, bias = load(
        [enc_query, enc_key, enc_value, enc_output], enc_bias, src_len, src_len, enc_normed
    )

    arrived = lax.ppermute(sent, ("dp", "tensor"), to_source)
    dec_rows = arrived[:target_len]
    dec_lang = jnp.broadcast_to(arrived[target_len:target_len + 1], dec_rows.shape)
    dec_normed, dec_input = norm_sum([dec_rows, dec_lang], cross_gain, 1, True)
    def enc_pair(k, blocks):
        return attention(src_lengths, 2 * k, blocks, None, *enc_weights, bias)

    dec_own, dec_other, early = spread(dec_normed)
    enc_terms = exchange(enc_normed, enc_pair, early)
    memory_out, enc_memory = norm_sum([enc_tokens[0]] + enc_terms, mem_gain, 2, False)

    def cross_pair(k, blocks):
        return attention(
            src_lengths, 2 * k, blocks, [dec_own, dec_other],
            cross_query, cross_key, cross_value, cross_output, None,
        )

    cross_terms = exchange(enc_memory, cross_pair)
    ffn_normed, hidden = norm_sum([dec_input] + cross_terms, ffn_gain, 1, True)

    def ffn_pair(k, blocks):
        return ffn(blocks, ffn_in, ffn_out)

    ffn_terms = exchange(ffn_normed, ffn_pair)
    ends = jnp.broadcast_to(arrived[target_len + 1:target_len + 2, :HD], (target_len, HD))
    dec_sum = masked_sum([hidden] + ffn_terms, ends)
    dec_out = lax.ppermute(dec_sum, ("dp", "tensor"), to_home)
    return (memory_out[None], dec_out[None])


def solution(mesh):
    in_specs = (
        P(("dp", "tensor"), None, None),
        P(),
        P(),
        P(None, "tensor"),
        P(None, "tensor"),
        P(None, "tensor"),
        P("tensor", None),
        P("tensor", None),
        P(),
        P(("dp", "tensor"), None, None),
        P(("dp", "tensor")),
        P("dp"),
        P(),
        P(),
        P(None, "tensor"),
        P(None, "tensor"),
        P(None, "tensor"),
        P("tensor", None),
        P(),
        P(None, "tensor"),
        P("tensor", None),
    )
    out_specs = (P(("dp", "tensor"), None, None), P(("dp", "tensor"), None, None))
    return jax.shard_map(
        on_device, mesh=mesh, in_specs=in_specs, out_specs=out_specs, check_vma=False
    )
```

profile of v0, /device:TPU:4, one launch (start us, length us, event | category | flops | bytes accessed | tf_op | source)
XLA Modules:
  0.0 147.7 jit_solution(1864149447837112023)
XLA Ops:
  1.3 0.6 copy-done.9
  1.9 1.2 prologue.1
  3.3 2.7 %collective-permute-start.3 = (bf16[128,1024]{1,0:T(8,128)(2,1)S(1)}, bf16[128,1024]{1,0:T(8,128)(2,1)S(1)}, u32[]{:S(2)}, u32[]{:S(2)}) collective-permute-start(bf16[128,1024]{1,0:T(8,128)(2,1)S(1)} %get-tuple-element.51.refs_5_.refs_1_), channel_id=1, source_target_pairs={{0,4},{1,5},{2,6},{3,7},{4,0},{5,1},{6,2},{7,3},{8,12},{9,13},{10,... | collective-permute-start | bytes 786440 | tf_op jit(solution)/shard_map/ppermute | solution.py:223
  5.9 1.6 %collective-permute-start.2 = (bf16[128,1024]{1,0:T(8,128)(2,1)S(1)}, bf16[128,1024]{1,0:T(8,128)(2,1)S(1)}, u32[]{:S(2)}, u32[]{:S(2)}) collective-permute-start(bf16[128,1024]{1,0:T(8,128)(2,1)S(1)} %get-tuple-element.51.refs_5_.refs_1_), channel_id=1, source_target_pairs={{0,2},{1,3},{2,0},{3,1},{4,6},{5,7},{6,4},{7,5},{8,10},{9,11},{10,... | collective-permute-start | bytes 786440 | tf_op jit(solution)/shard_map/ppermute | solution.py:223
  7.5 3.5 %load.1 = (bf16[1024,1024]{1,0:T(8,128)(2,1)S(1)}, bf16[1024,1024]{1,0:T(8,128)(2,1)S(1)}, bf16[1024,1024]{1,0:T(8,128)(2,1)S(1)}, bf16[1024,1024]{1,0:T(8,128)(2,1)S(1)}, f32[8,128,128]{2,1,0:T(8,128)S(1)}) custom-call(bf16[1024,1024]{1,0:T(8,128)(2,1)} %refs_0_.9, bf16[1024,1024]{1,0:T(8,128)(2,1)} %refs_1_.1, bf16[1024,1024]{1,0:T(8,128)(2,1)} %refs_2_.5, ...), custom_call_target="tpu_custom_call" | custom-call | bytes 16777216 | tf_op jit(solution)/shard_map/load/pallas_call | solution.py:70
  11.0 3.6 %enc_attention.4 = (bf16[128,1024]{1,0:T(8,128)(2,1)S(1)}, bf16[128,1024]{1,0:T(8,128)(2,1)S(1)}) custom-call(s32[32]{0:T(128)S(1)} %copy-done.5, bf16[128,1024]{1,0:T(8,128)(2,1)S(1)} %get-tuple-element.51.refs_5_.refs_1_, bf16[128,1024]{1,0:T(8,128)(2,1)S(1)} %collective-permute-done.refs_2_, bf16[1024,1024]{1,0:T(8,128)(2,1)S(1)} %get-tuple-element.52.refs_3_, ...), custom_call_target="tpu_custom_call" | custom-call | flops 2281701376 | bytes 2097152 | tf_op jit(solution)/shard_map/enc_attention/pallas_call | solution.py:164
  14.7 3.9 %collective-permute-done.3.refs_1_ = bf16[128,1024]{1,0:T(8,128)(2,1)S(1)} collective-permute-done((bf16[128,1024]{1,0:T(8,128)(2,1)S(1)}, bf16[128,1024]{1,0:T(8,128)(2,1)S(1)}, u32[]{:S(2)}, u32[]{:S(2)}) %collective-permute-start.3) | collective-permute-done | bytes 262176 | tf_op jit(solution)/shard_map/ppermute | solution.py:223
  18.6 2.8 %collective-permute-start.9 = (bf16[80,1024]{1,0:T(8,128)(2,1)S(1)}, bf16[80,1024]{1,0:T(8,128)(2,1)S(1)}, u32[]{:S(2)}, u32[]{:S(2)}) collective-permute-start(bf16[80,1024]{1,0:T(8,128)(2,1)S(1)} %get-tuple-element.65), channel_id=1, source_target_pairs={{0,0},{1,4},{2,8},{3,12},{4,16},{5,20},{6,24},{7,28},{8,1},{9,5},{... | collective-permute-start | bytes 491528 | tf_op jit(solution)/shard_map/ppermute | solution.py:418
  21.4 1.6 %collective-permute-start.8 = (bf16[128,1024]{1,0:T(8,128)(2,1)S(1)}, bf16[128,1024]{1,0:T(8,128)(2,1)S(1)}, u32[]{:S(2)}, u32[]{:S(2)}) collective-permute-start(bf16[128,1024]{1,0:T(8,128)(2,1)S(1)} %collective-permute-done.3.refs_1_), channel_id=1, source_target_pairs={{0,2},{1,3},{2,0},{3,1},{4,6},{5,7},{6,4},{7,5},{8,10},{9,11},{10,... | collective-permute-start | bytes 786440 | tf_op jit(solution)/shard_map/ppermute | solution.py:223
  23.0 2.7 %collective-permute-start.5 = (bf16[128,1024]{1,0:T(8,128)(2,1)S(1)}, bf16[128,1024]{1,0:T(8,128)(2,1)S(1)}, u32[]{:S(2)}, u32[]{:S(2)}) collective-permute-start(bf16[128,1024]{1,0:T(8,128)(2,1)S(1)} %collective-permute-done.2.refs_1_), channel_id=1, source_target_pairs={{0,1},{1,0},{2,3},{3,2},{4,5},{5,4},{6,7},{7,6},{8,9},{9,8},{10,11... | collective-permute-start | bytes 786440 | tf_op jit(solution)/shard_map/ppermute | solution.py:223
  25.6 3.6 %enc_attention.5 = (bf16[128,1024]{1,0:T(8,128)(2,1)S(1)}, bf16[128,1024]{1,0:T(8,128)(2,1)S(1)}) custom-call(s32[32]{0:T(128)S(1)} %copy-done.5, bf16[128,1024]{1,0:T(8,128)(2,1)S(1)} %collective-permute-done.3.refs_1_, bf16[128,1024]{1,0:T(8,128)(2,1)S(1)} %collective-permute-done.4.refs_2_, bf16[1024,1024]{1,0:T(8,128)(2,1)S(1)} %get-tuple-element.52.refs_3_, ...), custom_call_target="tpu_custom_call" | custom-call | flops 2281701376 | bytes 2097152 | tf_op jit(solution)/shard_map/enc_attention/pallas_call | solution.py:164
  29.5 0.7 collective-permute-start.10
  30.2 3.4 %collective-permute-start.11 = (bf16[64,1024]{1,0:T(8,128)(2,1)S(1)}, bf16[64,1024]{1,0:T(8,128)(2,1)S(1)}, u32[]{:S(2)}, u32[]{:S(2)}) collective-permute-start(bf16[64,1024]{1,0:T(8,128)(2,1)S(1)} %get-tuple-element.66), channel_id=1, source_target_pairs={{0,2},{1,3},{2,0},{3,1},{4,6},{5,7},{6,4},{7,5},{8,10},{9,11},{10,... | collective-permute-start | bytes 393224 | tf_op jit(solution)/shard_map/ppermute | solution.py:223
  33.6 3.6 %enc_attention.6 = (bf16[128,1024]{1,0:T(8,128)(2,1)S(1)}, bf16[128,1024]{1,0:T(8,128)(2,1)S(1)}) custom-call(s32[32]{0:T(128)S(1)} %copy-done.5, bf16[128,1024]{1,0:T(8,128)(2,1)S(1)} %collective-permute-done.2.refs_1_, bf16[128,1024]{1,0:T(8,128)(2,1)S(1)} %collective-permute-done.5.refs_2_, bf16[1024,1024]{1,0:T(8,128)(2,1)S(1)} %get-tuple-element.52.refs_3_, ...), custom_call_target="tpu_custom_call" | custom-call | flops 2281701376 | bytes 2097152 | tf_op jit(solution)/shard_map/enc_attention/pallas_call | solution.py:164
  37.1 2.1 %collective-permute-done.10 = bf16[64,1024]{1,0:T(8,128)(2,1)S(1)} collective-permute-done((bf16[64,1024]{1,0:T(8,128)(2,1)S(1)}, bf16[64,1024]{1,0:T(8,128)(2,1)S(1)}, u32[]{:S(2)}, u32[]{:S(2)}) %collective-permute-start.10) | collective-permute-done | bytes 131104 | tf_op jit(solution)/shard_map/ppermute | solution.py:223
  39.5 0.4 collective-permute-start.6
  40.0 0.6 collective-permute-start.15
  40.5 0.4 collective-permute-done.12.refs_2_
  40.9 3.6 %enc_attention.7 = (bf16[128,1024]{1,0:T(8,128)(2,1)S(1)}, bf16[128,1024]{1,0:T(8,128)(2,1)S(1)}) custom-call(s32[32]{0:T(128)S(1)} %copy-done.5, bf16[128,1024]{1,0:T(8,128)(2,1)S(1)} %collective-permute-done.8.refs_1_, bf16[128,1024]{1,0:T(8,128)(2,1)S(1)} %collective-permute-done.12.refs_2_, bf16[1024,1024]{1,0:T(8,128)(2,1)S(1)} %get-tuple-element.52.refs_3_, ...), custom_call_target="tpu_custom_call" | custom-call | flops 2281701376 | bytes 2097152 | tf_op jit(solution)/shard_map/enc_attention/pallas_call | solution.py:164
  44.7 1.1 collective-permute-start.18
  45.9 1.0 collective-permute-start.7
  46.9 2.0 %collective-permute-done.15 = bf16[128,1024]{1,0:T(8,128)(2,1)S(1)} collective-permute-done((bf16[128,1024]{1,0:T(8,128)(2,1)S(1)}, bf16[128,1024]{1,0:T(8,128)(2,1)S(1)}, u32[]{:S(2)}, u32[]{:S(2)}) %collective-permute-start.15) | collective-permute-done | bytes 262176 | tf_op jit(solution)/shard_map/ppermute | solution.py:223
  49.1 4.1 %collective-permute-start.16 = (bf16[128,1024]{1,0:T(8,128)(2,1)S(1)}, bf16[128,1024]{1,0:T(8,128)(2,1)S(1)}, u32[]{:S(2)}, u32[]{:S(2)}) collective-permute-start(bf16[128,1024]{1,0:T(8,128)(2,1)S(1)} %add_convert_fusion), channel_id=1, source_target_pairs={{0,6},{1,7},{2,4},{3,5},{4,2},{5,3},{6,0},{7,1},{8,14},{9,15},{10,... | collective-permute-start | bytes 786440 | tf_op jit(solution)/shard_map/ppermute | solution.py:223
  53.3 3.5 %collective-permute-done.7.refs_3_ = bf16[128,1024]{1,0:T(8,128)(2,1)S(1)} collective-permute-done((bf16[128,1024]{1,0:T(8,128)(2,1)S(1)}, bf16[128,1024]{1,0:T(8,128)(2,1)S(1)}, u32[]{:S(2)}, u32[]{:S(2)}) %collective-permute-start.7) | collective-permute-done | bytes 262176 | tf_op jit(solution)/shard_map/ppermute | solution.py:223
  56.8 7.9 %collective-permute-done.16.refs_4_ = bf16[128,1024]{1,0:T(8,128)(2,1)S(1)} collective-permute-done((bf16[128,1024]{1,0:T(8,128)(2,1)S(1)}, bf16[128,1024]{1,0:T(8,128)(2,1)S(1)}, u32[]{:S(2)}, u32[]{:S(2)}) %collective-permute-start.16) | collective-permute-done | bytes 262176 | tf_op jit(solution)/shard_map/ppermute | solution.py:223
  64.7 1.0 sum_norm.4
  65.8 2.0 %collective-permute-start.21 = (bf16[128,1024]{1,0:T(8,128)(2,1)S(1)}, bf16[128,1024]{1,0:T(8,128)(2,1)S(1)}, u32[]{:S(2)}, u32[]{:S(2)}) collective-permute-start(bf16[128,1024]{1,0:T(8,128)(2,1)S(1)} %get-tuple-element.73.refs_1_), channel_id=1, source_target_pairs={{0,2},{1,3},{2,0},{3,1},{4,6},{5,7},{6,4},{7,5},{8,10},{9,11},{10,... | collective-permute-start | bytes 786440 | tf_op jit(solution)/shard_map/ppermute | solution.py:223
  67.9 3.0 %cross_attention.4 = (bf16[64,1024]{1,0:T(8,128)(2,1)S(1)}, bf16[64,1024]{1,0:T(8,128)(2,1)S(1)}) custom-call(s32[32]{0:T(128)S(1)} %copy-done.5, bf16[128,1024]{1,0:T(8,128)(2,1)S(1)} %get-tuple-element.73.refs_1_, bf16[128,1024]{1,0:T(8,128)(2,1)S(1)} %collective-permute-done.17.refs_2_, bf16[4,64,1024]{2,1,0:T(8,128)(2,1)S(1)} %pad_maximum_fusion.refs_3_, ...), custom_call_target="tpu_custom_call" | custom-call | flops 1677721600 | bytes 1572864 | tf_op jit(solution)/shard_map/cross_attention/pallas_call | solution.py:164
  70.9 9.1 %collective-permute-done.22.refs_1_ = bf16[128,1024]{1,0:T(8,128)(2,1)S(1)} collective-permute-done((bf16[128,1024]{1,0:T(8,128)(2,1)S(1)}, bf16[128,1024]{1,0:T(8,128)(2,1)S(1)}, u32[]{:S(2)}, u32[]{:S(2)}) %collective-permute-start.22) | collective-permute-done | bytes 262176 | tf_op jit(solution)/shard_map/ppermute | solution.py:223
  80.0 0.5 collective-permute-start.20
  80.5 1.2 collective-permute-done.20.refs_2_
  81.7 3.2 %cross_attention.5 = (bf16[64,1024]{1,0:T(8,128)(2,1)S(1)}, bf16[64,1024]{1,0:T(8,128)(2,1)S(1)}) custom-call(s32[32]{0:T(128)S(1)} %copy-done.5, bf16[128,1024]{1,0:T(8,128)(2,1)S(1)} %collective-permute-done.22.refs_1_, bf16[128,1024]{1,0:T(8,128)(2,1)S(1)} %collective-permute-done.23.refs_2_, bf16[4,64,1024]{2,1,0:T(8,128)(2,1)S(1)} %pad_maximum_fusion.refs_3_, ...), custom_call_target="tpu_custom_call" | custom-call | flops 1677721600 | bytes 1572864 | tf_op jit(solution)/shard_map/cross_attention/pallas_call | solution.py:164
  85.0 0.2 collective-permute-start.30
  85.2 3.0 %cross_attention.6 = (bf16[64,1024]{1,0:T(8,128)(2,1)S(1)}, bf16[64,1024]{1,0:T(8,128)(2,1)S(1)}) custom-call(s32[32]{0:T(128)S(1)} %copy-done.5, bf16[128,1024]{1,0:T(8,128)(2,1)S(1)} %collective-permute-done.21.refs_1_, bf16[128,1024]{1,0:T(8,128)(2,1)S(1)} %collective-permute-done.24.refs_2_, bf16[4,64,1024]{2,1,0:T(8,128)(2,1)S(1)} %pad_maximum_fusion.refs_3_, ...), custom_call_target="tpu_custom_call" | custom-call | flops 1677721600 | bytes 1572864 | tf_op jit(solution)/shard_map/cross_attention/pallas_call | solution.py:164
  88.2 1.0 collective-permute-done.27.refs_1_
  89.2 0.5 collective-permute-start.25
  89.8 0.3 collective-permute-start.31
  90.1 0.6 collective-permute-done.28.refs_2_
  90.8 3.0 %cross_attention.7 = (bf16[64,1024]{1,0:T(8,128)(2,1)S(1)}, bf16[64,1024]{1,0:T(8,128)(2,1)S(1)}) custom-call(s32[32]{0:T(128)S(1)} %copy-done.5, bf16[128,1024]{1,0:T(8,128)(2,1)S(1)} %collective-permute-done.27.refs_1_, bf16[128,1024]{1,0:T(8,128)(2,1)S(1)} %collective-permute-done.28.refs_2_, bf16[4,64,1024]{2,1,0:T(8,128)(2,1)S(1)} %pad_maximum_fusion.refs_3_, ...), custom_call_target="tpu_custom_call" | custom-call | flops 1677721600 | bytes 1572864 | tf_op jit(solution)/shard_map/cross_attention/pallas_call | solution.py:164
  94.0 1.1 collective-permute-start.26
  95.3 2.3 %collective-permute-start.32 = (bf16[64,1024]{1,0:T(8,128)(2,1)S(1)}, bf16[64,1024]{1,0:T(8,128)(2,1)S(1)}, u32[]{:S(2)}, u32[]{:S(2)}) collective-permute-start(bf16[64,1024]{1,0:T(8,128)(2,1)S(1)} %add_convert_fusion.6), channel_id=1, source_target_pairs={{0,6},{1,7},{2,4},{3,5},{4,2},{5,3},{6,0},{7,1},{8,14},{9,15},{10,... | collective-permute-start | bytes 393224 | tf_op jit(solution)/shard_map/ppermute | solution.py:223
  97.6 2.2 %collective-permute-done.26.refs_3_ = bf16[64,1024]{1,0:T(8,128)(2,1)S(1)} collective-permute-done((bf16[64,1024]{1,0:T(8,128)(2,1)S(1)}, bf16[64,1024]{1,0:T(8,128)(2,1)S(1)}, u32[]{:S(2)}, u32[]{:S(2)}) %collective-permute-start.26) | collective-permute-done | bytes 131104 | tf_op jit(solution)/shard_map/ppermute | solution.py:223
  99.8 4.2 %collective-permute-done.32.refs_4_ = bf16[64,1024]{1,0:T(8,128)(2,1)S(1)} collective-permute-done((bf16[64,1024]{1,0:T(8,128)(2,1)S(1)}, bf16[64,1024]{1,0:T(8,128)(2,1)S(1)}, u32[]{:S(2)}, u32[]{:S(2)}) %collective-permute-start.32) | collective-permute-done | bytes 131104 | tf_op jit(solution)/shard_map/ppermute | solution.py:223
  104.3 0.8 collective-permute-start.35
  105.1 1.5 collective-permute-start.36
  106.6 2.4 %feed_forward.4 = (bf16[64,1024]{1,0:T(8,128)(2,1)S(1)}, bf16[64,1024]{1,0:T(8,128)(2,1)S(1)}) custom-call(bf16[64,1024]{1,0:T(8,128)(2,1)S(1)} %get-tuple-element.87.refs_0_, bf16[64,1024]{1,0:T(8,128)(2,1)S(1)} %collective-permute-done.33.refs_1_, bf16[1024,4096]{1,0:T(8,128)(2,1)S(1)} %bitcast.15, bf16[4096,1024]{1,0:T(8,128)(2,1)S(1)} %bitcast.17), custom_call_target="tpu_custom_call" | custom-call | flops 2147483648 | bytes 524288 | tf_op jit(solution)/shard_map/feed_forward/pallas_call | solution.py:205
  109.1 5.3 %collective-permute-done.36.refs_0_ = bf16[64,1024]{1,0:T(8,128)(2,1)S(1)} collective-permute-done((bf16[64,1024]{1,0:T(8,128)(2,1)S(1)}, bf16[64,1024]{1,0:T(8,128)(2,1)S(1)}, u32[]{:S(2)}, u32[]{:S(2)}) %collective-permute-start.36) | collective-permute-done | bytes 131104 | tf_op jit(solution)/shard_map/ppermute | solution.py:223
  114.6 0.3 collective-permute-start.38
  115.0 0.8 collective-permute-done.37.refs_1_
  115.8 2.4 %feed_forward.5 = (bf16[64,1024]{1,0:T(8,128)(2,1)S(1)}, bf16[64,1024]{1,0:T(8,128)(2,1)S(1)}) custom-call(bf16[64,1024]{1,0:T(8,128)(2,1)S(1)} %collective-permute-done.36.refs_0_, bf16[64,1024]{1,0:T(8,128)(2,1)S(1)} %collective-permute-done.37.refs_1_, bf16[1024,4096]{1,0:T(8,128)(2,1)S(1)} %bitcast.15, bf16[4096,1024]{1,0:T(8,128)(2,1)S(1)} %bitcast.17), custom_call_target="tpu_custom_call" | custom-call | flops 2147483648 | bytes 524288 | tf_op jit(solution)/shard_map/feed_forward/pallas_call | solution.py:205
  118.2 0.2 collective-permute-start.44
  118.4 2.6 %feed_forward.6 = (bf16[64,1024]{1,0:T(8,128)(2,1)S(1)}, bf16[64,1024]{1,0:T(8,128)(2,1)S(1)}) custom-call(bf16[64,1024]{1,0:T(8,128)(2,1)S(1)} %collective-permute-done.35.refs_0_, bf16[64,1024]{1,0:T(8,128)(2,1)S(1)} %collective-permute-done.38.refs_1_, bf16[1024,4096]{1,0:T(8,128)(2,1)S(1)} %bitcast.15, bf16[4096,1024]{1,0:T(8,128)(2,1)S(1)} %bitcast.17), custom_call_target="tpu_custom_call" | custom-call | flops 2147483648 | bytes 524288 | tf_op jit(solution)/shard_map/feed_forward/pallas_call | solution.py:205
  121.0 0.4 collective-permute-start.39
  121.7 1.1 collective-permute-start.45
  122.8 2.4 %feed_forward.7 = (bf16[64,1024]{1,0:T(8,128)(2,1)S(1)}, bf16[64,1024]{1,0:T(8,128)(2,1)S(1)}) custom-call(bf16[64,1024]{1,0:T(8,128)(2,1)S(1)} %collective-permute-done.41.refs_0_, bf16[64,1024]{1,0:T(8,128)(2,1)S(1)} %collective-permute-done.42.refs_1_, bf16[1024,4096]{1,0:T(8,128)(2,1)S(1)} %bitcast.15, bf16[4096,1024]{1,0:T(8,128)(2,1)S(1)} %bitcast.17), custom_call_target="tpu_custom_call" | custom-call | flops 2147483648 | bytes 524288 | tf_op jit(solution)/shard_map/feed_forward/pallas_call | solution.py:205
  125.2 0.2 collective-permute-start.43
  125.5 1.1 collective-permute-start.40
  126.6 0.9 collective-permute-done.45
  127.5 2.3 %collective-permute-start.46 = (bf16[64,1024]{1,0:T(8,128)(2,1)S(1)}, bf16[64,1024]{1,0:T(8,128)(2,1)S(1)}, u32[]{:S(2)}, u32[]{:S(2)}) collective-permute-start(bf16[64,1024]{1,0:T(8,128)(2,1)S(1)} %add_convert_fusion.3), channel_id=1, source_target_pairs={{0,6},{1,7},{2,4},{3,5},{4,2},{5,3},{6,0},{7,1},{8,14},{9,15},{10,... | collective-permute-start | bytes 393224 | tf_op jit(solution)/shard_map/ppermute | solution.py:223
  129.8 1.5 collective-permute-done.40.refs_3_
  131.3 4.0 %collective-permute-done.46.refs_4_ = bf16[64,1024]{1,0:T(8,128)(2,1)S(1)} collective-permute-done((bf16[64,1024]{1,0:T(8,128)(2,1)S(1)}, bf16[64,1024]{1,0:T(8,128)(2,1)S(1)}, u32[]{:S(2)}, u32[]{:S(2)}) %collective-permute-start.46) | collective-permute-done | bytes 131104 | tf_op jit(solution)/shard_map/ppermute | solution.py:223
  135.4 3.2 %collective-permute-start.47 = (bf16[64,1024]{1,0:T(8,128)(2,1)S(1)}, bf16[64,1024]{1,0:T(8,128)(2,1)S(1)}, u32[]{:S(2)}, u32[]{:S(2)}) collective-permute-start(bf16[64,1024]{1,0:T(8,128)(2,1)S(1)} %masked_sum.1), channel_id=1, source_target_pairs={{0,0},{4,1},{8,2},{12,3},{16,4},{20,5},{24,6},{28,7},{1,8},{5,9},{... | collective-permute-start | bytes 393224 | tf_op jit(solution)/shard_map/ppermute | solution.py:444
  138.6 8.5 %collective-permute-done.47 = bf16[64,1024]{1,0:T(8,128)(2,1)S(1)} collective-permute-done((bf16[64,1024]{1,0:T(8,128)(2,1)S(1)}, bf16[64,1024]{1,0:T(8,128)(2,1)S(1)}, u32[]{:S(2)}, u32[]{:S(2)}) %collective-permute-start.47) | collective-permute-done | bytes 131104 | tf_op jit(solution)/shard_map/ppermute | solution.py:444
  147.1 0.7 copy.25
  (96 shorter events, 3.0 us)
Async XLA Ops:
  1.3 0.7 copy-start.9
  3.2 7.9 %copy-start.5 = (s32[32]{0:T(128)S(1)}, s32[32]{0:T(128)}, u32[]{:S(2)}) copy-start(s32[32]{0:T(128)} %refs_0_.17) | copy-start | bytes 388
  3.2 7.8 %collective-permute-start = (bf16[128,1024]{1,0:T(8,128)(2,1)S(1)}, bf16[128,1024]{1,0:T(8,128)(2,1)S(1)}, u32[]{:S(2)}, u32[]{:S(2)}) collective-permute-start(bf16[128,1024]{1,0:T(8,128)(2,1)S(1)} %get-tuple-element.51.refs_5_.refs_1_), channel_id=1, source_target_pairs={{0,1},{1,0},{2,3},{3,2},{4,5},{5,4},{6,7},{7,6},{8,9},{9,8},{10,11... | collective-permute-start | bytes 786440 | tf_op jit(solution)/shard_map/ppermute | solution.py:223
  3.3 15.3 %collective-permute-start.3 = (bf16[128,1024]{1,0:T(8,128)(2,1)S(1)}, bf16[128,1024]{1,0:T(8,128)(2,1)S(1)}, u32[]{:S(2)}, u32[]{:S(2)}) collective-permute-start(bf16[128,1024]{1,0:T(8,128)(2,1)S(1)} %get-tuple-element.51.refs_5_.refs_1_), channel_id=1, source_target_pairs={{0,4},{1,5},{2,6},{3,7},{4,0},{5,1},{6,2},{7,3},{8,12},{9,13},{10,... | collective-permute-start | bytes 786440 | tf_op jit(solution)/shard_map/ppermute | solution.py:223
  5.9 17.0 %collective-permute-start.2 = (bf16[128,1024]{1,0:T(8,128)(2,1)S(1)}, bf16[128,1024]{1,0:T(8,128)(2,1)S(1)}, u32[]{:S(2)}, u32[]{:S(2)}) collective-permute-start(bf16[128,1024]{1,0:T(8,128)(2,1)S(1)} %get-tuple-element.51.refs_5_.refs_1_), channel_id=1, source_target_pairs={{0,2},{1,3},{2,0},{3,1},{4,6},{5,7},{6,4},{7,5},{8,10},{9,11},{10,... | collective-permute-start | bytes 786440 | tf_op jit(solution)/shard_map/ppermute | solution.py:223
  14.6 11.0 %collective-permute-start.1 = (bf16[128,1024]{1,0:T(8,128)(2,1)S(1)}, bf16[128,1024]{1,0:T(8,128)(2,1)S(1)}, u32[]{:S(2)}, u32[]{:S(2)}) collective-permute-start(bf16[128,1024]{1,0:T(8,128)(2,1)S(1)} %get-tuple-element.58), channel_id=1, source_target_pairs={{0,1},{1,0},{2,3},{3,2},{4,5},{5,4},{6,7},{7,6},{8,9},{9,8},{10,11... | collective-permute-start | bytes 786440 | tf_op jit(solution)/shard_map/ppermute | solution.py:223
  18.6 7.0 %collective-permute-start.4 = (bf16[128,1024]{1,0:T(8,128)(2,1)S(1)}, bf16[128,1024]{1,0:T(8,128)(2,1)S(1)}, u32[]{:S(2)}, u32[]{:S(2)}) collective-permute-start(bf16[128,1024]{1,0:T(8,128)(2,1)S(1)} %collective-permute-done.3.refs_1_), channel_id=1, source_target_pairs={{0,1},{1,0},{2,3},{3,2},{4,5},{5,4},{6,7},{7,6},{8,9},{9,8},{10,11... | collective-permute-start | bytes 786440 | tf_op jit(solution)/shard_map/ppermute | solution.py:223
  18.6 10.8 %copy-start.6 = (f32[1024]{0:T(1024)S(1)}, f32[1024]{0:T(1024)}, u32[]{:S(2)}) copy-start(f32[1024]{0:T(1024)} %param.34) | copy-start | bytes 12292
  18.6 10.7 %collective-permute-start.9 = (bf16[80,1024]{1,0:T(8,128)(2,1)S(1)}, bf16[80,1024]{1,0:T(8,128)(2,1)S(1)}, u32[]{:S(2)}, u32[]{:S(2)}) collective-permute-start(bf16[80,1024]{1,0:T(8,128)(2,1)S(1)} %get-tuple-element.65), channel_id=1, source_target_pairs={{0,0},{1,4},{2,8},{3,12},{4,16},{5,20},{6,24},{7,28},{8,1},{9,5},{... | collective-permute-start | bytes 491528 | tf_op jit(solution)/shard_map/ppermute | solution.py:418
  21.4 18.0 %collective-permute-start.8 = (bf16[128,1024]{1,0:T(8,128)(2,1)S(1)}, bf16[128,1024]{1,0:T(8,128)(2,1)S(1)}, u32[]{:S(2)}, u32[]{:S(2)}) collective-permute-start(bf16[128,1024]{1,0:T(8,128)(2,1)S(1)} %collective-permute-done.3.refs_1_), channel_id=1, source_target_pairs={{0,2},{1,3},{2,0},{3,1},{4,6},{5,7},{6,4},{7,5},{8,10},{9,11},{10,... | collective-permute-start | bytes 786440 | tf_op jit(solution)/shard_map/ppermute | solution.py:223
  23.0 10.6 %collective-permute-start.5 = (bf16[128,1024]{1,0:T(8,128)(2,1)S(1)}, bf16[128,1024]{1,0:T(8,128)(2,1)S(1)}, u32[]{:S(2)}, u32[]{:S(2)}) collective-permute-start(bf16[128,1024]{1,0:T(8,128)(2,1)S(1)} %collective-permute-done.2.refs_1_), channel_id=1, source_target_pairs={{0,1},{1,0},{2,3},{3,2},{4,5},{5,4},{6,7},{7,6},{8,9},{9,8},{10,11... | collective-permute-start | bytes 786440 | tf_op jit(solution)/shard_map/ppermute | solution.py:223
  29.2 10.7 %collective-permute-start.14 = (bf16[128,1024]{1,0:T(8,128)(2,1)S(1)}, bf16[128,1024]{1,0:T(8,128)(2,1)S(1)}, u32[]{:S(2)}, u32[]{:S(2)}) collective-permute-start(bf16[128,1024]{1,0:T(8,128)(2,1)S(1)} %get-tuple-element.70), channel_id=1, source_target_pairs={{0,1},{1,0},{2,3},{3,2},{4,5},{5,4},{6,7},{7,6},{8,9},{9,8},{10,11... | collective-permute-start | bytes 786440 | tf_op jit(solution)/shard_map/ppermute | solution.py:223
  29.5 9.8 %collective-permute-start.10 = (bf16[64,1024]{1,0:T(8,128)(2,1)S(1)}, bf16[64,1024]{1,0:T(8,128)(2,1)S(1)}, u32[]{:S(2)}, u32[]{:S(2)}) collective-permute-start(bf16[64,1024]{1,0:T(8,128)(2,1)S(1)} %get-tuple-element.66), channel_id=1, source_target_pairs={{0,4},{1,5},{2,6},{3,7},{4,0},{5,1},{6,2},{7,3},{8,12},{9,13},{10,... | collective-permute-start | bytes 393224 | tf_op jit(solution)/shard_map/ppermute | solution.py:223
  30.2 9.2 %collective-permute-start.11 = (bf16[64,1024]{1,0:T(8,128)(2,1)S(1)}, bf16[64,1024]{1,0:T(8,128)(2,1)S(1)}, u32[]{:S(2)}, u32[]{:S(2)}) collective-permute-start(bf16[64,1024]{1,0:T(8,128)(2,1)S(1)} %get-tuple-element.66), channel_id=1, source_target_pairs={{0,2},{1,3},{2,0},{3,1},{4,6},{5,7},{6,4},{7,5},{8,10},{9,11},{10,... | collective-permute-start | bytes 393224 | tf_op jit(solution)/shard_map/ppermute | solution.py:223
  39.4 1.5 %collective-permute-start.12 = (bf16[128,1024]{1,0:T(8,128)(2,1)S(1)}, bf16[128,1024]{1,0:T(8,128)(2,1)S(1)}, u32[]{:S(2)}, u32[]{:S(2)}) collective-permute-start(bf16[128,1024]{1,0:T(8,128)(2,1)S(1)} %collective-permute-done.8.refs_1_), channel_id=1, source_target_pairs={{0,1},{1,0},{2,3},{3,2},{4,5},{5,4},{6,7},{7,6},{8,9},{9,8},{10,11... | collective-permute-start | bytes 786440 | tf_op jit(solution)/shard_map/ppermute | solution.py:223
  39.5 6.4 %collective-permute-start.6 = (bf16[128,1024]{1,0:T(8,128)(2,1)S(1)}, bf16[128,1024]{1,0:T(8,128)(2,1)S(1)}, u32[]{:S(2)}, u32[]{:S(2)}) collective-permute-start(bf16[128,1024]{1,0:T(8,128)(2,1)S(1)} %get-tuple-element.64), channel_id=1, source_target_pairs={{0,1},{1,0},{2,3},{3,2},{4,5},{5,4},{6,7},{7,6},{8,9},{9,8},{10,11... | collective-permute-start | bytes 786440 | tf_op jit(solution)/shard_map/ppermute | solution.py:223
  40.0 9.0 %collective-permute-start.15 = (bf16[128,1024]{1,0:T(8,128)(2,1)S(1)}, bf16[128,1024]{1,0:T(8,128)(2,1)S(1)}, u32[]{:S(2)}, u32[]{:S(2)}) collective-permute-start(bf16[128,1024]{1,0:T(8,128)(2,1)S(1)} %add_convert_fusion.1), channel_id=1, source_target_pairs={{0,2},{1,3},{2,0},{3,1},{4,6},{5,7},{6,4},{7,5},{8,10},{9,11},{10,... | collective-permute-start | bytes 786440 | tf_op jit(solution)/shard_map/ppermute | solution.py:223
  40.9 23.8 %copy-start.4 = (bf16[1,128,1024]{2,1,0:T(8,128)(2,1)S(1)}, bf16[1,128,1024]{2,1,0:T(8,128)(2,1)}, u32[]{:S(2)}) copy-start(bf16[1,128,1024]{2,1,0:T(8,128)(2,1)} %param.21) | copy-start | bytes 786436
  40.9 26.9 %copy-start.2 = (bf16[1024,1024]{1,0:T(8,128)(2,1)S(1)}, bf16[1024,1024]{1,0:T(8,128)(2,1)}, u32[]{:S(2)}) copy-start(bf16[1024,1024]{1,0:T(8,128)(2,1)} %refs_7_.7) | copy-start | bytes 6291460
  40.9 26.9 %copy-start.3 = (bf16[1024,1024]{1,0:T(8,128)(2,1)S(1)}, bf16[1024,1024]{1,0:T(8,128)(2,1)}, u32[]{:S(2)}) copy-start(bf16[1024,1024]{1,0:T(8,128)(2,1)} %refs_8_.7) | copy-start | bytes 6291460
  44.5 20.2 %copy-start.7 = (f32[1024]{0:T(1024)S(1)}, f32[1024]{0:T(1024)}, u32[]{:S(2)}) copy-start(f32[1024]{0:T(1024)} %param.29) | copy-start | bytes 12292
  44.5 23.4 %copy-start = (bf16[1024,1024]{1,0:T(8,128)(2,1)S(1)}, bf16[1024,1024]{1,0:T(8,128)(2,1)}, u32[]{:S(2)}) copy-start(bf16[1024,1024]{1,0:T(8,128)(2,1)} %refs_5_.7) | copy-start | bytes 6291460
  44.5 23.4 %copy-start.1 = (bf16[1024,1024]{1,0:T(8,128)(2,1)S(1)}, bf16[1024,1024]{1,0:T(8,128)(2,1)}, u32[]{:S(2)}) copy-start(bf16[1024,1024]{1,0:T(8,128)(2,1)} %refs_6_.7) | copy-start | bytes 6291460
  44.5 4.4 %collective-permute-start.13 = (bf16[128,1024]{1,0:T(8,128)(2,1)S(1)}, bf16[128,1024]{1,0:T(8,128)(2,1)S(1)}, u32[]{:S(2)}, u32[]{:S(2)}) collective-permute-start(bf16[128,1024]{1,0:T(8,128)(2,1)S(1)} %get-tuple-element.69), channel_id=1, source_target_pairs={{0,1},{1,0},{2,3},{3,2},{4,5},{5,4},{6,7},{7,6},{8,9},{9,8},{10,11... | collective-permute-start | bytes 786440 | tf_op jit(solution)/shard_map/ppermute | solution.py:223
  44.7 8.4 %collective-permute-start.18 = (bf16[64,1024]{1,0:T(8,128)(2,1)S(1)}, bf16[64,1024]{1,0:T(8,128)(2,1)S(1)}, u32[]{:S(2)}, u32[]{:S(2)}) collective-permute-start(bf16[64,1024]{1,0:T(8,128)(2,1)S(1)} %collective-permute-done.10), channel_id=1, source_target_pairs={{0,2},{1,3},{2,0},{3,1},{4,6},{5,7},{6,4},{7,5},{8,10},{9,11},{10,... | collective-permute-start | bytes 393224 | tf_op jit(solution)/shard_map/ppermute | solution.py:223
  45.9 10.9 %collective-permute-start.7 = (bf16[128,1024]{1,0:T(8,128)(2,1)S(1)}, bf16[128,1024]{1,0:T(8,128)(2,1)S(1)}, u32[]{:S(2)}, u32[]{:S(2)}) collective-permute-start(bf16[128,1024]{1,0:T(8,128)(2,1)S(1)} %add_convert_fusion.2), channel_id=1, source_target_pairs={{0,2},{1,3},{2,0},{3,1},{4,6},{5,7},{6,4},{7,5},{8,10},{9,11},{10,... | collective-permute-start | bytes 786440 | tf_op jit(solution)/shard_map/ppermute | solution.py:223
  49.1 15.6 %collective-permute-start.16 = (bf16[128,1024]{1,0:T(8,128)(2,1)S(1)}, bf16[128,1024]{1,0:T(8,128)(2,1)S(1)}, u32[]{:S(2)}, u32[]{:S(2)}) collective-permute-start(bf16[128,1024]{1,0:T(8,128)(2,1)S(1)} %add_convert_fusion), channel_id=1, source_target_pairs={{0,6},{1,7},{2,4},{3,5},{4,2},{5,3},{6,0},{7,1},{8,14},{9,15},{10,... | collective-permute-start | bytes 786440 | tf_op jit(solution)/shard_map/ppermute | solution.py:223
  53.2 14.6 %collective-permute-start.19 = (bf16[4,64,1024]{2,1,0:T(8,128)(2,1)S(1)}, bf16[4,64,1024]{2,1,0:T(8,128)(2,1)S(1)}, u32[]{:S(2)}, u32[]{:S(2)}) collective-permute-start(bf16[4,64,1024]{2,1,0:T(8,128)(2,1)S(1)} %pad_maximum_fusion.refs_3_), channel_id=1, source_target_pairs={{0,1},{1,0},{2,3},{3,2},{4,5},{5,4},{6,7},{7,6},{8,9},{9,8},{10,11... | collective-permute-start | bytes 1572872 | tf_op jit(solution)/shard_map/ppermute | solution.py:223
  65.7 2.2 %collective-permute-start.17 = (bf16[128,1024]{1,0:T(8,128)(2,1)S(1)}, bf16[128,1024]{1,0:T(8,128)(2,1)S(1)}, u32[]{:S(2)}, u32[]{:S(2)}) collective-permute-start(bf16[128,1024]{1,0:T(8,128)(2,1)S(1)} %get-tuple-element.73.refs_1_), channel_id=1, source_target_pairs={{0,1},{1,0},{2,3},{3,2},{4,5},{5,4},{6,7},{7,6},{8,9},{9,8},{10,11... | collective-permute-start | bytes 786440 | tf_op jit(solution)/shard_map/ppermute | solution.py:223
  65.7 14.3 %collective-permute-start.22 = (bf16[128,1024]{1,0:T(8,128)(2,1)S(1)}, bf16[128,1024]{1,0:T(8,128)(2,1)S(1)}, u32[]{:S(2)}, u32[]{:S(2)}) collective-permute-start(bf16[128,1024]{1,0:T(8,128)(2,1)S(1)} %get-tuple-element.73.refs_1_), channel_id=1, source_target_pairs={{0,4},{1,5},{2,6},{3,7},{4,0},{5,1},{6,2},{7,3},{8,12},{9,13},{10,... | collective-permute-start | bytes 786440 | tf_op jit(solution)/shard_map/ppermute | solution.py:223
  65.8 14.7 %collective-permute-start.21 = (bf16[128,1024]{1,0:T(8,128)(2,1)S(1)}, bf16[128,1024]{1,0:T(8,128)(2,1)S(1)}, u32[]{:S(2)}, u32[]{:S(2)}) collective-permute-start(bf16[128,1024]{1,0:T(8,128)(2,1)S(1)} %get-tuple-element.73.refs_1_), channel_id=1, source_target_pairs={{0,2},{1,3},{2,0},{3,1},{4,6},{5,7},{6,4},{7,5},{8,10},{9,11},{10,... | collective-permute-start | bytes 786440 | tf_op jit(solution)/shard_map/ppermute | solution.py:223
  80.0 1.7 %collective-permute-start.23 = (bf16[128,1024]{1,0:T(8,128)(2,1)S(1)}, bf16[128,1024]{1,0:T(8,128)(2,1)S(1)}, u32[]{:S(2)}, u32[]{:S(2)}) collective-permute-start(bf16[128,1024]{1,0:T(8,128)(2,1)S(1)} %collective-permute-done.22.refs_1_), channel_id=1, source_target_pairs={{0,1},{1,0},{2,3},{3,2},{4,5},{5,4},{6,7},{7,6},{8,9},{9,8},{10,11... | collective-permute-start | bytes 786440 | tf_op jit(solution)/shard_map/ppermute | solution.py:223
  80.0 1.7 %collective-permute-start.20 = (bf16[64,1024]{1,0:T(8,128)(2,1)S(1)}, bf16[64,1024]{1,0:T(8,128)(2,1)S(1)}, u32[]{:S(2)}, u32[]{:S(2)}) collective-permute-start(bf16[64,1024]{1,0:T(8,128)(2,1)S(1)} %get-tuple-element.75), channel_id=1, source_target_pairs={{0,1},{1,0},{2,3},{3,2},{4,5},{5,4},{6,7},{7,6},{8,9},{9,8},{10,11... | collective-permute-start | bytes 393224 | tf_op jit(solution)/shard_map/ppermute | solution.py:223
  80.5 4.7 %collective-permute-start.24 = (bf16[128,1024]{1,0:T(8,128)(2,1)S(1)}, bf16[128,1024]{1,0:T(8,128)(2,1)S(1)}, u32[]{:S(2)}, u32[]{:S(2)}) collective-permute-start(bf16[128,1024]{1,0:T(8,128)(2,1)S(1)} %collective-permute-done.21.refs_1_), channel_id=1, source_target_pairs={{0,1},{1,0},{2,3},{3,2},{4,5},{5,4},{6,7},{7,6},{8,9},{9,8},{10,11... | collective-permute-start | bytes 786440 | tf_op jit(solution)/shard_map/ppermute | solution.py:223
  80.5 8.7 %collective-permute-start.27 = (bf16[128,1024]{1,0:T(8,128)(2,1)S(1)}, bf16[128,1024]{1,0:T(8,128)(2,1)S(1)}, u32[]{:S(2)}, u32[]{:S(2)}) collective-permute-start(bf16[128,1024]{1,0:T(8,128)(2,1)S(1)} %collective-permute-done.22.refs_1_), channel_id=1, source_target_pairs={{0,2},{1,3},{2,0},{3,1},{4,6},{5,7},{6,4},{7,5},{8,10},{9,11},{10,... | collective-permute-start | bytes 786440 | tf_op jit(solution)/shard_map/ppermute | solution.py:223
  81.7 24.9 %slice-start.2 = ((s8[8388608]{0:T(1024)(128)(4,1)}), s8[4194304]{0:T(1024)(128)(4,1)S(1)}, s32[]{:S(2)}) async-start(s8[8388608]{0:T(1024)(128)(4,1)} %bitcast.16), calls=%async_computation.2 | async-start | bytes 8388608
  85.0 21.6 %slice-start.3 = ((s8[8388608]{0:T(1024)(128)(4,1)}), s8[4194304]{0:T(1024)(128)(4,1)S(1)}, s32[]{:S(2)}) async-start(s8[8388608]{0:T(1024)(128)(4,1)} %bitcast.16), calls=%async_computation.3 | async-start | bytes 8388608
  85.0 4.8 %collective-permute-start.30 = (bf16[64,1024]{1,0:T(8,128)(2,1)S(1)}, bf16[64,1024]{1,0:T(8,128)(2,1)S(1)}, u32[]{:S(2)}, u32[]{:S(2)}) collective-permute-start(bf16[64,1024]{1,0:T(8,128)(2,1)S(1)} %get-tuple-element.85), channel_id=1, source_target_pairs={{0,1},{1,0},{2,3},{3,2},{4,5},{5,4},{6,7},{7,6},{8,9},{9,8},{10,11... | collective-permute-start | bytes 393224 | tf_op jit(solution)/shard_map/ppermute | solution.py:223
  85.2 21.4 %slice-start = ((s8[8388608]{0:T(1024)(128)(4,1)}), s8[4194304]{0:T(1024)(128)(4,1)S(1)}, s32[]{:S(2)}) async-start(s8[8388608]{0:T(1024)(128)(4,1)} %bitcast.14), calls=%async_computation | async-start | bytes 8388608
  89.2 1.5 %collective-permute-start.28 = (bf16[128,1024]{1,0:T(8,128)(2,1)S(1)}, bf16[128,1024]{1,0:T(8,128)(2,1)S(1)}, u32[]{:S(2)}, u32[]{:S(2)}) collective-permute-start(bf16[128,1024]{1,0:T(8,128)(2,1)S(1)} %collective-permute-done.27.refs_1_), channel_id=1, source_target_pairs={{0,1},{1,0},{2,3},{3,2},{4,5},{5,4},{6,7},{7,6},{8,9},{9,8},{10,11... | collective-permute-start | bytes 786440 | tf_op jit(solution)/shard_map/ppermute | solution.py:223
  89.2 4.7 %collective-permute-start.25 = (bf16[64,1024]{1,0:T(8,128)(2,1)S(1)}, bf16[64,1024]{1,0:T(8,128)(2,1)S(1)}, u32[]{:S(2)}, u32[]{:S(2)}) collective-permute-start(bf16[64,1024]{1,0:T(8,128)(2,1)S(1)} %get-tuple-element.81), channel_id=1, source_target_pairs={{0,1},{1,0},{2,3},{3,2},{4,5},{5,4},{6,7},{7,6},{8,9},{9,8},{10,11... | collective-permute-start | bytes 393224 | tf_op jit(solution)/shard_map/ppermute | solution.py:223
  89.8 14.3 %copy-start.8 = (f32[1024]{0:T(1024)S(1)}, f32[1024]{0:T(1024)}, u32[]{:S(2)}) copy-start(f32[1024]{0:T(1024)} %param.39) | copy-start | bytes 12292
  89.8 16.8 %slice-start.1 = ((s8[8388608]{0:T(1024)(128)(4,1)}), s8[4194304]{0:T(1024)(128)(4,1)S(1)}, s32[]{:S(2)}) async-start(s8[8388608]{0:T(1024)(128)(4,1)} %bitcast.14), calls=%async_computation.1 | async-start | bytes 8388608
  89.8 5.5 %collective-permute-start.31 = (bf16[64,1024]{1,0:T(8,128)(2,1)S(1)}, bf16[64,1024]{1,0:T(8,128)(2,1)S(1)}, u32[]{:S(2)}, u32[]{:S(2)}) collective-permute-start(bf16[64,1024]{1,0:T(8,128)(2,1)S(1)} %add_convert_fusion.7), channel_id=1, source_target_pairs={{0,2},{1,3},{2,0},{3,1},{4,6},{5,7},{6,4},{7,5},{8,10},{9,11},{10,... | collective-permute-start | bytes 393224 | tf_op jit(solution)/shard_map/ppermute | solution.py:223
  93.8 1.5 %collective-permute-start.29 = (bf16[64,1024]{1,0:T(8,128)(2,1)S(1)}, bf16[64,1024]{1,0:T(8,128)(2,1)S(1)}, u32[]{:S(2)}, u32[]{:S(2)}) collective-permute-start(bf16[64,1024]{1,0:T(8,128)(2,1)S(1)} %get-tuple-element.84), channel_id=1, source_target_pairs={{0,1},{1,0},{2,3},{3,2},{4,5},{5,4},{6,7},{7,6},{8,9},{9,8},{10,11... | collective-permute-start | bytes 393224 | tf_op jit(solution)/shard_map/ppermute | solution.py:223
  94.0 5.8 %collective-permute-start.26 = (bf16[64,1024]{1,0:T(8,128)(2,1)S(1)}, bf16[64,1024]{1,0:T(8,128)(2,1)S(1)}, u32[]{:S(2)}, u32[]{:S(2)}) collective-permute-start(bf16[64,1024]{1,0:T(8,128)(2,1)S(1)} %add_convert_fusion.8), channel_id=1, source_target_pairs={{0,2},{1,3},{2,0},{3,1},{4,6},{5,7},{6,4},{7,5},{8,10},{9,11},{10,... | collective-permute-start | bytes 393224 | tf_op jit(solution)/shard_map/ppermute | solution.py:223
  95.3 8.7 %collective-permute-start.32 = (bf16[64,1024]{1,0:T(8,128)(2,1)S(1)}, bf16[64,1024]{1,0:T(8,128)(2,1)S(1)}, u32[]{:S(2)}, u32[]{:S(2)}) collective-permute-start(bf16[64,1024]{1,0:T(8,128)(2,1)S(1)} %add_convert_fusion.6), channel_id=1, source_target_pairs={{0,6},{1,7},{2,4},{3,5},{4,2},{5,3},{6,0},{7,1},{8,14},{9,15},{10,... | collective-permute-start | bytes 393224 | tf_op jit(solution)/shard_map/ppermute | solution.py:223
  104.2 2.3 %collective-permute-start.33 = (bf16[64,1024]{1,0:T(8,128)(2,1)S(1)}, bf16[64,1024]{1,0:T(8,128)(2,1)S(1)}, u32[]{:S(2)}, u32[]{:S(2)}) collective-permute-start(bf16[64,1024]{1,0:T(8,128)(2,1)S(1)} %get-tuple-element.87.refs_0_), channel_id=1, source_target_pairs={{0,1},{1,0},{2,3},{3,2},{4,5},{5,4},{6,7},{7,6},{8,9},{9,8},{10,11... | collective-permute-start | bytes 393224 | tf_op jit(solution)/shard_map/ppermute | solution.py:223
  104.3 10.3 %collective-permute-start.35 = (bf16[64,1024]{1,0:T(8,128)(2,1)S(1)}, bf16[64,1024]{1,0:T(8,128)(2,1)S(1)}, u32[]{:S(2)}, u32[]{:S(2)}) collective-permute-start(bf16[64,1024]{1,0:T(8,128)(2,1)S(1)} %get-tuple-element.87.refs_0_), channel_id=1, source_target_pairs={{0,2},{1,3},{2,0},{3,1},{4,6},{5,7},{6,4},{7,5},{8,10},{9,11},{10,... | collective-permute-start | bytes 393224 | tf_op jit(solution)/shard_map/ppermute | solution.py:223
  105.1 9.3 %collective-permute-start.36 = (bf16[64,1024]{1,0:T(8,128)(2,1)S(1)}, bf16[64,1024]{1,0:T(8,128)(2,1)S(1)}, u32[]{:S(2)}, u32[]{:S(2)}) collective-permute-start(bf16[64,1024]{1,0:T(8,128)(2,1)S(1)} %get-tuple-element.87.refs_0_), channel_id=1, source_target_pairs={{0,4},{1,5},{2,6},{3,7},{4,0},{5,1},{6,2},{7,3},{8,12},{9,13},{10,... | collective-permute-start | bytes 393224 | tf_op jit(solution)/shard_map/ppermute | solution.py:223
  109.0 5.9 %collective-permute-start.34 = (bf16[64,1024]{1,0:T(8,128)(2,1)S(1)}, bf16[64,1024]{1,0:T(8,128)(2,1)S(1)}, u32[]{:S(2)}, u32[]{:S(2)}) collective-permute-start(bf16[64,1024]{1,0:T(8,128)(2,1)S(1)} %get-tuple-element.89), channel_id=1, source_target_pairs={{0,1},{1,0},{2,3},{3,2},{4,5},{5,4},{6,7},{7,6},{8,9},{9,8},{10,11... | collective-permute-start | bytes 393224 | tf_op jit(solution)/shard_map/ppermute | solution.py:223
  114.4 1.3 collective-permute-start.37
  114.4 7.0 %collective-permute-start.41 = (bf16[64,1024]{1,0:T(8,128)(2,1)S(1)}, bf16[64,1024]{1,0:T(8,128)(2,1)S(1)}, u32[]{:S(2)}, u32[]{:S(2)}) collective-permute-start(bf16[64,1024]{1,0:T(8,128)(2,1)S(1)} %collective-permute-done.36.refs_0_), channel_id=1, source_target_pairs={{0,2},{1,3},{2,0},{3,1},{4,6},{5,7},{6,4},{7,5},{8,10},{9,11},{10,... | collective-permute-start | bytes 393224 | tf_op jit(solution)/shard_map/ppermute | solution.py:223
  114.6 3.8 %collective-permute-start.38 = (bf16[64,1024]{1,0:T(8,128)(2,1)S(1)}, bf16[64,1024]{1,0:T(8,128)(2,1)S(1)}, u32[]{:S(2)}, u32[]{:S(2)}) collective-permute-start(bf16[64,1024]{1,0:T(8,128)(2,1)S(1)} %collective-permute-done.35.refs_0_), channel_id=1, source_target_pairs={{0,1},{1,0},{2,3},{3,2},{4,5},{5,4},{6,7},{7,6},{8,9},{9,8},{10,11... | collective-permute-start | bytes 393224 | tf_op jit(solution)/shard_map/ppermute | solution.py:223
  118.2 3.5 %collective-permute-start.44 = (bf16[64,1024]{1,0:T(8,128)(2,1)S(1)}, bf16[64,1024]{1,0:T(8,128)(2,1)S(1)}, u32[]{:S(2)}, u32[]{:S(2)}) collective-permute-start(bf16[64,1024]{1,0:T(8,128)(2,1)S(1)} %get-tuple-element.99), channel_id=1, source_target_pairs={{0,1},{1,0},{2,3},{3,2},{4,5},{5,4},{6,7},{7,6},{8,9},{9,8},{10,11... | collective-permute-start | bytes 393224 | tf_op jit(solution)/shard_map/ppermute | solution.py:223
  121.0 4.4 %collective-permute-start.39 = (bf16[64,1024]{1,0:T(8,128)(2,1)S(1)}, bf16[64,1024]{1,0:T(8,128)(2,1)S(1)}, u32[]{:S(2)}, u32[]{:S(2)}) collective-permute-start(bf16[64,1024]{1,0:T(8,128)(2,1)S(1)} %get-tuple-element.95), channel_id=1, source_target_pairs={{0,1},{1,0},{2,3},{3,2},{4,5},{5,4},{6,7},{7,6},{8,9},{9,8},{10,11... | collective-permute-start | bytes 393224 | tf_op jit(solution)/shard_map/ppermute | solution.py:223
  121.5 1.3 collective-permute-start.42
  121.7 5.8 %collective-permute-start.45 = (bf16[64,1024]{1,0:T(8,128)(2,1)S(1)}, bf16[64,1024]{1,0:T(8,128)(2,1)S(1)}, u32[]{:S(2)}, u32[]{:S(2)}) collective-permute-start(bf16[64,1024]{1,0:T(8,128)(2,1)S(1)} %add_convert_fusion.4), channel_id=1, source_target_pairs={{0,2},{1,3},{2,0},{3,1},{4,6},{5,7},{6,4},{7,5},{8,10},{9,11},{10,... | collective-permute-start | bytes 393224 | tf_op jit(solution)/shard_map/ppermute | solution.py:223
  125.2 2.3 %collective-permute-start.43 = (bf16[64,1024]{1,0:T(8,128)(2,1)S(1)}, bf16[64,1024]{1,0:T(8,128)(2,1)S(1)}, u32[]{:S(2)}, u32[]{:S(2)}) collective-permute-start(bf16[64,1024]{1,0:T(8,128)(2,1)S(1)} %get-tuple-element.98), channel_id=1, source_target_pairs={{0,1},{1,0},{2,3},{3,2},{4,5},{5,4},{6,7},{7,6},{8,9},{9,8},{10,11... | collective-permute-start | bytes 393224 | tf_op jit(solution)/shard_map/ppermute | solution.py:223
  125.5 5.8 %collective-permute-start.40 = (bf16[64,1024]{1,0:T(8,128)(2,1)S(1)}, bf16[64,1024]{1,0:T(8,128)(2,1)S(1)}, u32[]{:S(2)}, u32[]{:S(2)}) collective-permute-start(bf16[64,1024]{1,0:T(8,128)(2,1)S(1)} %add_convert_fusion.5), channel_id=1, source_target_pairs={{0,2},{1,3},{2,0},{3,1},{4,6},{5,7},{6,4},{7,5},{8,10},{9,11},{10,... | collective-permute-start | bytes 393224 | tf_op jit(solution)/shard_map/ppermute | solution.py:223
  127.5 7.8 %collective-permute-start.46 = (bf16[64,1024]{1,0:T(8,128)(2,1)S(1)}, bf16[64,1024]{1,0:T(8,128)(2,1)S(1)}, u32[]{:S(2)}, u32[]{:S(2)}) collective-permute-start(bf16[64,1024]{1,0:T(8,128)(2,1)S(1)} %add_convert_fusion.3), channel_id=1, source_target_pairs={{0,6},{1,7},{2,4},{3,5},{4,2},{5,3},{6,0},{7,1},{8,14},{9,15},{10,... | collective-permute-start | bytes 393224 | tf_op jit(solution)/shard_map/ppermute | solution.py:223
  135.4 11.6 %collective-permute-start.47 = (bf16[64,1024]{1,0:T(8,128)(2,1)S(1)}, bf16[64,1024]{1,0:T(8,128)(2,1)S(1)}, u32[]{:S(2)}, u32[]{:S(2)}) collective-permute-start(bf16[64,1024]{1,0:T(8,128)(2,1)S(1)} %masked_sum.1), channel_id=1, source_target_pairs={{0,0},{4,1},{8,2},{12,3},{16,4},{20,5},{24,6},{28,7},{1,8},{5,9},{... | collective-permute-start | bytes 393224 | tf_op jit(solution)/shard_map/ppermute | solution.py:444
where the time goes:
time: 148 us
  waiting for transfers between devices  59.6 us (40%)
  Pallas kernels  42.4 us (29%)
  starting transfers between devices  41.9 us (28%)
  between operations  1.72 us (1%)
    ppermute x46, waiting for transfers between devices, swap(): return lax.ppermute(value, 'tensor', [(i, i ^ bits) for i in range(size)])  51.2 us
    ppermute x46, starting transfers between devices, swap(): return lax.ppermute(value, 'tensor', [(i, i ^ bits) for i in range(size)])  36 us
    pallas_call x8, Pallas kernels, attention(): pl.pallas_call(functools.partial(attention_body, has_bias, parts, first_s...  26.5 us
    pallas_call x4, Pallas kernels, ffn(): pl.pallas_call(functools.partial(ffn_body, parts), in_specs=[IN_VMEM] * (...  9.75 us
    ppermute x1, waiting for transfers between devices, on_device(): dec_out = lax.ppermute(dec_sum, ('dp', 'tensor'), to_home)  8.45 us
    pallas_call x1, Pallas kernels, load(): pl.pallas_call(functools.partial(load_body, count), in_specs=[IN_HBM] * (...  3.51 us
    ppermute x1, starting transfers between devices, on_device(): dec_out = lax.ppermute(dec_sum, ('dp', 'tensor'), to_home)  3.16 us
  transfers between devices with their start and end apart: 48, of which 20 were waited for; matrix products, arithmetic and copies ran while one was open for 0% of the time, Pallas kernels for 28%

commit v1 on v0

--- a/solution.py
+++ b/solution.py
@@ -11,8 +11,7 @@
 MAXREL = 16
 NB = 33
 LANG_ROWS = 16
-TIE_OWN = True
-TIE_NEAR = False
+OPT = dict(enc="213", mem="213", ffn="213", p3=(), p1=(), dec="early", norm2=True, p3tie=("enc", "mem", "ffn"), straight=False, home="w", dtie=False, w="all", ls=2)
 EPSILON = 1e-06
 NEG_FILL = -1e30
 FFN_STEP = 512
@@ -41,8 +40,8 @@
 
 def load_body(count, *refs):
     sources = refs[:count + 1]
-    targets, bias = refs[count + 2:2 * count + 2], refs[2 * count + 2]
-    table, sems = refs[2 * count + 3:]
+    targets, bias = refs[count + 1:2 * count + 1], refs[2 * count + 1]
+    table, sems = refs[2 * count + 2:]
     copies = [
         pltpu.make_async_copy(source, target, sems.at[i])
         for i, (source, target) in enumerate(zip(sources, [*targets, table]))
@@ -63,13 +62,13 @@
         copy.wait()
 
 
-def load(weights, bias_table, query_len, key_len, earlier):
+def load(weights, bias_table, query_len, key_len):
     count = len(weights)
     heads = bias_table.shape[0]
     size = sum(w.size * w.dtype.itemsize for w in weights)
     return pl.pallas_call(
         functools.partial(load_body, count),
-        in_specs=[IN_HBM] * (count + 1) + [IN_VMEM],
+        in_specs=[IN_HBM] * (count + 1),
         out_specs=[IN_VMEM] * (count + 1),
         out_shape=[jax.ShapeDtypeStruct(w.shape, w.dtype) for w in weights]
         + [jax.ShapeDtypeStruct((heads, query_len, key_len), F32)],
@@ -80,14 +79,39 @@
         compiler_params=pltpu.CompilerParams(vmem_limit_bytes=VMEM_LIMIT),
         cost_estimate=pl.CostEstimate(flops=0, bytes_accessed=2 * size, transcendentals=0),
         name="load",
-    )(*in_hbm(*weights, bias_table), earlier)
+    )(*in_hbm(*weights, bias_table))
+
+
+def stack_body(*refs):
+    sources, out, sems = refs[:-2], refs[-2], refs[-1]
+    copies = [
+        pltpu.make_async_copy(source, out.at[i], sems.at[i]) for i, source in enumerate(sources)
+    ]
+    for copy in copies:
+        copy.start()
+    for copy in copies:
+        copy.wait()
+
+
+def load_stack(weights):
+    count = len(weights)
+    return pl.pallas_call(
+        stack_body,
+        in_specs=[IN_HBM] * count,
+        out_specs=IN_VMEM,
+        out_shape=jax.ShapeDtypeStruct((count,) + weights[0].shape, weights[0].dtype),
+        scratch_shapes=[pltpu.SemaphoreType.DMA((count,))],
+        compiler_params=pltpu.CompilerParams(vmem_limit_bytes=VMEM_LIMIT),
+        name="load_stack",
+    )(*in_hbm(*weights))
 
 
 def dot(a, b):
     return jnp.dot(a, b, preferred_element_type=F32)
 
 
-def softmax_contexts(query, key, value, bias, masks, parts):
+def softmax_contexts(query, key, value, bias, masks):
+    parts = len(masks)
     query_len, key_len = query.shape[0] // parts, key.shape[0] // parts
     ones = jnp.ones((key_len, HD), BF16)
     units = [(i, h) for i in range(parts) for h in range(query.shape[1] // HD)]
@@ -120,62 +144,79 @@
     )
 
 
-def attention_body(has_bias, parts, first_slot, size, *refs):
-    refs = list(refs)
-    lengths = refs.pop(0)
-    key_parts = [refs.pop(0) for _ in range(parts)]
-    queries_in = [] if has_bias else [refs.pop(0), refs.pop(0)]
-    wq, wk, wv, wo = [refs.pop(0) for _ in range(4)]
-    bias = refs.pop(0) if has_bias else None
-    outs = refs
-    key_len, query_len = key_parts[0].shape[0], outs[0].shape[0]
-    key_rows = jnp.concatenate([ref[...] for ref in key_parts], axis=0)
-    query_rows = key_rows
+def self_body(parts, first_slot, size, *refs):
+    lengths, rows_in, weights = refs[0], refs[1:1 + parts], refs[1 + parts:5 + parts]
+    bias, gain, outs = refs[5 + parts], refs[6 + parts], refs[7 + parts:]
+    rows = jnp.concatenate([ref[...] for ref in rows_in], axis=0)
+    rows = rms_norm(rows.astype(F32), gain[...]).astype(BF16)
+    length = rows_in[0].shape[0]
     first = lax.axis_index("dp") * size
     here = lax.axis_index("tensor")
-    if not has_bias:
-        query_rows = jnp.concatenate(
-            [queries_in[i][first_slot // 2] for i in range(parts)], axis=0
-        )
-    key_index = lax.broadcasted_iota(jnp.int32, (query_len, key_len), 1)
+    key_index = lax.broadcasted_iota(jnp.int32, (length, length), 1)
     masks = [key_index < lengths[first + (here ^ (first_slot + i))] for i in range(parts)]
-    keys = dot(key_rows, wk[...]).astype(BF16)
-    values = dot(key_rows, wv[...]).astype(BF16)
-    queries = dot(query_rows, wq[...]).astype(BF16)
-    context = softmax_contexts(queries, keys, values, bias, masks, parts)
-    term = dot(context, wo[...]).astype(BF16)
+    queries, keys, values = [dot(rows, weights[i][...]).astype(BF16) for i in range(3)]
+    context = softmax_contexts(queries, keys, values, bias, masks)
+    term = dot(context, weights[3][...]).astype(BF16)
     for i in range(parts):
-        outs[i][...] = term[i * query_len:(i + 1) * query_len]
-
-
-def attention(lengths, first_slot, key_parts, queries_in, wq, wk, wv, wo, bias):
-    parts = len(key_parts)
-    key_len, width = key_parts[0].shape
-    query_len = queries_in[0].shape[1] if queries_in else key_len
-    columns = wq.shape[1]
-    has_bias = bias is not None
-    operands = list(key_parts)
-    if queries_in:
-        operands += queries_in
-    operands += [wq, wk, wv, wo]
-    if has_bias:
-        operands += [bias]
-    rows_q, rows_k = parts * query_len, parts * key_len
-    return pl.pallas_call(
-        functools.partial(
-            attention_body, has_bias, parts, first_slot, lax.axis_size("tensor")
-        ),
+        outs[i][...] = term[i * length:(i + 1) * length]
+
+
+def self_attention(lengths, first_slot, rows, weights, bias, gain):
+    parts = len(rows)
+    length, width = rows[0].shape
+    columns = weights[0].shape[1]
+    operands = [*rows, *weights, bias, gain]
+    return pl.pallas_call(
+        functools.partial(self_body, parts, first_slot, lax.axis_size("tensor")),
         in_specs=[IN_SMEM] + [IN_VMEM] * len(operands),
         out_specs=[IN_VMEM] * parts,
-        out_shape=[jax.ShapeDtypeStruct((query_len, width), BF16)] * parts,
+        out_shape=[jax.ShapeDtypeStruct((length, width), BF16)] * parts,
         compiler_params=pltpu.CompilerParams(vmem_limit_bytes=VMEM_LIMIT),
         cost_estimate=pl.CostEstimate(
-            flops=4 * width * columns * (rows_q + rows_k) + 4 * rows_q * key_len * columns,
-            bytes_accessed=4 * width * (rows_q + rows_k),
+            flops=parts * length * columns * (8 * width + 4 * length),
+            bytes_accessed=4 * parts * length * width,
             transcendentals=0,
         ),
-        name="enc_attention" if has_bias else "cross_attention",
+        name="self_attention",
     )(lengths, *operands)
+
+
+def cross_body(slot, size, stacks, lengths, keys_in, queries_in, *refs):
+    own = [ref.at[i] for ref in refs[:stacks] for i in range(ref.shape[0])]
+    other = [ref.at[i] for ref in refs[stacks:2 * stacks] for i in range(ref.shape[0])]
+    out = refs[-1]
+    length = lengths[lax.axis_index("dp") * size + (lax.axis_index("tensor") ^ slot)]
+    shape = (queries_in.shape[0], keys_in.shape[0])
+    mask = lax.broadcasted_iota(jnp.int32, shape, 1) < length
+
+    def project(rows, which):
+        parts = [dot(rows[...], weights[which][...]) for weights in (own, other)]
+        return jnp.concatenate(parts, axis=1).astype(BF16)
+
+    queries, keys, values = project(queries_in, 0), project(keys_in, 1), project(keys_in, 2)
+    context = softmax_contexts(queries, keys, values, None, [mask])
+    half = context.shape[1] // 2
+    term = dot(context[:, :half], own[3][...]) + dot(context[:, half:], other[3][...])
+    out[...] = term.astype(BF16)
+
+
+def cross_attention(lengths, slot, key_rows, query_rows, own, other):
+    key_len, width = key_rows.shape
+    query_len = query_rows.shape[0]
+    columns = own[0].shape[2] * 2
+    return pl.pallas_call(
+        functools.partial(cross_body, slot, lax.axis_size("tensor"), len(own)),
+        in_specs=[IN_SMEM] + [IN_VMEM] * (2 + 2 * len(own)),
+        out_specs=IN_VMEM,
+        out_shape=jax.ShapeDtypeStruct((query_len, width), BF16),
+        compiler_params=pltpu.CompilerParams(vmem_limit_bytes=VMEM_LIMIT),
+        cost_estimate=pl.CostEstimate(
+            flops=4 * columns * (width * (query_len + key_len) + query_len * key_len),
+            bytes_accessed=4 * width * (query_len + key_len),
+            transcendentals=0,
+        ),
+        name="cross_attention",
+    )(lengths, key_rows, query_rows, *own, *other)
 
 
 def ffn_body(parts, *refs):
@@ -231,8 +272,7 @@
         for k in sorted(slots):
             slots[k ^ bit] = swap(slots[k], bit)
         bit //= 2
-    own = jnp.stack([slots[2 * k] for k in range(size // 2)])
-    return own, swap(own, 1), [slots[size // 2], slots[size // 4]]
+    return [slots[2 * k] for k in range(size // 2)]
 
 
 def bf16_sum(*terms):
@@ -242,83 +282,95 @@
     return total.astype(BF16)
 
 
-def exchange(block, run, before_last=()):
+def pair_order(name, last):
+    if OPT[name] == "213":
+        return [*range(2, last, 2), *range(1, last + 1, 2)]
+    return list(range(1, last + 1))
+
+
+def exchange(name, block, run, both, hook=None, done=None, straight=False):
     size = lax.axis_size("tensor")
     last = size // 2 - 1
-    outs = {0: run(0, [block, swap(block, 1)])}
-    addends = [outs[0][0], swap(outs[0][1], 1)]
+    before, late = {}, []
+    order = pair_order(name, last)
+
+    def work(k, rows, other_rows):
+        if not both:
+            return [run(k, rows)]
+        own, other = run(k, [rows, other_rows])
+        return [own, swap(other, 1)]
+
+    block_other = swap(block, 1) if both else block
+    addends = work(0, block, block_other)
+    if hook is not None:
+        before, late = hook(addends[0])
     slots = {0: block}
     bit = size // 2
     while bit > 1:
         for k in sorted(slots):
             slots[k ^ bit] = swap(slots[k], bit)
         bit //= 2
-        if bit > 1:
+        if bit > 1 and name in OPT["p3tie"]:
             for k in sorted(slots):
                 if k:
-                    slots[k] = after(slots[k], outs[0][0])
-    near, held = {}, [addends[1]] if TIE_OWN else [outs[0][0]]
-    for k in [*range(2, last, 2), *range(1, last + 1, 2)]:
-        first = slots[2 * k]
-        if k == last:
-            held += before_last
-        if k in near and TIE_NEAR:
-            held.append(near[k])
-        outs[k] = run(k, [after(first, *held), swap(after(first, *held) if k == last else first, 1)])
-        held = [outs[k][0]]
-        terms = [outs[k][0], swap(outs[k][1], 1)]
+                    slots[k] = after(slots[k], addends[0])
+    near, held, far = {}, [addends[0]], {}
+    for k in order:
+        held += before.get(k, [])
+        if k == 1 and name in OPT["p3"]:
+            held.append(slots[2 * last])
+        ready = after(slots[2 * k], *held)
+        other = ready if k == last else slots[2 * k]
+        terms = work(k, ready, swap(other, 1) if both else None)
+        held = [terms[0]]
         if k in near:
             terms.append(near[k])
-        partial_sum = bf16_sum(*terms)
-        if k % 2:
+        if k == last and late:
+            terms[0] = after(terms[0], *late)
+        partial_sum = bf16_sum(*terms) if len(terms) > 1 else terms[0]
+        if done is not None:
+            done[k] = partial_sum
+        if k % 2 == 0:
+            near[k + 1] = swap(partial_sum, 2)
+        elif k == 1 or not straight:
             addends.append(swap(partial_sum, 2 * k))
         else:
-            near[k + 1] = swap(partial_sum, 2)
-    return addends
-
-
-def prologue_body(tokens, gain, dec_rows, table, tags, ends, normed, sent, *scratch):
-    buffers, sems = scratch[:6], scratch[6]
+            far[k] = partial_sum
+    return (addends, far) if straight else addends
+
+
+def decoder_body(tags, dec_rows, table, sent, *scratch):
+    langs, sems = scratch
     copies = [
-        pltpu.make_async_copy(source, target, sems.at[i])
-        for i, (source, target) in enumerate(
-            zip((tokens, gain, dec_rows, table, tags, ends), buffers)
-        )
+        pltpu.make_async_copy(dec_rows, sent.at[:dec_rows.shape[0]], sems.at[0]),
+        pltpu.make_async_copy(table, langs, sems.at[1]),
     ]
     for copy in copies:
         copy.start()
     for copy in copies:
         copy.wait()
-    normed[...] = rms_norm(buffers[0][...].astype(F32), buffers[1][...]).astype(BF16)
     count = dec_rows.shape[0]
-    sent[:count, :] = buffers[2][...]
-    langs, width = table.shape
-    tag = buffers[4][lax.axis_index("tensor")]
-    chosen = lax.broadcasted_iota(jnp.int32, (langs, width), 0) == tag
-    row = jnp.sum(jnp.where(chosen, buffers[3][...].astype(F32), 0.0), axis=0, keepdims=True)
-    shape = (sent.shape[0] - count, width)
-    end = jnp.full(shape, buffers[5][0], jnp.int32).astype(F32)
-    is_row = lax.broadcasted_iota(jnp.int32, shape, 0) == 0
-    sent[count:, :] = jnp.where(is_row, jnp.broadcast_to(row, shape), end).astype(BF16)
-
-
-def prologue(tokens, gain, dec_rows, table, tags, ends):
-    (rows, width), count = tokens.shape, dec_rows.shape[0]
-    operands = [tokens, gain[None, :], dec_rows, table, tags, ends]
-    return pl.pallas_call(
-        prologue_body,
-        in_specs=[IN_HBM] * 6,
-        out_specs=[IN_VMEM] * 2,
-        out_shape=[
-            jax.ShapeDtypeStruct((rows, width), BF16),
-            jax.ShapeDtypeStruct((count + LANG_ROWS, width), BF16),
+    tag = tags[lax.axis_index("tensor")]
+    chosen = lax.broadcasted_iota(jnp.int32, langs.shape, 0) == tag
+    row = jnp.sum(jnp.where(chosen, langs[...].astype(F32), 0.0), axis=0, keepdims=True)
+    shape = (sent.shape[0] - count, langs.shape[1])
+    sent[count:, :] = jnp.broadcast_to(row, shape).astype(BF16)
+
+
+def decoder_rows(dec_rows, table, tags):
+    count, width = dec_rows.shape
+    return pl.pallas_call(
+        decoder_body,
+        in_specs=[IN_SMEM] + [IN_HBM] * 2,
+        out_specs=IN_VMEM,
+        out_shape=jax.ShapeDtypeStruct((count + LANG_ROWS, width), BF16),
+        scratch_shapes=[
+            pltpu.VMEM(table.shape, table.dtype),
+            pltpu.SemaphoreType.DMA((2,)),
         ],
-        scratch_shapes=[pltpu.VMEM(x.shape, x.dtype) for x in operands[:4]]
-        + [pltpu.SMEM(x.shape, x.dtype) for x in operands[4:]]
-        + [pltpu.SemaphoreType.DMA((6,))],
-        compiler_params=pltpu.CompilerParams(vmem_limit_bytes=VMEM_LIMIT),
-        name="prologue",
-    )(*in_hbm(*operands[:4]), *operands[4:])
+        compiler_params=pltpu.CompilerParams(vmem_limit_bytes=VMEM_LIMIT),
+        name="decoder_rows",
+    )(tags, *in_hbm(dec_rows, table))
 
 
 def norm_body(count, copies, *refs):
@@ -354,12 +406,11 @@
 
 
 def masked_body(count, *refs):
-    addends, ends, out = refs[:count], refs[count], refs[count + 1]
+    ends, addends, out = refs[0], refs[1:count + 1], refs[count + 1]
     total = addends[0][...].astype(F32)
     for ref in addends[1:]:
         total = total + ref[...].astype(F32)
-    row = lax.broadcasted_iota(jnp.int32, total.shape, 0).astype(F32)
-    keep = row < ends[:, :1].astype(F32)
+    keep = lax.broadcasted_iota(jnp.int32, total.shape, 0) < ends[0]
     out[...] = jnp.where(keep, total, 0.0).astype(BF16)
 
 
@@ -367,10 +418,12 @@
     rows, width = addends[0].shape
     return pl.pallas_call(
         functools.partial(masked_body, len(addends)),
+        in_specs=[IN_SMEM] + [IN_VMEM] * len(addends),
+        out_specs=IN_VMEM,
         out_shape=jax.ShapeDtypeStruct((rows, width), BF16),
         compiler_params=pltpu.CompilerParams(vmem_limit_bytes=VMEM_LIMIT),
         name="masked_sum",
-    )(*addends, ends)
+    )(ends, *addends)
 
 
 def on_device(
@@ -408,40 +461,69 @@
         to_source.append((row, (m // per_pair) * size + (m % per_pair) * groups + j))
     to_home = [(b, a) for a, b in to_source]
 
-    enc_normed, sent = prologue(
-        enc_tokens[0], enc_gain, dec_tokens[0], lang_table, lang_tags, tgt_lengths
+    *enc_weights, bias = load(
+        [enc_query, enc_key, enc_value, enc_output], enc_bias, src_len, src_len
     )
-    *enc_weights, bias = load(
-        [enc_query, enc_key, enc_value, enc_output], enc_bias, src_len, src_len, enc_normed
-    )
-
+    sent = decoder_rows(dec_tokens[0], lang_table, lang_tags)
+    if OPT["home"] != "free":
+        sent = after(sent, enc_weights[0])
     arrived = lax.ppermute(sent, ("dp", "tensor"), to_source)
     dec_rows = arrived[:target_len]
     dec_lang = jnp.broadcast_to(arrived[target_len:target_len + 1], dec_rows.shape)
     dec_normed, dec_input = norm_sum([dec_rows, dec_lang], cross_gain, 1, True)
-    def enc_pair(k, blocks):
-        return attention(src_lengths, 2 * k, blocks, None, *enc_weights, bias)
-
-    dec_own, dec_other, early = spread(dec_normed)
-    enc_terms = exchange(enc_normed, enc_pair, early)
+    def enc_run(k, rows):
+        return self_attention(src_lengths, 2 * k, rows, enc_weights, bias, enc_gain[None, :])
+
+    dec_slots, done = [], {}
+    stacks = [[cross_query, cross_key, cross_value, cross_output]]
+    if cross_query.shape != cross_output.shape:
+        stacks = [stacks[0][:3], stacks[0][3:]]
+    cross_own = [load_stack(weights) for weights in stacks]
+
+    def hook(out):
+        rows = after(dec_normed, out) if OPT["dtie"] else dec_normed
+        dec_slots.extend(spread(rows))
+        wanted = [dec_slots[1], dec_slots[size // 4]]
+        before = {2: [dec_normed]} if OPT["norm2"] else {}
+        late = []
+        before[OPT["ls"]] = before.get(OPT["ls"], []) + cross_own
+        if OPT["dec"] == "early":
+            before[1] = before.get(1, []) + wanted[:1]
+            before[size // 2 - 1] = before.get(size // 2 - 1, []) + wanted[1:]
+        elif OPT["dec"] == "last":
+            before[size // 2 - 1] = before.get(size // 2 - 1, []) + wanted
+        elif OPT["dec"] == "late":
+            late = wanted
+        return before, late
+
+    enc_terms = exchange("enc", enc_tokens[0], enc_run, True, hook, done)
     memory_out, enc_memory = norm_sum([enc_tokens[0]] + enc_terms, mem_gain, 2, False)
 
-    def cross_pair(k, blocks):
-        return attention(
-            src_lengths, 2 * k, blocks, [dec_own, dec_other],
-            cross_query, cross_key, cross_value, cross_output, None,
-        )
-
-    cross_terms = exchange(enc_memory, cross_pair)
+    last_sums = [*done.values(), enc_terms[1]] if OPT["w"] == "all" else [*done.values()]
+    if OPT["w"] == "got":
+        last_sums.append(enc_terms[2])
+    cross_other = [swap(after(stack, *last_sums), 1) for stack in cross_own]
+
+    def cross_run(k, rows):
+        return cross_attention(src_lengths, 2 * k, rows, dec_slots[k], cross_own, cross_other)
+
+    cross_terms = exchange("mem", enc_memory, cross_run, False)
     ffn_normed, hidden = norm_sum([dec_input] + cross_terms, ffn_gain, 1, True)
 
     def ffn_pair(k, blocks):
         return ffn(blocks, ffn_in, ffn_out)
 
-    ffn_terms = exchange(ffn_normed, ffn_pair)
-    ends = jnp.broadcast_to(arrived[target_len + 1:target_len + 2, :HD], (target_len, HD))
-    dec_sum = masked_sum([hidden] + ffn_terms, ends)
-    dec_out = lax.ppermute(dec_sum, ("dp", "tensor"), to_home)
+    ffn_terms = exchange("ffn", ffn_normed, ffn_pair, True, straight=OPT["straight"])
+
+    far_terms = {}
+    if OPT["straight"]:
+        ffn_terms, far_terms = ffn_terms
+    home = dict(to_home)
+    arrivals = [lax.ppermute(bf16_sum(hidden, *ffn_terms), ("dp", "tensor"), to_home)]
+    for k, term in far_terms.items():
+        way = [(d, home[d ^ (2 * k)]) for d in range(groups * size)]
+        arrivals.append(lax.ppermute(term, ("dp", "tensor"), way))
+    dec_out = masked_sum(arrivals, tgt_lengths)
     return (memory_out[None], dec_out[None])
 
 

time: 148 us -> 144 us (0.973)
  waiting for transfers between devices: 59.6 us -> 48.9 us
  Pallas kernels: 42.4 us -> 51 us
    ppermute x46 -> x38, waiting for transfers between devices: 51.2 us -> 40.5 us  [swap(): return lax.ppermute(value, 'tensor', [(i, i ^ bits) for i in range(size)])]
    pallas_call x10 -> x11, Pallas kernels: 27.9 us -> 36.1 us  [the longest x4 15.6 us: cross_attention(): pl.pallas_call(functools.partial(cross_body, slot, lax.axis_size('tensor'...]
    ppermute x46 -> x38, starting transfers between devices: 36 us -> 33.2 us  [swap(): return lax.ppermute(value, 'tensor', [(i, i ^ bits) for i in range(size)])]
    ppermute x1, starting transfers between devices: 3.16 us -> 5.13 us  [on_device(): lax.ppermute(bf16_sum(hidden, *ffn_terms), ('dp', 'tensor'), to_home)]
  transfers between devices with their start and end apart: 48 -> 40, of which waited for: 20 -> 15; matrix products, arithmetic and copies ran while one was open for 0% -> 0% of each run, Pallas kernels for 28% -> 35%
where the time goes in v1:
time: 144 us
  Pallas kernels  51 us (35%)
  waiting for transfers between devices  48.9 us (34%)
  starting transfers between devices  40.7 us (28%)
  between operations  1.74 us (1%)
    ppermute x38, waiting for transfers between devices, swap(): return lax.ppermute(value, 'tensor', [(i, i ^ bits) for i in range(size)])  40.5 us
    ppermute x38, starting transfers between devices, swap(): return lax.ppermute(value, 'tensor', [(i, i ^ bits) for i in range(size)])  33.2 us
    pallas_call x4, Pallas kernels, cross_attention(): pl.pallas_call(functools.partial(cross_body, slot, lax.axis_size('tensor'...  15.6 us
    pallas_call x4, Pallas kernels, self_attention(): pl.pallas_call(functools.partial(self_body, parts, first_slot, lax.axis_s...  14.9 us
    pallas_call x4, Pallas kernels, ffn(): pl.pallas_call(functools.partial(ffn_body, parts), in_specs=[IN_VMEM] * (...  10 us
    ppermute x1, waiting for transfers between devices, on_device(): lax.ppermute(bf16_sum(hidden, *ffn_terms), ('dp', 'tensor'), to_home)  8.27 us
    ppermute x1, starting transfers between devices, on_device(): lax.ppermute(bf16_sum(hidden, *ffn_terms), ('dp', 'tensor'), to_home)  5.13 us
    pallas_call x1, Pallas kernels, load(): pl.pallas_call(functools.partial(load_body, count), in_specs=[IN_HBM] * (...  3.55 us
  transfers between devices with their start and end apart: 40, of which 15 were waited for; matrix products, arithmetic and copies ran while one was open for 0% of the time, Pallas kernels for 35%

profile of v1, /device:TPU:4, one launch (start us, length us, event | category | flops | bytes accessed | tf_op | source)
XLA Modules:
  0.0 143.5 jit_solution(1568620706289041898)
XLA Ops:
  0.7 2.7 %collective-permute-start.3 = (bf16[128,1024]{1,0:T(8,128)(2,1)}, bf16[128,1024]{1,0:T(8,128)(2,1)S(1)}, u32[]{:S(2)}, u32[]{:S(2)}) collective-permute-start(bf16[128,1024]{1,0:T(8,128)(2,1)} %bitcast.13), channel_id=1, source_target_pairs={{0,4},{1,5},{2,6},{3,7},{4,0},{5,1},{6,2},{7,3},{8,12},{9,13},{10,... | collective-permute-start | bytes 786440 | tf_op jit(solution)/shard_map/ppermute | solution.py:264
  3.4 1.6 %collective-permute-start.2 = (bf16[128,1024]{1,0:T(8,128)(2,1)}, bf16[128,1024]{1,0:T(8,128)(2,1)S(1)}, u32[]{:S(2)}, u32[]{:S(2)}) collective-permute-start(bf16[128,1024]{1,0:T(8,128)(2,1)} %bitcast.14), channel_id=1, source_target_pairs={{0,2},{1,3},{2,0},{3,1},{4,6},{5,7},{6,4},{7,5},{8,10},{9,11},{10,... | collective-permute-start | bytes 786440 | tf_op jit(solution)/shard_map/ppermute | solution.py:264
  4.9 0.7 copy-done.6
  5.6 1.5 %decoder_rows.1 = bf16[80,1024]{1,0:T(8,128)(2,1)S(1)} custom-call(s32[8]{0:T(128)S(1)} %copy-done.6, bf16[64,1024]{1,0:T(8,128)(2,1)} %bitcast.24, bf16[8,1024]{1,0:T(8,128)(2,1)} %table.1), custom_call_target="tpu_custom_call" | custom-call | tf_op jit(solution)/shard_map/decoder_rows/pallas_call | solution.py:362
  7.1 3.5 %load.1 = (bf16[1024,1024]{1,0:T(8,128)(2,1)S(1)}, bf16[1024,1024]{1,0:T(8,128)(2,1)S(1)}, bf16[1024,1024]{1,0:T(8,128)(2,1)S(1)}, bf16[1024,1024]{1,0:T(8,128)(2,1)S(1)}, f32[8,128,128]{2,1,0:T(8,128)S(1)}) custom-call(bf16[1024,1024]{1,0:T(8,128)(2,1)} %refs_0_.7, bf16[1024,1024]{1,0:T(8,128)(2,1)} %refs_1_.2, bf16[1024,1024]{1,0:T(8,128)(2,1)} %refs_2_.6, ...), custom_call_target="tpu_custom_call" | custom-call | bytes 16777216 | tf_op jit(solution)/shard_map/load/pallas_call | solution.py:69
  10.7 2.3 %collective-permute-start.4 = (bf16[80,1024]{1,0:T(8,128)(2,1)S(1)}, bf16[80,1024]{1,0:T(8,128)(2,1)S(1)}, u32[]{:S(2)}, u32[]{:S(2)}) collective-permute-start(bf16[80,1024]{1,0:T(8,128)(2,1)S(1)} %decoder_rows.1), channel_id=1, source_target_pairs={{0,0},{1,4},{2,8},{3,12},{4,16},{5,20},{6,24},{7,28},{8,1},{9,5},{... | collective-permute-start | bytes 491528 | tf_op jit(solution)/shard_map/ppermute | solution.py:470
  13.0 3.7 %self_attention.4 = (bf16[128,1024]{1,0:T(8,128)(2,1)S(1)}, bf16[128,1024]{1,0:T(8,128)(2,1)S(1)}) custom-call(s32[32]{0:T(128)S(1)} %copy-done.2, bf16[128,1024]{1,0:T(8,128)(2,1)S(1)} %bitcast.15, bf16[128,1024]{1,0:T(8,128)(2,1)S(1)} %collective-permute-done.refs_2_, bf16[1024,1024]{1,0:T(8,128)(2,1)S(1)} %get-tuple-element.43.refs_3_, ...), custom_call_target="tpu_custom_call" | custom-call | flops 2281701376 | bytes 1048576 | tf_op jit(solution)/shard_map/self_attention/pallas_call | solution.py:169
  16.9 3.5 %load_stack.1.refs_0_ = bf16[4,1024,1024]{2,1,0:T(8,128)(2,1)S(1)} custom-call(bf16[1024,1024]{1,0:T(8,128)(2,1)} %refs_0_.9, bf16[1024,1024]{1,0:T(8,128)(2,1)} %refs_1_.3, bf16[1024,1024]{1,0:T(8,128)(2,1)} %refs_2_.7, bf16[1024,1024]{1,0:T(8,128)(2,1)} %refs_3_.7), custom_call_target="tpu_custom_call" | custom-call | tf_op jit(solution)/shard_map/load_stack/pallas_call | solution.py:98
  20.4 0.6 collective-permute-start.7
  21.1 0.1 sum_norm.3
  21.2 1.5 %collective-permute-start.6 = (bf16[64,1024]{1,0:T(8,128)(2,1)S(1)}, bf16[64,1024]{1,0:T(8,128)(2,1)S(1)}, u32[]{:S(2)}, u32[]{:S(2)}) collective-permute-start(bf16[64,1024]{1,0:T(8,128)(2,1)S(1)} %get-tuple-element.52.queries_in), channel_id=1, source_target_pairs={{0,2},{1,3},{2,0},{3,1},{4,6},{5,7},{6,4},{7,5},{8,10},{9,11},{10,... | collective-permute-start | bytes 393224 | tf_op jit(solution)/shard_map/ppermute | solution.py:264
  22.7 0.6 collective-permute-start.10
  23.3 3.7 %self_attention.5 = (bf16[128,1024]{1,0:T(8,128)(2,1)S(1)}, bf16[128,1024]{1,0:T(8,128)(2,1)S(1)}) custom-call(s32[32]{0:T(128)S(1)} %copy-done.2, bf16[128,1024]{1,0:T(8,128)(2,1)S(1)} %collective-permute-done.3.refs_1_, bf16[128,1024]{1,0:T(8,128)(2,1)S(1)} %collective-permute-done.5.refs_2_, bf16[1024,1024]{1,0:T(8,128)(2,1)S(1)} %get-tuple-element.43.refs_3_, ...), custom_call_target="tpu_custom_call" | custom-call | flops 2281701376 | bytes 1048576 | tf_op jit(solution)/shard_map/self_attention/pallas_call | solution.py:169
  27.1 0.2 collective-permute-start.14
  27.3 2.8 %collective-permute-start.11 = (bf16[64,1024]{1,0:T(8,128)(2,1)S(1)}, bf16[64,1024]{1,0:T(8,128)(2,1)S(1)}, u32[]{:S(2)}, u32[]{:S(2)}) collective-permute-start(bf16[64,1024]{1,0:T(8,128)(2,1)S(1)} %get-tuple-element.52.queries_in), channel_id=1, source_target_pairs={{0,4},{1,5},{2,6},{3,7},{4,0},{5,1},{6,2},{7,3},{8,12},{9,13},{10,... | collective-permute-start | bytes 393224 | tf_op jit(solution)/shard_map/ppermute | solution.py:264
  30.1 3.7 %self_attention.6 = (bf16[128,1024]{1,0:T(8,128)(2,1)S(1)}, bf16[128,1024]{1,0:T(8,128)(2,1)S(1)}) custom-call(s32[32]{0:T(128)S(1)} %copy-done.2, bf16[128,1024]{1,0:T(8,128)(2,1)S(1)} %collective-permute-done.2.refs_1_, bf16[128,1024]{1,0:T(8,128)(2,1)S(1)} %collective-permute-done.7.refs_2_, bf16[1024,1024]{1,0:T(8,128)(2,1)S(1)} %get-tuple-element.43.refs_3_, ...), custom_call_target="tpu_custom_call" | custom-call | flops 2281701376 | bytes 1048576 | tf_op jit(solution)/shard_map/self_attention/pallas_call | solution.py:169
  33.8 0.3 collective-permute-done.11.queries_in
  34.1 1.7 %collective-permute-done.10.refs_1_ = bf16[128,1024]{1,0:T(8,128)(2,1)S(1)} collective-permute-done((bf16[128,1024]{1,0:T(8,128)(2,1)S(1)}, bf16[128,1024]{1,0:T(8,128)(2,1)S(1)}, u32[]{:S(2)}, u32[]{:S(2)}) %collective-permute-start.10) | collective-permute-done | bytes 262176 | tf_op jit(solution)/shard_map/ppermute | solution.py:264
  35.9 0.5 collective-permute-start.8
  36.5 2.7 %collective-permute-start.15 = (bf16[128,1024]{1,0:T(8,128)(2,1)S(1)}, bf16[128,1024]{1,0:T(8,128)(2,1)S(1)}, u32[]{:S(2)}, u32[]{:S(2)}) collective-permute-start(bf16[128,1024]{1,0:T(8,128)(2,1)S(1)} %add_convert_fusion.1), channel_id=1, source_target_pairs={{0,2},{1,3},{2,0},{3,1},{4,6},{5,7},{6,4},{7,5},{8,10},{9,11},{10,... | collective-permute-start | bytes 786440 | tf_op jit(solution)/shard_map/ppermute | solution.py:264
  39.1 3.7 %self_attention.7 = (bf16[128,1024]{1,0:T(8,128)(2,1)S(1)}, bf16[128,1024]{1,0:T(8,128)(2,1)S(1)}) custom-call(s32[32]{0:T(128)S(1)} %copy-done.2, bf16[128,1024]{1,0:T(8,128)(2,1)S(1)} %collective-permute-done.10.refs_1_, bf16[128,1024]{1,0:T(8,128)(2,1)S(1)} %collective-permute-done.12.refs_2_, bf16[1024,1024]{1,0:T(8,128)(2,1)S(1)} %get-tuple-element.43.refs_3_, ...), custom_call_target="tpu_custom_call" | custom-call | flops 2281701376 | bytes 1048576 | tf_op jit(solution)/shard_map/self_attention/pallas_call | solution.py:169
  42.9 0.5 collective-permute-start.1
  43.5 2.2 %collective-permute-done.15 = bf16[128,1024]{1,0:T(8,128)(2,1)S(1)} collective-permute-done((bf16[128,1024]{1,0:T(8,128)(2,1)S(1)}, bf16[128,1024]{1,0:T(8,128)(2,1)S(1)}, u32[]{:S(2)}, u32[]{:S(2)}) %collective-permute-start.15) | collective-permute-done | bytes 262176 | tf_op jit(solution)/shard_map/ppermute | solution.py:264
  45.7 0.1 add_convert_fusion
  45.9 1.8 %collective-permute-start.9 = (bf16[128,1024]{1,0:T(8,128)(2,1)S(1)}, bf16[128,1024]{1,0:T(8,128)(2,1)S(1)}, u32[]{:S(2)}, u32[]{:S(2)}) collective-permute-start(bf16[128,1024]{1,0:T(8,128)(2,1)S(1)} %add_convert_fusion.2), channel_id=1, source_target_pairs={{0,2},{1,3},{2,0},{3,1},{4,6},{5,7},{6,4},{7,5},{8,10},{9,11},{10,... | collective-permute-start | bytes 786440 | tf_op jit(solution)/shard_map/ppermute | solution.py:264
  47.8 2.1 %collective-permute-start.16 = (bf16[128,1024]{1,0:T(8,128)(2,1)S(1)}, bf16[128,1024]{1,0:T(8,128)(2,1)S(1)}, u32[]{:S(2)}, u32[]{:S(2)}) collective-permute-start(bf16[128,1024]{1,0:T(8,128)(2,1)S(1)} %add_convert_fusion), channel_id=1, source_target_pairs={{0,6},{1,7},{2,4},{3,5},{4,2},{5,3},{6,0},{7,1},{8,14},{9,15},{10,... | collective-permute-start | bytes 786440 | tf_op jit(solution)/shard_map/ppermute | solution.py:264
  49.9 4.8 %collective-permute-done.9.refs_3_ = bf16[128,1024]{1,0:T(8,128)(2,1)S(1)} collective-permute-done((bf16[128,1024]{1,0:T(8,128)(2,1)S(1)}, bf16[128,1024]{1,0:T(8,128)(2,1)S(1)}, u32[]{:S(2)}, u32[]{:S(2)}) %collective-permute-start.9) | collective-permute-done | bytes 262176 | tf_op jit(solution)/shard_map/ppermute | solution.py:264
  54.7 7.6 %collective-permute-done.16.refs_4_ = bf16[128,1024]{1,0:T(8,128)(2,1)S(1)} collective-permute-done((bf16[128,1024]{1,0:T(8,128)(2,1)S(1)}, bf16[128,1024]{1,0:T(8,128)(2,1)S(1)}, u32[]{:S(2)}, u32[]{:S(2)}) %collective-permute-start.16) | collective-permute-done | bytes 262176 | tf_op jit(solution)/shard_map/ppermute | solution.py:264
  62.2 1.0 sum_norm.4
  63.2 1.9 %collective-permute-start.19 = (bf16[128,1024]{1,0:T(8,128)(2,1)S(1)}, bf16[128,1024]{1,0:T(8,128)(2,1)S(1)}, u32[]{:S(2)}, u32[]{:S(2)}) collective-permute-start(bf16[128,1024]{1,0:T(8,128)(2,1)S(1)} %get-tuple-element.64.keys_in), channel_id=1, source_target_pairs={{0,4},{1,5},{2,6},{3,7},{4,0},{5,1},{6,2},{7,3},{8,12},{9,13},{10,... | collective-permute-start | bytes 786440 | tf_op jit(solution)/shard_map/ppermute | solution.py:264
  65.2 0.3 collective-permute-start.22
  65.5 1.7 %collective-permute-start.18 = (bf16[128,1024]{1,0:T(8,128)(2,1)S(1)}, bf16[128,1024]{1,0:T(8,128)(2,1)S(1)}, u32[]{:S(2)}, u32[]{:S(2)}) collective-permute-start(bf16[128,1024]{1,0:T(8,128)(2,1)S(1)} %get-tuple-element.64.keys_in), channel_id=1, source_target_pairs={{0,2},{1,3},{2,0},{3,1},{4,6},{5,7},{6,4},{7,5},{8,10},{9,11},{10,... | collective-permute-start | bytes 786440 | tf_op jit(solution)/shard_map/ppermute | solution.py:264
  67.2 4.0 %cross_attention.4.refs_1_ = bf16[64,1024]{1,0:T(8,128)(2,1)S(1)} custom-call(s32[32]{0:T(128)S(1)} %copy-done.2, bf16[128,1024]{1,0:T(8,128)(2,1)S(1)} %get-tuple-element.64.keys_in, bf16[64,1024]{1,0:T(8,128)(2,1)S(1)} %get-tuple-element.52.queries_in, bf16[4,1024,1024]{2,1,0:T(8,128)(2,1)S(1)} %load_stack.1.refs_0_, ...), custom_call_target="tpu_custom_call" | custom-call | flops 1677721600 | bytes 786432 | tf_op jit(solution)/shard_map/cross_attention/pallas_call | solution.py:207
  71.2 5.5 %collective-permute-done.19.keys_in = bf16[128,1024]{1,0:T(8,128)(2,1)S(1)} collective-permute-done((bf16[128,1024]{1,0:T(8,128)(2,1)S(1)}, bf16[128,1024]{1,0:T(8,128)(2,1)S(1)}, u32[]{:S(2)}, u32[]{:S(2)}) %collective-permute-start.19) | collective-permute-done | bytes 262176 | tf_op jit(solution)/shard_map/ppermute | solution.py:264
  76.7 3.9 %cross_attention.5 = bf16[64,1024]{1,0:T(8,128)(2,1)S(1)} custom-call(s32[32]{0:T(128)S(1)} %copy-done.2, bf16[128,1024]{1,0:T(8,128)(2,1)S(1)} %collective-permute-done.19.keys_in, bf16[64,1024]{1,0:T(8,128)(2,1)S(1)} %collective-permute-done.11.queries_in, bf16[4,1024,1024]{2,1,0:T(8,128)(2,1)S(1)} %load_stack.1.refs_0_, ...), custom_call_target="tpu_custom_call" | custom-call | flops 1677721600 | bytes 786432 | tf_op jit(solution)/shard_map/cross_attention/pallas_call | solution.py:207
  80.6 2.1 %collective-permute-start.23 = (bf16[64,1024]{1,0:T(8,128)(2,1)S(1)}, bf16[64,1024]{1,0:T(8,128)(2,1)S(1)}, u32[]{:S(2)}, u32[]{:S(2)}) collective-permute-start(bf16[64,1024]{1,0:T(8,128)(2,1)S(1)} %cross_attention.5), channel_id=1, source_target_pairs={{0,2},{1,3},{2,0},{3,1},{4,6},{5,7},{6,4},{7,5},{8,10},{9,11},{10,... | collective-permute-start | bytes 393224 | tf_op jit(solution)/shard_map/ppermute | solution.py:264
  82.7 3.9 %cross_attention.6 = bf16[64,1024]{1,0:T(8,128)(2,1)S(1)} custom-call(s32[32]{0:T(128)S(1)} %copy-done.2, bf16[128,1024]{1,0:T(8,128)(2,1)S(1)} %collective-permute-done.18.keys_in, bf16[64,1024]{1,0:T(8,128)(2,1)S(1)} %collective-permute-done.6.queries_in, bf16[4,1024,1024]{2,1,0:T(8,128)(2,1)S(1)} %load_stack.1.refs_0_, ...), custom_call_target="tpu_custom_call" | custom-call | flops 1677721600 | bytes 786432 | tf_op jit(solution)/shard_map/cross_attention/pallas_call | solution.py:207
  86.6 0.1 collective-permute-start.20
  86.7 1.1 collective-permute-done.21.keys_in
  87.8 3.9 %cross_attention.7 = bf16[64,1024]{1,0:T(8,128)(2,1)S(1)} custom-call(s32[32]{0:T(128)S(1)} %copy-done.2, bf16[128,1024]{1,0:T(8,128)(2,1)S(1)} %collective-permute-done.21.keys_in, bf16[64,1024]{1,0:T(8,128)(2,1)S(1)} %collective-permute-done.22.queries_in, bf16[4,1024,1024]{2,1,0:T(8,128)(2,1)S(1)} %load_stack.1.refs_0_, ...), custom_call_target="tpu_custom_call" | custom-call | flops 1677721600 | bytes 786432 | tf_op jit(solution)/shard_map/cross_attention/pallas_call | solution.py:207
  91.8 1.6 %collective-permute-start.24 = (bf16[64,1024]{1,0:T(8,128)(2,1)S(1)}, bf16[64,1024]{1,0:T(8,128)(2,1)S(1)}, u32[]{:S(2)}, u32[]{:S(2)}) collective-permute-start(bf16[64,1024]{1,0:T(8,128)(2,1)S(1)} %add_convert_fusion.7), channel_id=1, source_target_pairs={{0,6},{1,7},{2,4},{3,5},{4,2},{5,3},{6,0},{7,1},{8,14},{9,15},{10,... | collective-permute-start | bytes 393224 | tf_op jit(solution)/shard_map/ppermute | solution.py:264
  93.4 5.3 %collective-permute-done.24.refs_3_ = bf16[64,1024]{1,0:T(8,128)(2,1)S(1)} collective-permute-done((bf16[64,1024]{1,0:T(8,128)(2,1)S(1)}, bf16[64,1024]{1,0:T(8,128)(2,1)S(1)}, u32[]{:S(2)}, u32[]{:S(2)}) %collective-permute-start.24) | collective-permute-done | bytes 131104 | tf_op jit(solution)/shard_map/ppermute | solution.py:264
  98.7 0.2 sum_norm.5
  98.9 1.6 %collective-permute-start.28 = (bf16[64,1024]{1,0:T(8,128)(2,1)S(1)}, bf16[64,1024]{1,0:T(8,128)(2,1)S(1)}, u32[]{:S(2)}, u32[]{:S(2)}) collective-permute-start(bf16[64,1024]{1,0:T(8,128)(2,1)S(1)} %get-tuple-element.71.refs_0_), channel_id=1, source_target_pairs={{0,4},{1,5},{2,6},{3,7},{4,0},{5,1},{6,2},{7,3},{8,12},{9,13},{10,... | collective-permute-start | bytes 393224 | tf_op jit(solution)/shard_map/ppermute | solution.py:264
  100.6 0.5 collective-permute-start.27
  101.1 2.7 %feed_forward.4 = (bf16[64,1024]{1,0:T(8,128)(2,1)S(1)}, bf16[64,1024]{1,0:T(8,128)(2,1)S(1)}) custom-call(bf16[64,1024]{1,0:T(8,128)(2,1)S(1)} %get-tuple-element.71.refs_0_, bf16[64,1024]{1,0:T(8,128)(2,1)S(1)} %collective-permute-done.25.refs_1_, bf16[1024,4096]{1,0:T(8,128)(2,1)S(1)} %bitcast.9, bf16[4096,1024]{1,0:T(8,128)(2,1)S(1)} %bitcast.11), custom_call_target="tpu_custom_call" | custom-call | flops 2147483648 | bytes 524288 | tf_op jit(solution)/shard_map/feed_forward/pallas_call | solution.py:246
  103.8 4.7 %collective-permute-done.28.refs_0_ = bf16[64,1024]{1,0:T(8,128)(2,1)S(1)} collective-permute-done((bf16[64,1024]{1,0:T(8,128)(2,1)S(1)}, bf16[64,1024]{1,0:T(8,128)(2,1)S(1)}, u32[]{:S(2)}, u32[]{:S(2)}) %collective-permute-start.28) | collective-permute-done | bytes 131104 | tf_op jit(solution)/shard_map/ppermute | solution.py:264
  108.6 0.5 collective-permute-start.26
  109.2 0.8 collective-permute-done.29.refs_1_
  109.9 2.4 %feed_forward.5 = (bf16[64,1024]{1,0:T(8,128)(2,1)S(1)}, bf16[64,1024]{1,0:T(8,128)(2,1)S(1)}) custom-call(bf16[64,1024]{1,0:T(8,128)(2,1)S(1)} %collective-permute-done.28.refs_0_, bf16[64,1024]{1,0:T(8,128)(2,1)S(1)} %collective-permute-done.29.refs_1_, bf16[1024,4096]{1,0:T(8,128)(2,1)S(1)} %bitcast.9, bf16[4096,1024]{1,0:T(8,128)(2,1)S(1)} %bitcast.11), custom_call_target="tpu_custom_call" | custom-call | flops 2147483648 | bytes 524288 | tf_op jit(solution)/shard_map/feed_forward/pallas_call | solution.py:246
  112.4 0.2 collective-permute-start.36
  112.6 2.4 %feed_forward.6 = (bf16[64,1024]{1,0:T(8,128)(2,1)S(1)}, bf16[64,1024]{1,0:T(8,128)(2,1)S(1)}) custom-call(bf16[64,1024]{1,0:T(8,128)(2,1)S(1)} %collective-permute-done.27.refs_0_, bf16[64,1024]{1,0:T(8,128)(2,1)S(1)} %collective-permute-done.30.refs_1_, bf16[1024,4096]{1,0:T(8,128)(2,1)S(1)} %bitcast.9, bf16[4096,1024]{1,0:T(8,128)(2,1)S(1)} %bitcast.11), custom_call_target="tpu_custom_call" | custom-call | flops 2147483648 | bytes 524288 | tf_op jit(solution)/shard_map/feed_forward/pallas_call | solution.py:246
  115.0 0.4 collective-permute-start.34
  115.5 0.1 collective-permute-start.31
  115.6 1.3 collective-permute-start.37
  117.0 2.4 %feed_forward.7 = (bf16[64,1024]{1,0:T(8,128)(2,1)S(1)}, bf16[64,1024]{1,0:T(8,128)(2,1)S(1)}) custom-call(bf16[64,1024]{1,0:T(8,128)(2,1)S(1)} %collective-permute-done.33.refs_0_, bf16[64,1024]{1,0:T(8,128)(2,1)S(1)} %collective-permute-done.34.refs_1_, bf16[1024,4096]{1,0:T(8,128)(2,1)S(1)} %bitcast.9, bf16[4096,1024]{1,0:T(8,128)(2,1)S(1)} %bitcast.11), custom_call_target="tpu_custom_call" | custom-call | flops 2147483648 | bytes 524288 | tf_op jit(solution)/shard_map/feed_forward/pallas_call | solution.py:246
  119.6 1.1 collective-permute-start.32
  120.6 0.9 collective-permute-done.37
  121.5 1.6 %collective-permute-start.38 = (bf16[64,1024]{1,0:T(8,128)(2,1)S(1)}, bf16[64,1024]{1,0:T(8,128)(2,1)S(1)}, u32[]{:S(2)}, u32[]{:S(2)}) collective-permute-start(bf16[64,1024]{1,0:T(8,128)(2,1)S(1)} %add_convert_fusion.4), channel_id=1, source_target_pairs={{0,6},{1,7},{2,4},{3,5},{4,2},{5,3},{6,0},{7,1},{8,14},{9,15},{10,... | collective-permute-start | bytes 393224 | tf_op jit(solution)/shard_map/ppermute | solution.py:264
  123.1 2.4 %collective-permute-done.32 = bf16[64,1024]{1,0:T(8,128)(2,1)S(1)} collective-permute-done((bf16[64,1024]{1,0:T(8,128)(2,1)S(1)}, bf16[64,1024]{1,0:T(8,128)(2,1)S(1)}, u32[]{:S(2)}, u32[]{:S(2)}) %collective-permute-start.32) | collective-permute-done | bytes 131104 | tf_op jit(solution)/shard_map/ppermute | solution.py:264
  125.5 3.2 %collective-permute-done.38 = bf16[64,1024]{1,0:T(8,128)(2,1)S(1)} collective-permute-done((bf16[64,1024]{1,0:T(8,128)(2,1)S(1)}, bf16[64,1024]{1,0:T(8,128)(2,1)S(1)}, u32[]{:S(2)}, u32[]{:S(2)}) %collective-permute-start.38) | collective-permute-done | bytes 131104 | tf_op jit(solution)/shard_map/ppermute | solution.py:264
  128.8 5.1 %collective-permute-start.39 = (bf16[64,1024]{1,0:T(8,128)(2,1)S(1)}, bf16[64,1024]{1,0:T(8,128)(2,1)S(1)}, u32[]{:S(2)}, u32[]{:S(2)}) collective-permute-start(bf16[64,1024]{1,0:T(8,128)(2,1)S(1)} %add_convert_fusion.3), channel_id=1, source_target_pairs={{0,0},{4,1},{8,2},{12,3},{16,4},{20,5},{24,6},{28,7},{1,8},{5,9},{... | collective-permute-start | bytes 393224 | tf_op jit(solution)/shard_map/ppermute | solution.py:522
  134.6 8.3 %collective-permute-done.39.refs_1_ = bf16[64,1024]{1,0:T(8,128)(2,1)S(1)} collective-permute-done((bf16[64,1024]{1,0:T(8,128)(2,1)S(1)}, bf16[64,1024]{1,0:T(8,128)(2,1)S(1)}, u32[]{:S(2)}, u32[]{:S(2)}) %collective-permute-start.39) | collective-permute-done | bytes 131104 | tf_op jit(solution)/shard_map/ppermute | solution.py:522
  142.9 0.7 masked_sum.1
  (70 shorter events, 1.2 us)
Async XLA Ops:
  0.6 12.4 %collective-permute-start = (bf16[128,1024]{1,0:T(8,128)(2,1)}, bf16[128,1024]{1,0:T(8,128)(2,1)S(1)}, u32[]{:S(2)}, u32[]{:S(2)}) collective-permute-start(bf16[128,1024]{1,0:T(8,128)(2,1)} %bitcast.12), channel_id=1, source_target_pairs={{0,1},{1,0},{2,3},{3,2},{4,5},{5,4},{6,7},{7,6},{8,9},{9,8},{10,11... | collective-permute-start | bytes 786440 | tf_op jit(solution)/shard_map/ppermute | solution.py:264
  0.7 16.0 %collective-permute-start.3 = (bf16[128,1024]{1,0:T(8,128)(2,1)}, bf16[128,1024]{1,0:T(8,128)(2,1)S(1)}, u32[]{:S(2)}, u32[]{:S(2)}) collective-permute-start(bf16[128,1024]{1,0:T(8,128)(2,1)} %bitcast.13), channel_id=1, source_target_pairs={{0,4},{1,5},{2,6},{3,7},{4,0},{5,1},{6,2},{7,3},{8,12},{9,13},{10,... | collective-permute-start | bytes 786440 | tf_op jit(solution)/shard_map/ppermute | solution.py:264
  3.4 17.0 %collective-permute-start.2 = (bf16[128,1024]{1,0:T(8,128)(2,1)}, bf16[128,1024]{1,0:T(8,128)(2,1)S(1)}, u32[]{:S(2)}, u32[]{:S(2)}) collective-permute-start(bf16[128,1024]{1,0:T(8,128)(2,1)} %bitcast.14), channel_id=1, source_target_pairs={{0,2},{1,3},{2,0},{3,1},{4,6},{5,7},{6,4},{7,5},{8,10},{9,11},{10,... | collective-permute-start | bytes 786440 | tf_op jit(solution)/shard_map/ppermute | solution.py:264
  4.9 0.7 copy-start.6
  7.1 5.9 %copy-start = (bf16[1,128,1024]{2,1,0:T(8,128)(2,1)S(1)}, bf16[1,128,1024]{2,1,0:T(8,128)(2,1)}, u32[]{:S(2)}) copy-start(bf16[1,128,1024]{2,1,0:T(8,128)(2,1)} %param.21) | copy-start | bytes 786436
  7.1 5.9 %copy-start.1 = (f32[1024]{0:T(1024)S(1)}, f32[1024]{0:T(1024)}, u32[]{:S(2)}) copy-start(f32[1024]{0:T(1024)} %param.23) | copy-start | bytes 12292
  7.1 5.9 %copy-start.2 = (s32[32]{0:T(128)S(1)}, s32[32]{0:T(128)}, u32[]{:S(2)}) copy-start(s32[32]{0:T(128)} %lengths.7) | copy-start | bytes 388
  10.7 10.4 %collective-permute-start.4 = (bf16[80,1024]{1,0:T(8,128)(2,1)S(1)}, bf16[80,1024]{1,0:T(8,128)(2,1)S(1)}, u32[]{:S(2)}, u32[]{:S(2)}) collective-permute-start(bf16[80,1024]{1,0:T(8,128)(2,1)S(1)} %decoder_rows.1), channel_id=1, source_target_pairs={{0,0},{1,4},{2,8},{3,12},{4,16},{5,20},{6,24},{7,28},{8,1},{9,5},{... | collective-permute-start | bytes 491528 | tf_op jit(solution)/shard_map/ppermute | solution.py:470
  16.8 4.3 %copy-start.3 = (f32[1024]{0:T(1024)S(1)}, f32[1024]{0:T(1024)}, u32[]{:S(2)}) copy-start(f32[1024]{0:T(1024)} %param.34) | copy-start | bytes 12292
  16.8 6.6 %collective-permute-start.5 = (bf16[128,1024]{1,0:T(8,128)(2,1)S(1)}, bf16[128,1024]{1,0:T(8,128)(2,1)S(1)}, u32[]{:S(2)}, u32[]{:S(2)}) collective-permute-start(bf16[128,1024]{1,0:T(8,128)(2,1)S(1)} %collective-permute-done.3.refs_1_), channel_id=1, source_target_pairs={{0,1},{1,0},{2,3},{3,2},{4,5},{5,4},{6,7},{7,6},{8,9},{9,8},{10,11... | collective-permute-start | bytes 786440 | tf_op jit(solution)/shard_map/ppermute | solution.py:264
  20.4 9.7 %collective-permute-start.7 = (bf16[128,1024]{1,0:T(8,128)(2,1)S(1)}, bf16[128,1024]{1,0:T(8,128)(2,1)S(1)}, u32[]{:S(2)}, u32[]{:S(2)}) collective-permute-start(bf16[128,1024]{1,0:T(8,128)(2,1)S(1)} %collective-permute-done.2.refs_1_), channel_id=1, source_target_pairs={{0,1},{1,0},{2,3},{3,2},{4,5},{5,4},{6,7},{7,6},{8,9},{9,8},{10,11... | collective-permute-start | bytes 786440 | tf_op jit(solution)/shard_map/ppermute | solution.py:264
  21.2 8.9 %collective-permute-start.6 = (bf16[64,1024]{1,0:T(8,128)(2,1)S(1)}, bf16[64,1024]{1,0:T(8,128)(2,1)S(1)}, u32[]{:S(2)}, u32[]{:S(2)}) collective-permute-start(bf16[64,1024]{1,0:T(8,128)(2,1)S(1)} %get-tuple-element.52.queries_in), channel_id=1, source_target_pairs={{0,2},{1,3},{2,0},{3,1},{4,6},{5,7},{6,4},{7,5},{8,10},{9,11},{10,... | collective-permute-start | bytes 393224 | tf_op jit(solution)/shard_map/ppermute | solution.py:264
  22.7 13.1 %collective-permute-start.10 = (bf16[128,1024]{1,0:T(8,128)(2,1)S(1)}, bf16[128,1024]{1,0:T(8,128)(2,1)S(1)}, u32[]{:S(2)}, u32[]{:S(2)}) collective-permute-start(bf16[128,1024]{1,0:T(8,128)(2,1)S(1)} %collective-permute-done.3.refs_1_), channel_id=1, source_target_pairs={{0,2},{1,3},{2,0},{3,1},{4,6},{5,7},{6,4},{7,5},{8,10},{9,11},{10,... | collective-permute-start | bytes 786440 | tf_op jit(solution)/shard_map/ppermute | solution.py:264
  27.1 9.3 %collective-permute-start.14 = (bf16[128,1024]{1,0:T(8,128)(2,1)S(1)}, bf16[128,1024]{1,0:T(8,128)(2,1)S(1)}, u32[]{:S(2)}, u32[]{:S(2)}) collective-permute-start(bf16[128,1024]{1,0:T(8,128)(2,1)S(1)} %get-tuple-element.61), channel_id=1, source_target_pairs={{0,1},{1,0},{2,3},{3,2},{4,5},{5,4},{6,7},{7,6},{8,9},{9,8},{10,11... | collective-permute-start | bytes 786440 | tf_op jit(solution)/shard_map/ppermute | solution.py:264
  27.3 6.8 %collective-permute-start.11 = (bf16[64,1024]{1,0:T(8,128)(2,1)S(1)}, bf16[64,1024]{1,0:T(8,128)(2,1)S(1)}, u32[]{:S(2)}, u32[]{:S(2)}) collective-permute-start(bf16[64,1024]{1,0:T(8,128)(2,1)S(1)} %get-tuple-element.52.queries_in), channel_id=1, source_target_pairs={{0,4},{1,5},{2,6},{3,7},{4,0},{5,1},{6,2},{7,3},{8,12},{9,13},{10,... | collective-permute-start | bytes 393224 | tf_op jit(solution)/shard_map/ppermute | solution.py:264
  35.9 3.3 %collective-permute-start.12 = (bf16[128,1024]{1,0:T(8,128)(2,1)S(1)}, bf16[128,1024]{1,0:T(8,128)(2,1)S(1)}, u32[]{:S(2)}, u32[]{:S(2)}) collective-permute-start(bf16[128,1024]{1,0:T(8,128)(2,1)S(1)} %collective-permute-done.10.refs_1_), channel_id=1, source_target_pairs={{0,1},{1,0},{2,3},{3,2},{4,5},{5,4},{6,7},{7,6},{8,9},{9,8},{10,11... | collective-permute-start | bytes 786440 | tf_op jit(solution)/shard_map/ppermute | solution.py:264
  35.9 7.6 %collective-permute-start.8 = (bf16[128,1024]{1,0:T(8,128)(2,1)S(1)}, bf16[128,1024]{1,0:T(8,128)(2,1)S(1)}, u32[]{:S(2)}, u32[]{:S(2)}) collective-permute-start(bf16[128,1024]{1,0:T(8,128)(2,1)S(1)} %get-tuple-element.57), channel_id=1, source_target_pairs={{0,1},{1,0},{2,3},{3,2},{4,5},{5,4},{6,7},{7,6},{8,9},{9,8},{10,11... | collective-permute-start | bytes 786440 | tf_op jit(solution)/shard_map/ppermute | solution.py:264
  36.4 25.8 %copy-start.4 = (f32[1024]{0:T(1024)S(1)}, f32[1024]{0:T(1024)}, u32[]{:S(2)}) copy-start(f32[1024]{0:T(1024)} %param.29) | copy-start | bytes 12292
  36.5 9.3 %collective-permute-start.15 = (bf16[128,1024]{1,0:T(8,128)(2,1)S(1)}, bf16[128,1024]{1,0:T(8,128)(2,1)S(1)}, u32[]{:S(2)}, u32[]{:S(2)}) collective-permute-start(bf16[128,1024]{1,0:T(8,128)(2,1)S(1)} %add_convert_fusion.1), channel_id=1, source_target_pairs={{0,2},{1,3},{2,0},{3,1},{4,6},{5,7},{6,4},{7,5},{8,10},{9,11},{10,... | collective-permute-start | bytes 786440 | tf_op jit(solution)/shard_map/ppermute | solution.py:264
  42.9 2.9 %collective-permute-start.13 = (bf16[128,1024]{1,0:T(8,128)(2,1)S(1)}, bf16[128,1024]{1,0:T(8,128)(2,1)S(1)}, u32[]{:S(2)}, u32[]{:S(2)}) collective-permute-start(bf16[128,1024]{1,0:T(8,128)(2,1)S(1)} %get-tuple-element.60), channel_id=1, source_target_pairs={{0,1},{1,0},{2,3},{3,2},{4,5},{5,4},{6,7},{7,6},{8,9},{9,8},{10,11... | collective-permute-start | bytes 786440 | tf_op jit(solution)/shard_map/ppermute | solution.py:264
  42.9 2.9 %collective-permute-start.1 = (bf16[128,1024]{1,0:T(8,128)(2,1)S(1)}, bf16[128,1024]{1,0:T(8,128)(2,1)S(1)}, u32[]{:S(2)}, u32[]{:S(2)}) collective-permute-start(bf16[128,1024]{1,0:T(8,128)(2,1)S(1)} %get-tuple-element.49), channel_id=1, source_target_pairs={{0,1},{1,0},{2,3},{3,2},{4,5},{5,4},{6,7},{7,6},{8,9},{9,8},{10,11... | collective-permute-start | bytes 786440 | tf_op jit(solution)/shard_map/ppermute | solution.py:264
  45.9 21.3 %collective-permute-start.17 = (bf16[4,1024,1024]{2,1,0:T(8,128)(2,1)S(1)}, bf16[4,1024,1024]{2,1,0:T(8,128)(2,1)S(1)}, u32[]{:S(2)}, u32[]{:S(2)}) collective-permute-start(bf16[4,1024,1024]{2,1,0:T(8,128)(2,1)S(1)} %load_stack.1.refs_0_), channel_id=1, source_target_pairs={{0,1},{1,0},{2,3},{3,2},{4,5},{5,4},{6,7},{7,6},{8,9},{9,8},{10,11... | collective-permute-start | bytes 25165832 | tf_op jit(solution)/shard_map/ppermute | solution.py:264
  45.9 8.7 %collective-permute-start.9 = (bf16[128,1024]{1,0:T(8,128)(2,1)S(1)}, bf16[128,1024]{1,0:T(8,128)(2,1)S(1)}, u32[]{:S(2)}, u32[]{:S(2)}) collective-permute-start(bf16[128,1024]{1,0:T(8,128)(2,1)S(1)} %add_convert_fusion.2), channel_id=1, source_target_pairs={{0,2},{1,3},{2,0},{3,1},{4,6},{5,7},{6,4},{7,5},{8,10},{9,11},{10,... | collective-permute-start | bytes 786440 | tf_op jit(solution)/shard_map/ppermute | solution.py:264
  47.8 14.5 %collective-permute-start.16 = (bf16[128,1024]{1,0:T(8,128)(2,1)S(1)}, bf16[128,1024]{1,0:T(8,128)(2,1)S(1)}, u32[]{:S(2)}, u32[]{:S(2)}) collective-permute-start(bf16[128,1024]{1,0:T(8,128)(2,1)S(1)} %add_convert_fusion), channel_id=1, source_target_pairs={{0,6},{1,7},{2,4},{3,5},{4,2},{5,3},{6,0},{7,1},{8,14},{9,15},{10,... | collective-permute-start | bytes 786440 | tf_op jit(solution)/shard_map/ppermute | solution.py:264
  63.2 13.5 %collective-permute-start.19 = (bf16[128,1024]{1,0:T(8,128)(2,1)S(1)}, bf16[128,1024]{1,0:T(8,128)(2,1)S(1)}, u32[]{:S(2)}, u32[]{:S(2)}) collective-permute-start(bf16[128,1024]{1,0:T(8,128)(2,1)S(1)} %get-tuple-element.64.keys_in), channel_id=1, source_target_pairs={{0,4},{1,5},{2,6},{3,7},{4,0},{5,1},{6,2},{7,3},{8,12},{9,13},{10,... | collective-permute-start | bytes 786440 | tf_op jit(solution)/shard_map/ppermute | solution.py:264
  65.2 22.7 %collective-permute-start.22 = (bf16[64,1024]{1,0:T(8,128)(2,1)S(1)}, bf16[64,1024]{1,0:T(8,128)(2,1)S(1)}, u32[]{:S(2)}, u32[]{:S(2)}) collective-permute-start(bf16[64,1024]{1,0:T(8,128)(2,1)S(1)} %collective-permute-done.11.queries_in), channel_id=1, source_target_pairs={{0,2},{1,3},{2,0},{3,1},{4,6},{5,7},{6,4},{7,5},{8,10},{9,11},{10,... | collective-permute-start | bytes 393224 | tf_op jit(solution)/shard_map/ppermute | solution.py:264
  65.5 17.2 %collective-permute-start.18 = (bf16[128,1024]{1,0:T(8,128)(2,1)S(1)}, bf16[128,1024]{1,0:T(8,128)(2,1)S(1)}, u32[]{:S(2)}, u32[]{:S(2)}) collective-permute-start(bf16[128,1024]{1,0:T(8,128)(2,1)S(1)} %get-tuple-element.64.keys_in), channel_id=1, source_target_pairs={{0,2},{1,3},{2,0},{3,1},{4,6},{5,7},{6,4},{7,5},{8,10},{9,11},{10,... | collective-permute-start | bytes 786440 | tf_op jit(solution)/shard_map/ppermute | solution.py:264
  76.7 11.1 %collective-permute-start.21 = (bf16[128,1024]{1,0:T(8,128)(2,1)S(1)}, bf16[128,1024]{1,0:T(8,128)(2,1)S(1)}, u32[]{:S(2)}, u32[]{:S(2)}) collective-permute-start(bf16[128,1024]{1,0:T(8,128)(2,1)S(1)} %collective-permute-done.19.keys_in), channel_id=1, source_target_pairs={{0,2},{1,3},{2,0},{3,1},{4,6},{5,7},{6,4},{7,5},{8,10},{9,11},{10,... | collective-permute-start | bytes 786440 | tf_op jit(solution)/shard_map/ppermute | solution.py:264
  80.6 11.1 %collective-permute-start.23 = (bf16[64,1024]{1,0:T(8,128)(2,1)S(1)}, bf16[64,1024]{1,0:T(8,128)(2,1)S(1)}, u32[]{:S(2)}, u32[]{:S(2)}) collective-permute-start(bf16[64,1024]{1,0:T(8,128)(2,1)S(1)} %cross_attention.5), channel_id=1, source_target_pairs={{0,2},{1,3},{2,0},{3,1},{4,6},{5,7},{6,4},{7,5},{8,10},{9,11},{10,... | collective-permute-start | bytes 393224 | tf_op jit(solution)/shard_map/ppermute | solution.py:264
  82.7 18.4 %slice-start = ((s8[8388608]{0:T(1024)(128)(4,1)}), s8[4194304]{0:T(1024)(128)(4,1)S(1)}, s32[]{:S(2)}) async-start(s8[8388608]{0:T(1024)(128)(4,1)} %bitcast.8), calls=%async_computation | async-start | bytes 8388608
  82.7 18.4 %slice-start.2 = ((s8[8388608]{0:T(1024)(128)(4,1)}), s8[4194304]{0:T(1024)(128)(4,1)S(1)}, s32[]{:S(2)}) async-start(s8[8388608]{0:T(1024)(128)(4,1)} %bitcast.10), calls=%async_computation.2 | async-start | bytes 8388608
  86.5 12.1 %copy-start.5 = (f32[1024]{0:T(1024)S(1)}, f32[1024]{0:T(1024)}, u32[]{:S(2)}) copy-start(f32[1024]{0:T(1024)} %param.39) | copy-start | bytes 12292
  86.6 14.5 %slice-start.1 = ((s8[8388608]{0:T(1024)(128)(4,1)}), s8[4194304]{0:T(1024)(128)(4,1)S(1)}, s32[]{:S(2)}) async-start(s8[8388608]{0:T(1024)(128)(4,1)} %bitcast.8), calls=%async_computation.1 | async-start | bytes 8388608
  86.6 14.5 %slice-start.3 = ((s8[8388608]{0:T(1024)(128)(4,1)}), s8[4194304]{0:T(1024)(128)(4,1)S(1)}, s32[]{:S(2)}) async-start(s8[8388608]{0:T(1024)(128)(4,1)} %bitcast.10), calls=%async_computation.3 | async-start | bytes 8388608
  86.6 6.8 %collective-permute-start.20 = (bf16[64,1024]{1,0:T(8,128)(2,1)S(1)}, bf16[64,1024]{1,0:T(8,128)(2,1)S(1)}, u32[]{:S(2)}, u32[]{:S(2)}) collective-permute-start(bf16[64,1024]{1,0:T(8,128)(2,1)S(1)} %cross_attention.6), channel_id=1, source_target_pairs={{0,2},{1,3},{2,0},{3,1},{4,6},{5,7},{6,4},{7,5},{8,10},{9,11},{10,... | collective-permute-start | bytes 393224 | tf_op jit(solution)/shard_map/ppermute | solution.py:264
  91.8 6.9 %collective-permute-start.24 = (bf16[64,1024]{1,0:T(8,128)(2,1)S(1)}, bf16[64,1024]{1,0:T(8,128)(2,1)S(1)}, u32[]{:S(2)}, u32[]{:S(2)}) collective-permute-start(bf16[64,1024]{1,0:T(8,128)(2,1)S(1)} %add_convert_fusion.7), channel_id=1, source_target_pairs={{0,6},{1,7},{2,4},{3,5},{4,2},{5,3},{6,0},{7,1},{8,14},{9,15},{10,... | collective-permute-start | bytes 393224 | tf_op jit(solution)/shard_map/ppermute | solution.py:264
  98.9 2.2 %collective-permute-start.25 = (bf16[64,1024]{1,0:T(8,128)(2,1)S(1)}, bf16[64,1024]{1,0:T(8,128)(2,1)S(1)}, u32[]{:S(2)}, u32[]{:S(2)}) collective-permute-start(bf16[64,1024]{1,0:T(8,128)(2,1)S(1)} %get-tuple-element.71.refs_0_), channel_id=1, source_target_pairs={{0,1},{1,0},{2,3},{3,2},{4,5},{5,4},{6,7},{7,6},{8,9},{9,8},{10,11... | collective-permute-start | bytes 393224 | tf_op jit(solution)/shard_map/ppermute | solution.py:264
  98.9 9.6 %collective-permute-start.28 = (bf16[64,1024]{1,0:T(8,128)(2,1)S(1)}, bf16[64,1024]{1,0:T(8,128)(2,1)S(1)}, u32[]{:S(2)}, u32[]{:S(2)}) collective-permute-start(bf16[64,1024]{1,0:T(8,128)(2,1)S(1)} %get-tuple-element.71.refs_0_), channel_id=1, source_target_pairs={{0,4},{1,5},{2,6},{3,7},{4,0},{5,1},{6,2},{7,3},{8,12},{9,13},{10,... | collective-permute-start | bytes 393224 | tf_op jit(solution)/shard_map/ppermute | solution.py:264
  100.6 8.5 %collective-permute-start.27 = (bf16[64,1024]{1,0:T(8,128)(2,1)S(1)}, bf16[64,1024]{1,0:T(8,128)(2,1)S(1)}, u32[]{:S(2)}, u32[]{:S(2)}) collective-permute-start(bf16[64,1024]{1,0:T(8,128)(2,1)S(1)} %get-tuple-element.71.refs_0_), channel_id=1, source_target_pairs={{0,2},{1,3},{2,0},{3,1},{4,6},{5,7},{6,4},{7,5},{8,10},{9,11},{10,... | collective-permute-start | bytes 393224 | tf_op jit(solution)/shard_map/ppermute | solution.py:264
  108.6 1.3 collective-permute-start.29
  108.6 6.5 %collective-permute-start.33 = (bf16[64,1024]{1,0:T(8,128)(2,1)S(1)}, bf16[64,1024]{1,0:T(8,128)(2,1)S(1)}, u32[]{:S(2)}, u32[]{:S(2)}) collective-permute-start(bf16[64,1024]{1,0:T(8,128)(2,1)S(1)} %collective-permute-done.28.refs_0_), channel_id=1, source_target_pairs={{0,2},{1,3},{2,0},{3,1},{4,6},{5,7},{6,4},{7,5},{8,10},{9,11},{10,... | collective-permute-start | bytes 393224 | tf_op jit(solution)/shard_map/ppermute | solution.py:264
  108.6 14.6 %collective-permute-start.26 = (bf16[64,1024]{1,0:T(8,128)(2,1)S(1)}, bf16[64,1024]{1,0:T(8,128)(2,1)S(1)}, u32[]{:S(2)}, u32[]{:S(2)}) collective-permute-start(bf16[64,1024]{1,0:T(8,128)(2,1)S(1)} %get-tuple-element.73), channel_id=1, source_target_pairs={{0,1},{1,0},{2,3},{3,2},{4,5},{5,4},{6,7},{7,6},{8,9},{9,8},{10,11... | collective-permute-start | bytes 393224 | tf_op jit(solution)/shard_map/ppermute | solution.py:264
  109.1 3.5 %collective-permute-start.30 = (bf16[64,1024]{1,0:T(8,128)(2,1)S(1)}, bf16[64,1024]{1,0:T(8,128)(2,1)S(1)}, u32[]{:S(2)}, u32[]{:S(2)}) collective-permute-start(bf16[64,1024]{1,0:T(8,128)(2,1)S(1)} %collective-permute-done.27.refs_0_), channel_id=1, source_target_pairs={{0,1},{1,0},{2,3},{3,2},{4,5},{5,4},{6,7},{7,6},{8,9},{9,8},{10,11... | collective-permute-start | bytes 393224 | tf_op jit(solution)/shard_map/ppermute | solution.py:264
  112.4 3.3 %collective-permute-start.36 = (bf16[64,1024]{1,0:T(8,128)(2,1)S(1)}, bf16[64,1024]{1,0:T(8,128)(2,1)S(1)}, u32[]{:S(2)}, u32[]{:S(2)}) collective-permute-start(bf16[64,1024]{1,0:T(8,128)(2,1)S(1)} %get-tuple-element.83), channel_id=1, source_target_pairs={{0,1},{1,0},{2,3},{3,2},{4,5},{5,4},{6,7},{7,6},{8,9},{9,8},{10,11... | collective-permute-start | bytes 393224 | tf_op jit(solution)/shard_map/ppermute | solution.py:264
  115.0 2.0 %collective-permute-start.34 = (bf16[64,1024]{1,0:T(8,128)(2,1)S(1)}, bf16[64,1024]{1,0:T(8,128)(2,1)S(1)}, u32[]{:S(2)}, u32[]{:S(2)}) collective-permute-start(bf16[64,1024]{1,0:T(8,128)(2,1)S(1)} %collective-permute-done.33.refs_0_), channel_id=1, source_target_pairs={{0,1},{1,0},{2,3},{3,2},{4,5},{5,4},{6,7},{7,6},{8,9},{9,8},{10,11... | collective-permute-start | bytes 393224 | tf_op jit(solution)/shard_map/ppermute | solution.py:264
  115.5 4.1 %collective-permute-start.31 = (bf16[64,1024]{1,0:T(8,128)(2,1)S(1)}, bf16[64,1024]{1,0:T(8,128)(2,1)S(1)}, u32[]{:S(2)}, u32[]{:S(2)}) collective-permute-start(bf16[64,1024]{1,0:T(8,128)(2,1)S(1)} %get-tuple-element.79), channel_id=1, source_target_pairs={{0,1},{1,0},{2,3},{3,2},{4,5},{5,4},{6,7},{7,6},{8,9},{9,8},{10,11... | collective-permute-start | bytes 393224 | tf_op jit(solution)/shard_map/ppermute | solution.py:264
  115.6 5.8 %collective-permute-start.37 = (bf16[64,1024]{1,0:T(8,128)(2,1)S(1)}, bf16[64,1024]{1,0:T(8,128)(2,1)S(1)}, u32[]{:S(2)}, u32[]{:S(2)}) collective-permute-start(bf16[64,1024]{1,0:T(8,128)(2,1)S(1)} %add_convert_fusion.5), channel_id=1, source_target_pairs={{0,2},{1,3},{2,0},{3,1},{4,6},{5,7},{6,4},{7,5},{8,10},{9,11},{10,... | collective-permute-start | bytes 393224 | tf_op jit(solution)/shard_map/ppermute | solution.py:264
  119.4 2.0 %collective-permute-start.35 = (bf16[64,1024]{1,0:T(8,128)(2,1)S(1)}, bf16[64,1024]{1,0:T(8,128)(2,1)S(1)}, u32[]{:S(2)}, u32[]{:S(2)}) collective-permute-start(bf16[64,1024]{1,0:T(8,128)(2,1)S(1)} %get-tuple-element.82), channel_id=1, source_target_pairs={{0,1},{1,0},{2,3},{3,2},{4,5},{5,4},{6,7},{7,6},{8,9},{9,8},{10,11... | collective-permute-start | bytes 393224 | tf_op jit(solution)/shard_map/ppermute | solution.py:264
  119.6 6.0 %collective-permute-start.32 = (bf16[64,1024]{1,0:T(8,128)(2,1)S(1)}, bf16[64,1024]{1,0:T(8,128)(2,1)S(1)}, u32[]{:S(2)}, u32[]{:S(2)}) collective-permute-start(bf16[64,1024]{1,0:T(8,128)(2,1)S(1)} %add_convert_fusion.6), channel_id=1, source_target_pairs={{0,2},{1,3},{2,0},{3,1},{4,6},{5,7},{6,4},{7,5},{8,10},{9,11},{10,... | collective-permute-start | bytes 393224 | tf_op jit(solution)/shard_map/ppermute | solution.py:264
  121.5 7.2 %collective-permute-start.38 = (bf16[64,1024]{1,0:T(8,128)(2,1)S(1)}, bf16[64,1024]{1,0:T(8,128)(2,1)S(1)}, u32[]{:S(2)}, u32[]{:S(2)}) collective-permute-start(bf16[64,1024]{1,0:T(8,128)(2,1)S(1)} %add_convert_fusion.4), channel_id=1, source_target_pairs={{0,6},{1,7},{2,4},{3,5},{4,2},{5,3},{6,0},{7,1},{8,14},{9,15},{10,... | collective-permute-start | bytes 393224 | tf_op jit(solution)/shard_map/ppermute | solution.py:264
  128.8 14.1 %collective-permute-start.39 = (bf16[64,1024]{1,0:T(8,128)(2,1)S(1)}, bf16[64,1024]{1,0:T(8,128)(2,1)S(1)}, u32[]{:S(2)}, u32[]{:S(2)}) collective-permute-start(bf16[64,1024]{1,0:T(8,128)(2,1)S(1)} %add_convert_fusion.3), channel_id=1, source_target_pairs={{0,0},{4,1},{8,2},{12,3},{16,4},{20,5},{24,6},{28,7},{1,8},{5,9},{... | collective-permute-start | bytes 393224 | tf_op jit(solution)/shard_map/ppermute | solution.py:522

commit v2 on v1

--- a/solution.py
+++ b/solution.py
@@ -11,7 +11,7 @@
 MAXREL = 16
 NB = 33
 LANG_ROWS = 16
-OPT = dict(enc="213", mem="213", ffn="213", p3=(), p1=(), dec="early", norm2=True, p3tie=("enc", "mem", "ffn"), straight=False, home="w", dtie=False, w="all", ls=2)
+OPT = dict(enc="213", mem="213", ffn="213", p3=("enc",), p1=(), dec="early", norm2=True, p3tie=("enc", "mem", "ffn"), straight=False, pieces=1, home="w", dtie=False, w="all", ls=2)
 EPSILON = 1e-06
 NEG_FILL = -1e30
 FFN_STEP = 512
@@ -405,25 +405,26 @@
     )(*addends, gain[None, :])
 
 
-def masked_body(count, *refs):
-    ends, addends, out = refs[0], refs[1:count + 1], refs[count + 1]
-    total = addends[0][...].astype(F32)
-    for ref in addends[1:]:
-        total = total + ref[...].astype(F32)
-    keep = lax.broadcasted_iota(jnp.int32, total.shape, 0) < ends[0]
-    out[...] = jnp.where(keep, total, 0.0).astype(BF16)
-
-
-def masked_sum(addends, ends):
-    rows, width = addends[0].shape
-    return pl.pallas_call(
-        functools.partial(masked_body, len(addends)),
-        in_specs=[IN_SMEM] + [IN_VMEM] * len(addends),
+def masked_body(ends, *refs):
+    pieces, out = refs[:-1], refs[-1]
+    count = pieces[0].shape[0]
+    for i, ref in enumerate(pieces):
+        index = lax.broadcasted_iota(jnp.int32, ref.shape, 0) + i * count
+        out[i * count:(i + 1) * count, :] = jnp.where(
+            index < ends[0], ref[...].astype(F32), 0.0
+        ).astype(BF16)
+
+
+def masked(pieces, ends):
+    rows, width = pieces[0].shape
+    return pl.pallas_call(
+        masked_body,
+        in_specs=[IN_SMEM] + [IN_VMEM] * len(pieces),
         out_specs=IN_VMEM,
-        out_shape=jax.ShapeDtypeStruct((rows, width), BF16),
-        compiler_params=pltpu.CompilerParams(vmem_limit_bytes=VMEM_LIMIT),
-        name="masked_sum",
-    )(ends, *addends)
+        out_shape=jax.ShapeDtypeStruct((rows * len(pieces), width), BF16),
+        compiler_params=pltpu.CompilerParams(vmem_limit_bytes=VMEM_LIMIT),
+        name="masked",
+    )(ends, *pieces)
 
 
 def on_device(
@@ -479,6 +480,8 @@
     if cross_query.shape != cross_output.shape:
         stacks = [stacks[0][:3], stacks[0][3:]]
     cross_own = [load_stack(weights) for weights in stacks]
+    if OPT["ls"] == 0:
+        enc_weights[0] = after(enc_weights[0], *cross_own)
 
     def hook(out):
         rows = after(dec_normed, out) if OPT["dtie"] else dec_normed
@@ -515,15 +518,18 @@
 
     ffn_terms = exchange("ffn", ffn_normed, ffn_pair, True, straight=OPT["straight"])
 
-    far_terms = {}
     if OPT["straight"]:
         ffn_terms, far_terms = ffn_terms
-    home = dict(to_home)
-    arrivals = [lax.ppermute(bf16_sum(hidden, *ffn_terms), ("dp", "tensor"), to_home)]
-    for k, term in far_terms.items():
-        way = [(d, home[d ^ (2 * k)]) for d in range(groups * size)]
-        arrivals.append(lax.ppermute(term, ("dp", "tensor"), way))
-    dec_out = masked_sum(arrivals, tgt_lengths)
+        pieces = []
+        step = target_len // OPT["pieces"]
+        for start in range(0, target_len, step):
+            rows = slice(start, start + step)
+            terms = [term[rows] for term in (hidden, *ffn_terms)]
+            terms += [swap(term[rows], 2 * k) for k, term in far_terms.items()]
+            pieces.append(lax.ppermute(bf16_sum(*terms), ("dp", "tensor"), to_home))
+    else:
+        pieces = [lax.ppermute(bf16_sum(hidden, *ffn_terms), ("dp", "tensor"), to_home)]
+    dec_out = masked(pieces, tgt_lengths)
     return (memory_out[None], dec_out[None])
 
 

time: 144 us -> 143 us (level)
  starting transfers between devices: 40.7 us -> 37.3 us
  waiting for transfers between devices: 48.9 us -> 51.8 us
    ppermute x38, waiting for transfers between devices: 40.5 us -> 43.7 us  [swap(): return lax.ppermute(value, 'tensor', [(i, i ^ bits) for i in range(size)])]
    ppermute x38, starting transfers between devices: 33.2 us -> 30.3 us  [swap(): return lax.ppermute(value, 'tensor', [(i, i ^ bits) for i in range(size)])]
  transfers between devices with their start and end apart: 40 -> 40, of which waited for: 15 -> 13; matrix products, arithmetic and copies ran while one was open for 0% -> 0% of each run, Pallas kernels for 35% -> 35%
where the time goes in v2:
time: 143 us
  waiting for transfers between devices  51.8 us (36%)
  Pallas kernels  51 us (36%)
  starting transfers between devices  37.3 us (26%)
  between operations  1.75 us (1%)
    ppermute x38, waiting for transfers between devices, swap(): return lax.ppermute(value, 'tensor', [(i, i ^ bits) for i in range(size)])  43.7 us
    ppermute x38, starting transfers between devices, swap(): return lax.ppermute(value, 'tensor', [(i, i ^ bits) for i in range(size)])  30.3 us
    pallas_call x4, Pallas kernels, cross_attention(): pl.pallas_call(functools.partial(cross_body, slot, lax.axis_size('tensor'...  15.6 us
    pallas_call x4, Pallas kernels, self_attention(): pl.pallas_call(functools.partial(self_body, parts, first_slot, lax.axis_s...  14.9 us
    pallas_call x4, Pallas kernels, ffn(): pl.pallas_call(functools.partial(ffn_body, parts), in_specs=[IN_VMEM] * (...  9.99 us
    ppermute x1, waiting for transfers between devices, on_device(): lax.ppermute(bf16_sum(hidden, *ffn_terms), ('dp', 'tensor'), to_home)  8.06 us
    ppermute x1, starting transfers between devices, on_device(): lax.ppermute(bf16_sum(hidden, *ffn_terms), ('dp', 'tensor'), to_home)  4.66 us
    pallas_call x1, Pallas kernels, load(): pl.pallas_call(functools.partial(load_body, count), in_specs=[IN_HBM] * (...  3.55 us
  transfers between devices with their start and end apart: 40, of which 13 were waited for; matrix products, arithmetic and copies ran while one was open for 0% of the time, Pallas kernels for 35%

profile of v2, /device:TPU:4, one launch (start us, length us, event | category | flops | bytes accessed | tf_op | source)
XLA Modules:
  0.0 143.1 jit_solution(14565947067783833585)
XLA Ops:
  0.7 2.7 %collective-permute-start.3 = (bf16[128,1024]{1,0:T(8,128)(2,1)}, bf16[128,1024]{1,0:T(8,128)(2,1)S(1)}, u32[]{:S(2)}, u32[]{:S(2)}) collective-permute-start(bf16[128,1024]{1,0:T(8,128)(2,1)} %bitcast.13), channel_id=1, source_target_pairs={{0,4},{1,5},{2,6},{3,7},{4,0},{5,1},{6,2},{7,3},{8,12},{9,13},{10,... | collective-permute-start | bytes 786440 | tf_op jit(solution)/shard_map/ppermute | solution.py:264
  3.4 1.6 %collective-permute-start.2 = (bf16[128,1024]{1,0:T(8,128)(2,1)}, bf16[128,1024]{1,0:T(8,128)(2,1)S(1)}, u32[]{:S(2)}, u32[]{:S(2)}) collective-permute-start(bf16[128,1024]{1,0:T(8,128)(2,1)} %bitcast.14), channel_id=1, source_target_pairs={{0,2},{1,3},{2,0},{3,1},{4,6},{5,7},{6,4},{7,5},{8,10},{9,11},{10,... | collective-permute-start | bytes 786440 | tf_op jit(solution)/shard_map/ppermute | solution.py:264
  4.9 0.7 copy-done.6
  5.6 1.5 %decoder_rows.1 = bf16[80,1024]{1,0:T(8,128)(2,1)S(1)} custom-call(s32[8]{0:T(128)S(1)} %copy-done.6, bf16[64,1024]{1,0:T(8,128)(2,1)} %bitcast.24, bf16[8,1024]{1,0:T(8,128)(2,1)} %table.1), custom_call_target="tpu_custom_call" | custom-call | tf_op jit(solution)/shard_map/decoder_rows/pallas_call | solution.py:362
  7.1 3.5 %load.1 = (bf16[1024,1024]{1,0:T(8,128)(2,1)S(1)}, bf16[1024,1024]{1,0:T(8,128)(2,1)S(1)}, bf16[1024,1024]{1,0:T(8,128)(2,1)S(1)}, bf16[1024,1024]{1,0:T(8,128)(2,1)S(1)}, f32[8,128,128]{2,1,0:T(8,128)S(1)}) custom-call(bf16[1024,1024]{1,0:T(8,128)(2,1)} %refs_0_.6, bf16[1024,1024]{1,0:T(8,128)(2,1)} %refs_1_.2, bf16[1024,1024]{1,0:T(8,128)(2,1)} %refs_2_.6, ...), custom_call_target="tpu_custom_call" | custom-call | bytes 16777216 | tf_op jit(solution)/shard_map/load/pallas_call | solution.py:69
  10.7 2.3 %collective-permute-start.4 = (bf16[80,1024]{1,0:T(8,128)(2,1)S(1)}, bf16[80,1024]{1,0:T(8,128)(2,1)S(1)}, u32[]{:S(2)}, u32[]{:S(2)}) collective-permute-start(bf16[80,1024]{1,0:T(8,128)(2,1)S(1)} %decoder_rows.1), channel_id=1, source_target_pairs={{0,0},{1,4},{2,8},{3,12},{4,16},{5,20},{6,24},{7,28},{8,1},{9,5},{... | collective-permute-start | bytes 491528 | tf_op jit(solution)/shard_map/ppermute | solution.py:471
  13.0 3.7 %self_attention.4 = (bf16[128,1024]{1,0:T(8,128)(2,1)S(1)}, bf16[128,1024]{1,0:T(8,128)(2,1)S(1)}) custom-call(s32[32]{0:T(128)S(1)} %copy-done.2, bf16[128,1024]{1,0:T(8,128)(2,1)S(1)} %bitcast.15, bf16[128,1024]{1,0:T(8,128)(2,1)S(1)} %collective-permute-done.refs_2_, bf16[1024,1024]{1,0:T(8,128)(2,1)S(1)} %get-tuple-element.43.refs_3_, ...), custom_call_target="tpu_custom_call" | custom-call | flops 2281701376 | bytes 1048576 | tf_op jit(solution)/shard_map/self_attention/pallas_call | solution.py:169
  16.9 3.5 %load_stack.1.refs_0_ = bf16[4,1024,1024]{2,1,0:T(8,128)(2,1)S(1)} custom-call(bf16[1024,1024]{1,0:T(8,128)(2,1)} %refs_0_.8, bf16[1024,1024]{1,0:T(8,128)(2,1)} %refs_1_.3, bf16[1024,1024]{1,0:T(8,128)(2,1)} %refs_2_.7, bf16[1024,1024]{1,0:T(8,128)(2,1)} %refs_3_.7), custom_call_target="tpu_custom_call" | custom-call | tf_op jit(solution)/shard_map/load_stack/pallas_call | solution.py:98
  20.4 1.6 %collective-permute-start.7 = (bf16[128,1024]{1,0:T(8,128)(2,1)S(1)}, bf16[128,1024]{1,0:T(8,128)(2,1)S(1)}, u32[]{:S(2)}, u32[]{:S(2)}) collective-permute-start(bf16[128,1024]{1,0:T(8,128)(2,1)S(1)} %collective-permute-done.3.refs_1_), channel_id=1, source_target_pairs={{0,2},{1,3},{2,0},{3,1},{4,6},{5,7},{6,4},{7,5},{8,10},{9,11},{10,... | collective-permute-start | bytes 786440 | tf_op jit(solution)/shard_map/ppermute | solution.py:264
  21.9 0.2 collective-permute-start.8
  22.2 0.1 sum_norm.3
  22.4 0.6 collective-permute-start.6
  23.0 3.7 %self_attention.5 = (bf16[128,1024]{1,0:T(8,128)(2,1)S(1)}, bf16[128,1024]{1,0:T(8,128)(2,1)S(1)}) custom-call(s32[32]{0:T(128)S(1)} %copy-done.2, bf16[128,1024]{1,0:T(8,128)(2,1)S(1)} %collective-permute-done.3.refs_1_, bf16[128,1024]{1,0:T(8,128)(2,1)S(1)} %collective-permute-done.5.refs_2_, bf16[1024,1024]{1,0:T(8,128)(2,1)S(1)} %get-tuple-element.43.refs_3_, ...), custom_call_target="tpu_custom_call" | custom-call | flops 2281701376 | bytes 1048576 | tf_op jit(solution)/shard_map/self_attention/pallas_call | solution.py:169
  26.7 0.1 collective-permute-start.14
  26.8 3.2 %collective-permute-start.11 = (bf16[64,1024]{1,0:T(8,128)(2,1)S(1)}, bf16[64,1024]{1,0:T(8,128)(2,1)S(1)}, u32[]{:S(2)}, u32[]{:S(2)}) collective-permute-start(bf16[64,1024]{1,0:T(8,128)(2,1)S(1)} %get-tuple-element.52.queries_in), channel_id=1, source_target_pairs={{0,4},{1,5},{2,6},{3,7},{4,0},{5,1},{6,2},{7,3},{8,12},{9,13},{10,... | collective-permute-start | bytes 393224 | tf_op jit(solution)/shard_map/ppermute | solution.py:264
  30.0 4.7 %collective-permute-done.6.queries_in = bf16[64,1024]{1,0:T(8,128)(2,1)S(1)} collective-permute-done((bf16[64,1024]{1,0:T(8,128)(2,1)S(1)}, bf16[64,1024]{1,0:T(8,128)(2,1)S(1)}, u32[]{:S(2)}, u32[]{:S(2)}) %collective-permute-start.6) | collective-permute-done | bytes 131104 | tf_op jit(solution)/shard_map/ppermute | solution.py:264
  34.7 3.7 %self_attention.6 = (bf16[128,1024]{1,0:T(8,128)(2,1)S(1)}, bf16[128,1024]{1,0:T(8,128)(2,1)S(1)}) custom-call(s32[32]{0:T(128)S(1)} %copy-done.2, bf16[128,1024]{1,0:T(8,128)(2,1)S(1)} %collective-permute-done.2.refs_1_, bf16[128,1024]{1,0:T(8,128)(2,1)S(1)} %collective-permute-done.8.refs_2_, bf16[1024,1024]{1,0:T(8,128)(2,1)S(1)} %get-tuple-element.43.refs_3_, ...), custom_call_target="tpu_custom_call" | custom-call | flops 2281701376 | bytes 1048576 | tf_op jit(solution)/shard_map/self_attention/pallas_call | solution.py:169
  38.5 0.5 collective-permute-start.9
  39.2 0.9 collective-permute-done.12.refs_2_
  40.0 3.7 %self_attention.7 = (bf16[128,1024]{1,0:T(8,128)(2,1)S(1)}, bf16[128,1024]{1,0:T(8,128)(2,1)S(1)}) custom-call(s32[32]{0:T(128)S(1)} %copy-done.2, bf16[128,1024]{1,0:T(8,128)(2,1)S(1)} %collective-permute-done.7.refs_1_, bf16[128,1024]{1,0:T(8,128)(2,1)S(1)} %collective-permute-done.12.refs_2_, bf16[1024,1024]{1,0:T(8,128)(2,1)S(1)} %get-tuple-element.43.refs_3_, ...), custom_call_target="tpu_custom_call" | custom-call | flops 2281701376 | bytes 1048576 | tf_op jit(solution)/shard_map/self_attention/pallas_call | solution.py:169
  43.8 0.2 collective-permute-start.13
  44.0 0.4 collective-permute-start.1
  44.4 3.0 %collective-permute-done.15 = bf16[128,1024]{1,0:T(8,128)(2,1)S(1)} collective-permute-done((bf16[128,1024]{1,0:T(8,128)(2,1)S(1)}, bf16[128,1024]{1,0:T(8,128)(2,1)S(1)}, u32[]{:S(2)}, u32[]{:S(2)}) %collective-permute-start.15) | collective-permute-done | bytes 262176 | tf_op jit(solution)/shard_map/ppermute | solution.py:264
  47.5 0.1 add_convert_fusion
  47.7 0.4 collective-permute-start.10
  48.0 1.8 %collective-permute-start.16 = (bf16[128,1024]{1,0:T(8,128)(2,1)S(1)}, bf16[128,1024]{1,0:T(8,128)(2,1)S(1)}, u32[]{:S(2)}, u32[]{:S(2)}) collective-permute-start(bf16[128,1024]{1,0:T(8,128)(2,1)S(1)} %add_convert_fusion), channel_id=1, source_target_pairs={{0,6},{1,7},{2,4},{3,5},{4,2},{5,3},{6,0},{7,1},{8,14},{9,15},{10,... | collective-permute-start | bytes 786440 | tf_op jit(solution)/shard_map/ppermute | solution.py:264
  49.9 6.9 %collective-permute-done.10.refs_3_ = bf16[128,1024]{1,0:T(8,128)(2,1)S(1)} collective-permute-done((bf16[128,1024]{1,0:T(8,128)(2,1)S(1)}, bf16[128,1024]{1,0:T(8,128)(2,1)S(1)}, u32[]{:S(2)}, u32[]{:S(2)}) %collective-permute-start.10) | collective-permute-done | bytes 262176 | tf_op jit(solution)/shard_map/ppermute | solution.py:264
  56.8 5.4 %collective-permute-done.16.refs_4_ = bf16[128,1024]{1,0:T(8,128)(2,1)S(1)} collective-permute-done((bf16[128,1024]{1,0:T(8,128)(2,1)S(1)}, bf16[128,1024]{1,0:T(8,128)(2,1)S(1)}, u32[]{:S(2)}, u32[]{:S(2)}) %collective-permute-start.16) | collective-permute-done | bytes 262176 | tf_op jit(solution)/shard_map/ppermute | solution.py:264
  62.2 1.0 sum_norm.4
  63.2 1.9 %collective-permute-start.19 = (bf16[128,1024]{1,0:T(8,128)(2,1)S(1)}, bf16[128,1024]{1,0:T(8,128)(2,1)S(1)}, u32[]{:S(2)}, u32[]{:S(2)}) collective-permute-start(bf16[128,1024]{1,0:T(8,128)(2,1)S(1)} %get-tuple-element.64.keys_in), channel_id=1, source_target_pairs={{0,4},{1,5},{2,6},{3,7},{4,0},{5,1},{6,2},{7,3},{8,12},{9,13},{10,... | collective-permute-start | bytes 786440 | tf_op jit(solution)/shard_map/ppermute | solution.py:264
  65.1 0.7 collective-permute-start.22
  65.8 1.4 collective-permute-start.18
  67.1 4.0 %cross_attention.4.refs_1_ = bf16[64,1024]{1,0:T(8,128)(2,1)S(1)} custom-call(s32[32]{0:T(128)S(1)} %copy-done.2, bf16[128,1024]{1,0:T(8,128)(2,1)S(1)} %get-tuple-element.64.keys_in, bf16[64,1024]{1,0:T(8,128)(2,1)S(1)} %get-tuple-element.52.queries_in, bf16[4,1024,1024]{2,1,0:T(8,128)(2,1)S(1)} %load_stack.1.refs_0_, ...), custom_call_target="tpu_custom_call" | custom-call | flops 1677721600 | bytes 786432 | tf_op jit(solution)/shard_map/cross_attention/pallas_call | solution.py:207
  71.2 6.4 %collective-permute-done.19.keys_in = bf16[128,1024]{1,0:T(8,128)(2,1)S(1)} collective-permute-done((bf16[128,1024]{1,0:T(8,128)(2,1)S(1)}, bf16[128,1024]{1,0:T(8,128)(2,1)S(1)}, u32[]{:S(2)}, u32[]{:S(2)}) %collective-permute-start.19) | collective-permute-done | bytes 262176 | tf_op jit(solution)/shard_map/ppermute | solution.py:264
  77.6 3.9 %cross_attention.5 = bf16[64,1024]{1,0:T(8,128)(2,1)S(1)} custom-call(s32[32]{0:T(128)S(1)} %copy-done.2, bf16[128,1024]{1,0:T(8,128)(2,1)S(1)} %collective-permute-done.19.keys_in, bf16[64,1024]{1,0:T(8,128)(2,1)S(1)} %collective-permute-done.11.queries_in, bf16[4,1024,1024]{2,1,0:T(8,128)(2,1)S(1)} %load_stack.1.refs_0_, ...), custom_call_target="tpu_custom_call" | custom-call | flops 1677721600 | bytes 786432 | tf_op jit(solution)/shard_map/cross_attention/pallas_call | solution.py:207
  81.5 2.1 %collective-permute-start.23 = (bf16[64,1024]{1,0:T(8,128)(2,1)S(1)}, bf16[64,1024]{1,0:T(8,128)(2,1)S(1)}, u32[]{:S(2)}, u32[]{:S(2)}) collective-permute-start(bf16[64,1024]{1,0:T(8,128)(2,1)S(1)} %cross_attention.5), channel_id=1, source_target_pairs={{0,2},{1,3},{2,0},{3,1},{4,6},{5,7},{6,4},{7,5},{8,10},{9,11},{10,... | collective-permute-start | bytes 393224 | tf_op jit(solution)/shard_map/ppermute | solution.py:264
  83.6 3.9 %cross_attention.6 = bf16[64,1024]{1,0:T(8,128)(2,1)S(1)} custom-call(s32[32]{0:T(128)S(1)} %copy-done.2, bf16[128,1024]{1,0:T(8,128)(2,1)S(1)} %collective-permute-done.18.keys_in, bf16[64,1024]{1,0:T(8,128)(2,1)S(1)} %collective-permute-done.6.queries_in, bf16[4,1024,1024]{2,1,0:T(8,128)(2,1)S(1)} %load_stack.1.refs_0_, ...), custom_call_target="tpu_custom_call" | custom-call | flops 1677721600 | bytes 786432 | tf_op jit(solution)/shard_map/cross_attention/pallas_call | solution.py:207
  87.5 0.1 collective-permute-start.20
  87.6 3.9 %cross_attention.7 = bf16[64,1024]{1,0:T(8,128)(2,1)S(1)} custom-call(s32[32]{0:T(128)S(1)} %copy-done.2, bf16[128,1024]{1,0:T(8,128)(2,1)S(1)} %collective-permute-done.21.keys_in, bf16[64,1024]{1,0:T(8,128)(2,1)S(1)} %collective-permute-done.22.queries_in, bf16[4,1024,1024]{2,1,0:T(8,128)(2,1)S(1)} %load_stack.1.refs_0_, ...), custom_call_target="tpu_custom_call" | custom-call | flops 1677721600 | bytes 786432 | tf_op jit(solution)/shard_map/cross_attention/pallas_call | solution.py:207
  91.5 2.1 %collective-permute-start.24 = (bf16[64,1024]{1,0:T(8,128)(2,1)S(1)}, bf16[64,1024]{1,0:T(8,128)(2,1)S(1)}, u32[]{:S(2)}, u32[]{:S(2)}) collective-permute-start(bf16[64,1024]{1,0:T(8,128)(2,1)S(1)} %add_convert_fusion.7), channel_id=1, source_target_pairs={{0,6},{1,7},{2,4},{3,5},{4,2},{5,3},{6,0},{7,1},{8,14},{9,15},{10,... | collective-permute-start | bytes 393224 | tf_op jit(solution)/shard_map/ppermute | solution.py:264
  93.6 4.9 %collective-permute-done.24.refs_3_ = bf16[64,1024]{1,0:T(8,128)(2,1)S(1)} collective-permute-done((bf16[64,1024]{1,0:T(8,128)(2,1)S(1)}, bf16[64,1024]{1,0:T(8,128)(2,1)S(1)}, u32[]{:S(2)}, u32[]{:S(2)}) %collective-permute-start.24) | collective-permute-done | bytes 131104 | tf_op jit(solution)/shard_map/ppermute | solution.py:264
  98.5 0.2 sum_norm.5
  98.7 2.4 %collective-permute-start.28 = (bf16[64,1024]{1,0:T(8,128)(2,1)S(1)}, bf16[64,1024]{1,0:T(8,128)(2,1)S(1)}, u32[]{:S(2)}, u32[]{:S(2)}) collective-permute-start(bf16[64,1024]{1,0:T(8,128)(2,1)S(1)} %get-tuple-element.71.refs_0_), channel_id=1, source_target_pairs={{0,4},{1,5},{2,6},{3,7},{4,0},{5,1},{6,2},{7,3},{8,12},{9,13},{10,... | collective-permute-start | bytes 393224 | tf_op jit(solution)/shard_map/ppermute | solution.py:264
  101.2 0.2 collective-permute-start.27
  101.4 2.7 %feed_forward.4 = (bf16[64,1024]{1,0:T(8,128)(2,1)S(1)}, bf16[64,1024]{1,0:T(8,128)(2,1)S(1)}) custom-call(bf16[64,1024]{1,0:T(8,128)(2,1)S(1)} %get-tuple-element.71.refs_0_, bf16[64,1024]{1,0:T(8,128)(2,1)S(1)} %collective-permute-done.25.refs_1_, bf16[1024,4096]{1,0:T(8,128)(2,1)S(1)} %bitcast.9, bf16[4096,1024]{1,0:T(8,128)(2,1)S(1)} %bitcast.11), custom_call_target="tpu_custom_call" | custom-call | flops 2147483648 | bytes 524288 | tf_op jit(solution)/shard_map/feed_forward/pallas_call | solution.py:246
  104.1 4.3 %collective-permute-done.28.refs_0_ = bf16[64,1024]{1,0:T(8,128)(2,1)S(1)} collective-permute-done((bf16[64,1024]{1,0:T(8,128)(2,1)S(1)}, bf16[64,1024]{1,0:T(8,128)(2,1)S(1)}, u32[]{:S(2)}, u32[]{:S(2)}) %collective-permute-start.28) | collective-permute-done | bytes 131104 | tf_op jit(solution)/shard_map/ppermute | solution.py:264
  108.4 0.5 collective-permute-start.26
  109.0 0.8 collective-permute-done.29.refs_1_
  109.7 2.4 %feed_forward.5 = (bf16[64,1024]{1,0:T(8,128)(2,1)S(1)}, bf16[64,1024]{1,0:T(8,128)(2,1)S(1)}) custom-call(bf16[64,1024]{1,0:T(8,128)(2,1)S(1)} %collective-permute-done.28.refs_0_, bf16[64,1024]{1,0:T(8,128)(2,1)S(1)} %collective-permute-done.29.refs_1_, bf16[1024,4096]{1,0:T(8,128)(2,1)S(1)} %bitcast.9, bf16[4096,1024]{1,0:T(8,128)(2,1)S(1)} %bitcast.11), custom_call_target="tpu_custom_call" | custom-call | flops 2147483648 | bytes 524288 | tf_op jit(solution)/shard_map/feed_forward/pallas_call | solution.py:246
  112.2 0.2 collective-permute-start.36
  112.4 2.4 %feed_forward.6 = (bf16[64,1024]{1,0:T(8,128)(2,1)S(1)}, bf16[64,1024]{1,0:T(8,128)(2,1)S(1)}) custom-call(bf16[64,1024]{1,0:T(8,128)(2,1)S(1)} %collective-permute-done.27.refs_0_, bf16[64,1024]{1,0:T(8,128)(2,1)S(1)} %collective-permute-done.30.refs_1_, bf16[1024,4096]{1,0:T(8,128)(2,1)S(1)} %bitcast.9, bf16[4096,1024]{1,0:T(8,128)(2,1)S(1)} %bitcast.11), custom_call_target="tpu_custom_call" | custom-call | flops 2147483648 | bytes 524288 | tf_op jit(solution)/shard_map/feed_forward/pallas_call | solution.py:246
  114.8 0.4 collective-permute-start.34
  115.3 0.1 collective-permute-start.31
  115.5 1.3 collective-permute-start.37
  116.8 2.4 %feed_forward.7 = (bf16[64,1024]{1,0:T(8,128)(2,1)S(1)}, bf16[64,1024]{1,0:T(8,128)(2,1)S(1)}) custom-call(bf16[64,1024]{1,0:T(8,128)(2,1)S(1)} %collective-permute-done.33.refs_0_, bf16[64,1024]{1,0:T(8,128)(2,1)S(1)} %collective-permute-done.34.refs_1_, bf16[1024,4096]{1,0:T(8,128)(2,1)S(1)} %bitcast.9, bf16[4096,1024]{1,0:T(8,128)(2,1)S(1)} %bitcast.11), custom_call_target="tpu_custom_call" | custom-call | flops 2147483648 | bytes 524288 | tf_op jit(solution)/shard_map/feed_forward/pallas_call | solution.py:246
  119.4 1.1 collective-permute-start.32
  120.4 0.9 collective-permute-done.37
  121.4 2.1 %collective-permute-start.38 = (bf16[64,1024]{1,0:T(8,128)(2,1)S(1)}, bf16[64,1024]{1,0:T(8,128)(2,1)S(1)}, u32[]{:S(2)}, u32[]{:S(2)}) collective-permute-start(bf16[64,1024]{1,0:T(8,128)(2,1)S(1)} %add_convert_fusion.4), channel_id=1, source_target_pairs={{0,6},{1,7},{2,4},{3,5},{4,2},{5,3},{6,0},{7,1},{8,14},{9,15},{10,... | collective-permute-start | bytes 393224 | tf_op jit(solution)/shard_map/ppermute | solution.py:264
  123.4 1.9 %collective-permute-done.32 = bf16[64,1024]{1,0:T(8,128)(2,1)S(1)} collective-permute-done((bf16[64,1024]{1,0:T(8,128)(2,1)S(1)}, bf16[64,1024]{1,0:T(8,128)(2,1)S(1)}, u32[]{:S(2)}, u32[]{:S(2)}) %collective-permute-start.32) | collective-permute-done | bytes 131104 | tf_op jit(solution)/shard_map/ppermute | solution.py:264
  125.3 3.6 %collective-permute-done.38 = bf16[64,1024]{1,0:T(8,128)(2,1)S(1)} collective-permute-done((bf16[64,1024]{1,0:T(8,128)(2,1)S(1)}, bf16[64,1024]{1,0:T(8,128)(2,1)S(1)}, u32[]{:S(2)}, u32[]{:S(2)}) %collective-permute-start.38) | collective-permute-done | bytes 131104 | tf_op jit(solution)/shard_map/ppermute | solution.py:264
  129.0 0.1 add_convert_fusion.3
  129.1 4.7 %collective-permute-start.39 = (bf16[64,1024]{1,0:T(8,128)(2,1)S(1)}, bf16[64,1024]{1,0:T(8,128)(2,1)S(1)}, u32[]{:S(2)}, u32[]{:S(2)}) collective-permute-start(bf16[64,1024]{1,0:T(8,128)(2,1)S(1)} %add_convert_fusion.3), channel_id=1, source_target_pairs={{0,0},{4,1},{8,2},{12,3},{16,4},{20,5},{24,6},{28,7},{1,8},{5,9},{... | collective-permute-start | bytes 393224 | tf_op jit(solution)/shard_map/ppermute | solution.py:531
  134.4 8.1 %collective-permute-done.39.refs_0_ = bf16[64,1024]{1,0:T(8,128)(2,1)S(1)} collective-permute-done((bf16[64,1024]{1,0:T(8,128)(2,1)S(1)}, bf16[64,1024]{1,0:T(8,128)(2,1)S(1)}, u32[]{:S(2)}, u32[]{:S(2)}) %collective-permute-start.39) | collective-permute-done | bytes 131104 | tf_op jit(solution)/shard_map/ppermute | solution.py:531
  142.4 0.7 masked.1
  (70 shorter events, 1.1 us)
Async XLA Ops:
  0.6 12.4 %collective-permute-start = (bf16[128,1024]{1,0:T(8,128)(2,1)}, bf16[128,1024]{1,0:T(8,128)(2,1)S(1)}, u32[]{:S(2)}, u32[]{:S(2)}) collective-permute-start(bf16[128,1024]{1,0:T(8,128)(2,1)} %bitcast.12), channel_id=1, source_target_pairs={{0,1},{1,0},{2,3},{3,2},{4,5},{5,4},{6,7},{7,6},{8,9},{9,8},{10,11... | collective-permute-start | bytes 786440 | tf_op jit(solution)/shard_map/ppermute | solution.py:264
  0.7 16.0 %collective-permute-start.3 = (bf16[128,1024]{1,0:T(8,128)(2,1)}, bf16[128,1024]{1,0:T(8,128)(2,1)S(1)}, u32[]{:S(2)}, u32[]{:S(2)}) collective-permute-start(bf16[128,1024]{1,0:T(8,128)(2,1)} %bitcast.13), channel_id=1, source_target_pairs={{0,4},{1,5},{2,6},{3,7},{4,0},{5,1},{6,2},{7,3},{8,12},{9,13},{10,... | collective-permute-start | bytes 786440 | tf_op jit(solution)/shard_map/ppermute | solution.py:264
  3.4 18.6 %collective-permute-start.2 = (bf16[128,1024]{1,0:T(8,128)(2,1)}, bf16[128,1024]{1,0:T(8,128)(2,1)S(1)}, u32[]{:S(2)}, u32[]{:S(2)}) collective-permute-start(bf16[128,1024]{1,0:T(8,128)(2,1)} %bitcast.14), channel_id=1, source_target_pairs={{0,2},{1,3},{2,0},{3,1},{4,6},{5,7},{6,4},{7,5},{8,10},{9,11},{10,... | collective-permute-start | bytes 786440 | tf_op jit(solution)/shard_map/ppermute | solution.py:264
  4.9 0.7 copy-start.6
  7.1 5.9 %copy-start = (bf16[1,128,1024]{2,1,0:T(8,128)(2,1)S(1)}, bf16[1,128,1024]{2,1,0:T(8,128)(2,1)}, u32[]{:S(2)}) copy-start(bf16[1,128,1024]{2,1,0:T(8,128)(2,1)} %param.21) | copy-start | bytes 786436
  7.1 5.9 %copy-start.1 = (f32[1024]{0:T(1024)S(1)}, f32[1024]{0:T(1024)}, u32[]{:S(2)}) copy-start(f32[1024]{0:T(1024)} %param.23) | copy-start | bytes 12292
  7.1 5.9 %copy-start.2 = (s32[32]{0:T(128)S(1)}, s32[32]{0:T(128)}, u32[]{:S(2)}) copy-start(s32[32]{0:T(128)} %lengths.7) | copy-start | bytes 388
  10.7 11.5 %collective-permute-start.4 = (bf16[80,1024]{1,0:T(8,128)(2,1)S(1)}, bf16[80,1024]{1,0:T(8,128)(2,1)S(1)}, u32[]{:S(2)}, u32[]{:S(2)}) collective-permute-start(bf16[80,1024]{1,0:T(8,128)(2,1)S(1)} %decoder_rows.1), channel_id=1, source_target_pairs={{0,0},{1,4},{2,8},{3,12},{4,16},{5,20},{6,24},{7,28},{8,1},{9,5},{... | collective-permute-start | bytes 491528 | tf_op jit(solution)/shard_map/ppermute | solution.py:471
  16.8 5.4 %copy-start.3 = (f32[1024]{0:T(1024)S(1)}, f32[1024]{0:T(1024)}, u32[]{:S(2)}) copy-start(f32[1024]{0:T(1024)} %param.34) | copy-start | bytes 12292
  16.8 6.2 %collective-permute-start.5 = (bf16[128,1024]{1,0:T(8,128)(2,1)S(1)}, bf16[128,1024]{1,0:T(8,128)(2,1)S(1)}, u32[]{:S(2)}, u32[]{:S(2)}) collective-permute-start(bf16[128,1024]{1,0:T(8,128)(2,1)S(1)} %collective-permute-done.3.refs_1_), channel_id=1, source_target_pairs={{0,1},{1,0},{2,3},{3,2},{4,5},{5,4},{6,7},{7,6},{8,9},{9,8},{10,11... | collective-permute-start | bytes 786440 | tf_op jit(solution)/shard_map/ppermute | solution.py:264
  20.4 14.3 %collective-permute-start.7 = (bf16[128,1024]{1,0:T(8,128)(2,1)S(1)}, bf16[128,1024]{1,0:T(8,128)(2,1)S(1)}, u32[]{:S(2)}, u32[]{:S(2)}) collective-permute-start(bf16[128,1024]{1,0:T(8,128)(2,1)S(1)} %collective-permute-done.3.refs_1_), channel_id=1, source_target_pairs={{0,2},{1,3},{2,0},{3,1},{4,6},{5,7},{6,4},{7,5},{8,10},{9,11},{10,... | collective-permute-start | bytes 786440 | tf_op jit(solution)/shard_map/ppermute | solution.py:264
  21.9 12.8 %collective-permute-start.8 = (bf16[128,1024]{1,0:T(8,128)(2,1)S(1)}, bf16[128,1024]{1,0:T(8,128)(2,1)S(1)}, u32[]{:S(2)}, u32[]{:S(2)}) collective-permute-start(bf16[128,1024]{1,0:T(8,128)(2,1)S(1)} %collective-permute-done.2.refs_1_), channel_id=1, source_target_pairs={{0,1},{1,0},{2,3},{3,2},{4,5},{5,4},{6,7},{7,6},{8,9},{9,8},{10,11... | collective-permute-start | bytes 786440 | tf_op jit(solution)/shard_map/ppermute | solution.py:264
  22.4 12.3 %collective-permute-start.6 = (bf16[64,1024]{1,0:T(8,128)(2,1)S(1)}, bf16[64,1024]{1,0:T(8,128)(2,1)S(1)}, u32[]{:S(2)}, u32[]{:S(2)}) collective-permute-start(bf16[64,1024]{1,0:T(8,128)(2,1)S(1)} %get-tuple-element.52.queries_in), channel_id=1, source_target_pairs={{0,2},{1,3},{2,0},{3,1},{4,6},{5,7},{6,4},{7,5},{8,10},{9,11},{10,... | collective-permute-start | bytes 393224 | tf_op jit(solution)/shard_map/ppermute | solution.py:264
  26.7 12.3 %collective-permute-start.14 = (bf16[128,1024]{1,0:T(8,128)(2,1)S(1)}, bf16[128,1024]{1,0:T(8,128)(2,1)S(1)}, u32[]{:S(2)}, u32[]{:S(2)}) collective-permute-start(bf16[128,1024]{1,0:T(8,128)(2,1)S(1)} %get-tuple-element.61), channel_id=1, source_target_pairs={{0,1},{1,0},{2,3},{3,2},{4,5},{5,4},{6,7},{7,6},{8,9},{9,8},{10,11... | collective-permute-start | bytes 786440 | tf_op jit(solution)/shard_map/ppermute | solution.py:264
  26.8 11.7 %collective-permute-start.11 = (bf16[64,1024]{1,0:T(8,128)(2,1)S(1)}, bf16[64,1024]{1,0:T(8,128)(2,1)S(1)}, u32[]{:S(2)}, u32[]{:S(2)}) collective-permute-start(bf16[64,1024]{1,0:T(8,128)(2,1)S(1)} %get-tuple-element.52.queries_in), channel_id=1, source_target_pairs={{0,4},{1,5},{2,6},{3,7},{4,0},{5,1},{6,2},{7,3},{8,12},{9,13},{10,... | collective-permute-start | bytes 393224 | tf_op jit(solution)/shard_map/ppermute | solution.py:264
  38.4 1.6 %collective-permute-start.12 = (bf16[128,1024]{1,0:T(8,128)(2,1)S(1)}, bf16[128,1024]{1,0:T(8,128)(2,1)S(1)}, u32[]{:S(2)}, u32[]{:S(2)}) collective-permute-start(bf16[128,1024]{1,0:T(8,128)(2,1)S(1)} %collective-permute-done.7.refs_1_), channel_id=1, source_target_pairs={{0,1},{1,0},{2,3},{3,2},{4,5},{5,4},{6,7},{7,6},{8,9},{9,8},{10,11... | collective-permute-start | bytes 786440 | tf_op jit(solution)/shard_map/ppermute | solution.py:264
  38.5 5.8 %collective-permute-start.9 = (bf16[128,1024]{1,0:T(8,128)(2,1)S(1)}, bf16[128,1024]{1,0:T(8,128)(2,1)S(1)}, u32[]{:S(2)}, u32[]{:S(2)}) collective-permute-start(bf16[128,1024]{1,0:T(8,128)(2,1)S(1)} %get-tuple-element.57), channel_id=1, source_target_pairs={{0,1},{1,0},{2,3},{3,2},{4,5},{5,4},{6,7},{7,6},{8,9},{9,8},{10,11... | collective-permute-start | bytes 786440 | tf_op jit(solution)/shard_map/ppermute | solution.py:264
  39.1 23.1 %copy-start.4 = (f32[1024]{0:T(1024)S(1)}, f32[1024]{0:T(1024)}, u32[]{:S(2)}) copy-start(f32[1024]{0:T(1024)} %param.29) | copy-start | bytes 12292
  39.1 8.4 %collective-permute-start.15 = (bf16[128,1024]{1,0:T(8,128)(2,1)S(1)}, bf16[128,1024]{1,0:T(8,128)(2,1)S(1)}, u32[]{:S(2)}, u32[]{:S(2)}) collective-permute-start(bf16[128,1024]{1,0:T(8,128)(2,1)S(1)} %add_convert_fusion.1), channel_id=1, source_target_pairs={{0,2},{1,3},{2,0},{3,1},{4,6},{5,7},{6,4},{7,5},{8,10},{9,11},{10,... | collective-permute-start | bytes 786440 | tf_op jit(solution)/shard_map/ppermute | solution.py:264
  43.8 3.7 %collective-permute-start.13 = (bf16[128,1024]{1,0:T(8,128)(2,1)S(1)}, bf16[128,1024]{1,0:T(8,128)(2,1)S(1)}, u32[]{:S(2)}, u32[]{:S(2)}) collective-permute-start(bf16[128,1024]{1,0:T(8,128)(2,1)S(1)} %get-tuple-element.60), channel_id=1, source_target_pairs={{0,1},{1,0},{2,3},{3,2},{4,5},{5,4},{6,7},{7,6},{8,9},{9,8},{10,11... | collective-permute-start | bytes 786440 | tf_op jit(solution)/shard_map/ppermute | solution.py:264
  44.0 3.6 %collective-permute-start.1 = (bf16[128,1024]{1,0:T(8,128)(2,1)S(1)}, bf16[128,1024]{1,0:T(8,128)(2,1)S(1)}, u32[]{:S(2)}, u32[]{:S(2)}) collective-permute-start(bf16[128,1024]{1,0:T(8,128)(2,1)S(1)} %get-tuple-element.49), channel_id=1, source_target_pairs={{0,1},{1,0},{2,3},{3,2},{4,5},{5,4},{6,7},{7,6},{8,9},{9,8},{10,11... | collective-permute-start | bytes 786440 | tf_op jit(solution)/shard_map/ppermute | solution.py:264
  47.6 19.5 %collective-permute-start.17 = (bf16[4,1024,1024]{2,1,0:T(8,128)(2,1)S(1)}, bf16[4,1024,1024]{2,1,0:T(8,128)(2,1)S(1)}, u32[]{:S(2)}, u32[]{:S(2)}) collective-permute-start(bf16[4,1024,1024]{2,1,0:T(8,128)(2,1)S(1)} %load_stack.1.refs_0_), channel_id=1, source_target_pairs={{0,1},{1,0},{2,3},{3,2},{4,5},{5,4},{6,7},{7,6},{8,9},{9,8},{10,11... | collective-permute-start | bytes 25165832 | tf_op jit(solution)/shard_map/ppermute | solution.py:264
  47.7 9.1 %collective-permute-start.10 = (bf16[128,1024]{1,0:T(8,128)(2,1)S(1)}, bf16[128,1024]{1,0:T(8,128)(2,1)S(1)}, u32[]{:S(2)}, u32[]{:S(2)}) collective-permute-start(bf16[128,1024]{1,0:T(8,128)(2,1)S(1)} %add_convert_fusion.2), channel_id=1, source_target_pairs={{0,2},{1,3},{2,0},{3,1},{4,6},{5,7},{6,4},{7,5},{8,10},{9,11},{10,... | collective-permute-start | bytes 786440 | tf_op jit(solution)/shard_map/ppermute | solution.py:264
  48.0 14.2 %collective-permute-start.16 = (bf16[128,1024]{1,0:T(8,128)(2,1)S(1)}, bf16[128,1024]{1,0:T(8,128)(2,1)S(1)}, u32[]{:S(2)}, u32[]{:S(2)}) collective-permute-start(bf16[128,1024]{1,0:T(8,128)(2,1)S(1)} %add_convert_fusion), channel_id=1, source_target_pairs={{0,6},{1,7},{2,4},{3,5},{4,2},{5,3},{6,0},{7,1},{8,14},{9,15},{10,... | collective-permute-start | bytes 786440 | tf_op jit(solution)/shard_map/ppermute | solution.py:264
  63.2 14.4 %collective-permute-start.19 = (bf16[128,1024]{1,0:T(8,128)(2,1)S(1)}, bf16[128,1024]{1,0:T(8,128)(2,1)S(1)}, u32[]{:S(2)}, u32[]{:S(2)}) collective-permute-start(bf16[128,1024]{1,0:T(8,128)(2,1)S(1)} %get-tuple-element.64.keys_in), channel_id=1, source_target_pairs={{0,4},{1,5},{2,6},{3,7},{4,0},{5,1},{6,2},{7,3},{8,12},{9,13},{10,... | collective-permute-start | bytes 786440 | tf_op jit(solution)/shard_map/ppermute | solution.py:264
  65.1 22.5 %collective-permute-start.22 = (bf16[64,1024]{1,0:T(8,128)(2,1)S(1)}, bf16[64,1024]{1,0:T(8,128)(2,1)S(1)}, u32[]{:S(2)}, u32[]{:S(2)}) collective-permute-start(bf16[64,1024]{1,0:T(8,128)(2,1)S(1)} %collective-permute-done.11.queries_in), channel_id=1, source_target_pairs={{0,2},{1,3},{2,0},{3,1},{4,6},{5,7},{6,4},{7,5},{8,10},{9,11},{10,... | collective-permute-start | bytes 393224 | tf_op jit(solution)/shard_map/ppermute | solution.py:264
  65.8 17.8 %collective-permute-start.18 = (bf16[128,1024]{1,0:T(8,128)(2,1)S(1)}, bf16[128,1024]{1,0:T(8,128)(2,1)S(1)}, u32[]{:S(2)}, u32[]{:S(2)}) collective-permute-start(bf16[128,1024]{1,0:T(8,128)(2,1)S(1)} %get-tuple-element.64.keys_in), channel_id=1, source_target_pairs={{0,2},{1,3},{2,0},{3,1},{4,6},{5,7},{6,4},{7,5},{8,10},{9,11},{10,... | collective-permute-start | bytes 786440 | tf_op jit(solution)/shard_map/ppermute | solution.py:264
  77.6 10.0 %collective-permute-start.21 = (bf16[128,1024]{1,0:T(8,128)(2,1)S(1)}, bf16[128,1024]{1,0:T(8,128)(2,1)S(1)}, u32[]{:S(2)}, u32[]{:S(2)}) collective-permute-start(bf16[128,1024]{1,0:T(8,128)(2,1)S(1)} %collective-permute-done.19.keys_in), channel_id=1, source_target_pairs={{0,2},{1,3},{2,0},{3,1},{4,6},{5,7},{6,4},{7,5},{8,10},{9,11},{10,... | collective-permute-start | bytes 786440 | tf_op jit(solution)/shard_map/ppermute | solution.py:264
  81.5 10.0 %collective-permute-start.23 = (bf16[64,1024]{1,0:T(8,128)(2,1)S(1)}, bf16[64,1024]{1,0:T(8,128)(2,1)S(1)}, u32[]{:S(2)}, u32[]{:S(2)}) collective-permute-start(bf16[64,1024]{1,0:T(8,128)(2,1)S(1)} %cross_attention.5), channel_id=1, source_target_pairs={{0,2},{1,3},{2,0},{3,1},{4,6},{5,7},{6,4},{7,5},{8,10},{9,11},{10,... | collective-permute-start | bytes 393224 | tf_op jit(solution)/shard_map/ppermute | solution.py:264
  83.6 17.8 %slice-start = ((s8[8388608]{0:T(1024)(128)(4,1)}), s8[4194304]{0:T(1024)(128)(4,1)S(1)}, s32[]{:S(2)}) async-start(s8[8388608]{0:T(1024)(128)(4,1)} %bitcast.8), calls=%async_computation | async-start | bytes 8388608
  83.6 17.8 %slice-start.2 = ((s8[8388608]{0:T(1024)(128)(4,1)}), s8[4194304]{0:T(1024)(128)(4,1)S(1)}, s32[]{:S(2)}) async-start(s8[8388608]{0:T(1024)(128)(4,1)} %bitcast.10), calls=%async_computation.2 | async-start | bytes 8388608
  87.5 11.0 %copy-start.5 = (f32[1024]{0:T(1024)S(1)}, f32[1024]{0:T(1024)}, u32[]{:S(2)}) copy-start(f32[1024]{0:T(1024)} %param.39) | copy-start | bytes 12292
  87.5 13.9 %slice-start.1 = ((s8[8388608]{0:T(1024)(128)(4,1)}), s8[4194304]{0:T(1024)(128)(4,1)S(1)}, s32[]{:S(2)}) async-start(s8[8388608]{0:T(1024)(128)(4,1)} %bitcast.8), calls=%async_computation.1 | async-start | bytes 8388608
  87.5 13.9 %slice-start.3 = ((s8[8388608]{0:T(1024)(128)(4,1)}), s8[4194304]{0:T(1024)(128)(4,1)S(1)}, s32[]{:S(2)}) async-start(s8[8388608]{0:T(1024)(128)(4,1)} %bitcast.10), calls=%async_computation.3 | async-start | bytes 8388608
  87.5 6.1 %collective-permute-start.20 = (bf16[64,1024]{1,0:T(8,128)(2,1)S(1)}, bf16[64,1024]{1,0:T(8,128)(2,1)S(1)}, u32[]{:S(2)}, u32[]{:S(2)}) collective-permute-start(bf16[64,1024]{1,0:T(8,128)(2,1)S(1)} %cross_attention.6), channel_id=1, source_target_pairs={{0,2},{1,3},{2,0},{3,1},{4,6},{5,7},{6,4},{7,5},{8,10},{9,11},{10,... | collective-permute-start | bytes 393224 | tf_op jit(solution)/shard_map/ppermute | solution.py:264
  91.5 6.9 %collective-permute-start.24 = (bf16[64,1024]{1,0:T(8,128)(2,1)S(1)}, bf16[64,1024]{1,0:T(8,128)(2,1)S(1)}, u32[]{:S(2)}, u32[]{:S(2)}) collective-permute-start(bf16[64,1024]{1,0:T(8,128)(2,1)S(1)} %add_convert_fusion.7), channel_id=1, source_target_pairs={{0,6},{1,7},{2,4},{3,5},{4,2},{5,3},{6,0},{7,1},{8,14},{9,15},{10,... | collective-permute-start | bytes 393224 | tf_op jit(solution)/shard_map/ppermute | solution.py:264
  98.7 2.7 %collective-permute-start.25 = (bf16[64,1024]{1,0:T(8,128)(2,1)S(1)}, bf16[64,1024]{1,0:T(8,128)(2,1)S(1)}, u32[]{:S(2)}, u32[]{:S(2)}) collective-permute-start(bf16[64,1024]{1,0:T(8,128)(2,1)S(1)} %get-tuple-element.71.refs_0_), channel_id=1, source_target_pairs={{0,1},{1,0},{2,3},{3,2},{4,5},{5,4},{6,7},{7,6},{8,9},{9,8},{10,11... | collective-permute-start | bytes 393224 | tf_op jit(solution)/shard_map/ppermute | solution.py:264
  98.7 9.6 %collective-permute-start.28 = (bf16[64,1024]{1,0:T(8,128)(2,1)S(1)}, bf16[64,1024]{1,0:T(8,128)(2,1)S(1)}, u32[]{:S(2)}, u32[]{:S(2)}) collective-permute-start(bf16[64,1024]{1,0:T(8,128)(2,1)S(1)} %get-tuple-element.71.refs_0_), channel_id=1, source_target_pairs={{0,4},{1,5},{2,6},{3,7},{4,0},{5,1},{6,2},{7,3},{8,12},{9,13},{10,... | collective-permute-start | bytes 393224 | tf_op jit(solution)/shard_map/ppermute | solution.py:264
  101.2 7.7 %collective-permute-start.27 = (bf16[64,1024]{1,0:T(8,128)(2,1)S(1)}, bf16[64,1024]{1,0:T(8,128)(2,1)S(1)}, u32[]{:S(2)}, u32[]{:S(2)}) collective-permute-start(bf16[64,1024]{1,0:T(8,128)(2,1)S(1)} %get-tuple-element.71.refs_0_), channel_id=1, source_target_pairs={{0,2},{1,3},{2,0},{3,1},{4,6},{5,7},{6,4},{7,5},{8,10},{9,11},{10,... | collective-permute-start | bytes 393224 | tf_op jit(solution)/shard_map/ppermute | solution.py:264
  108.4 1.3 collective-permute-start.29
  108.4 6.5 %collective-permute-start.33 = (bf16[64,1024]{1,0:T(8,128)(2,1)S(1)}, bf16[64,1024]{1,0:T(8,128)(2,1)S(1)}, u32[]{:S(2)}, u32[]{:S(2)}) collective-permute-start(bf16[64,1024]{1,0:T(8,128)(2,1)S(1)} %collective-permute-done.28.refs_0_), channel_id=1, source_target_pairs={{0,2},{1,3},{2,0},{3,1},{4,6},{5,7},{6,4},{7,5},{8,10},{9,11},{10,... | collective-permute-start | bytes 393224 | tf_op jit(solution)/shard_map/ppermute | solution.py:264
  108.4 15.0 %collective-permute-start.26 = (bf16[64,1024]{1,0:T(8,128)(2,1)S(1)}, bf16[64,1024]{1,0:T(8,128)(2,1)S(1)}, u32[]{:S(2)}, u32[]{:S(2)}) collective-permute-start(bf16[64,1024]{1,0:T(8,128)(2,1)S(1)} %get-tuple-element.73), channel_id=1, source_target_pairs={{0,1},{1,0},{2,3},{3,2},{4,5},{5,4},{6,7},{7,6},{8,9},{9,8},{10,11... | collective-permute-start | bytes 393224 | tf_op jit(solution)/shard_map/ppermute | solution.py:264
  108.9 3.5 %collective-permute-start.30 = (bf16[64,1024]{1,0:T(8,128)(2,1)S(1)}, bf16[64,1024]{1,0:T(8,128)(2,1)S(1)}, u32[]{:S(2)}, u32[]{:S(2)}) collective-permute-start(bf16[64,1024]{1,0:T(8,128)(2,1)S(1)} %collective-permute-done.27.refs_0_), channel_id=1, source_target_pairs={{0,1},{1,0},{2,3},{3,2},{4,5},{5,4},{6,7},{7,6},{8,9},{9,8},{10,11... | collective-permute-start | bytes 393224 | tf_op jit(solution)/shard_map/ppermute | solution.py:264
  112.2 3.3 %collective-permute-start.36 = (bf16[64,1024]{1,0:T(8,128)(2,1)S(1)}, bf16[64,1024]{1,0:T(8,128)(2,1)S(1)}, u32[]{:S(2)}, u32[]{:S(2)}) collective-permute-start(bf16[64,1024]{1,0:T(8,128)(2,1)S(1)} %get-tuple-element.83), channel_id=1, source_target_pairs={{0,1},{1,0},{2,3},{3,2},{4,5},{5,4},{6,7},{7,6},{8,9},{9,8},{10,11... | collective-permute-start | bytes 393224 | tf_op jit(solution)/shard_map/ppermute | solution.py:264
  114.8 2.0 %collective-permute-start.34 = (bf16[64,1024]{1,0:T(8,128)(2,1)S(1)}, bf16[64,1024]{1,0:T(8,128)(2,1)S(1)}, u32[]{:S(2)}, u32[]{:S(2)}) collective-permute-start(bf16[64,1024]{1,0:T(8,128)(2,1)S(1)} %collective-permute-done.33.refs_0_), channel_id=1, source_target_pairs={{0,1},{1,0},{2,3},{3,2},{4,5},{5,4},{6,7},{7,6},{8,9},{9,8},{10,11... | collective-permute-start | bytes 393224 | tf_op jit(solution)/shard_map/ppermute | solution.py:264
  115.3 4.1 %collective-permute-start.31 = (bf16[64,1024]{1,0:T(8,128)(2,1)S(1)}, bf16[64,1024]{1,0:T(8,128)(2,1)S(1)}, u32[]{:S(2)}, u32[]{:S(2)}) collective-permute-start(bf16[64,1024]{1,0:T(8,128)(2,1)S(1)} %get-tuple-element.79), channel_id=1, source_target_pairs={{0,1},{1,0},{2,3},{3,2},{4,5},{5,4},{6,7},{7,6},{8,9},{9,8},{10,11... | collective-permute-start | bytes 393224 | tf_op jit(solution)/shard_map/ppermute | solution.py:264
  115.5 5.8 %collective-permute-start.37 = (bf16[64,1024]{1,0:T(8,128)(2,1)S(1)}, bf16[64,1024]{1,0:T(8,128)(2,1)S(1)}, u32[]{:S(2)}, u32[]{:S(2)}) collective-permute-start(bf16[64,1024]{1,0:T(8,128)(2,1)S(1)} %add_convert_fusion.5), channel_id=1, source_target_pairs={{0,2},{1,3},{2,0},{3,1},{4,6},{5,7},{6,4},{7,5},{8,10},{9,11},{10,... | collective-permute-start | bytes 393224 | tf_op jit(solution)/shard_map/ppermute | solution.py:264
  119.2 2.0 %collective-permute-start.35 = (bf16[64,1024]{1,0:T(8,128)(2,1)S(1)}, bf16[64,1024]{1,0:T(8,128)(2,1)S(1)}, u32[]{:S(2)}, u32[]{:S(2)}) collective-permute-start(bf16[64,1024]{1,0:T(8,128)(2,1)S(1)} %get-tuple-element.82), channel_id=1, source_target_pairs={{0,1},{1,0},{2,3},{3,2},{4,5},{5,4},{6,7},{7,6},{8,9},{9,8},{10,11... | collective-permute-start | bytes 393224 | tf_op jit(solution)/shard_map/ppermute | solution.py:264
  119.4 6.0 %collective-permute-start.32 = (bf16[64,1024]{1,0:T(8,128)(2,1)S(1)}, bf16[64,1024]{1,0:T(8,128)(2,1)S(1)}, u32[]{:S(2)}, u32[]{:S(2)}) collective-permute-start(bf16[64,1024]{1,0:T(8,128)(2,1)S(1)} %add_convert_fusion.6), channel_id=1, source_target_pairs={{0,2},{1,3},{2,0},{3,1},{4,6},{5,7},{6,4},{7,5},{8,10},{9,11},{10,... | collective-permute-start | bytes 393224 | tf_op jit(solution)/shard_map/ppermute | solution.py:264
  121.4 7.6 %collective-permute-start.38 = (bf16[64,1024]{1,0:T(8,128)(2,1)S(1)}, bf16[64,1024]{1,0:T(8,128)(2,1)S(1)}, u32[]{:S(2)}, u32[]{:S(2)}) collective-permute-start(bf16[64,1024]{1,0:T(8,128)(2,1)S(1)} %add_convert_fusion.4), channel_id=1, source_target_pairs={{0,6},{1,7},{2,4},{3,5},{4,2},{5,3},{6,0},{7,1},{8,14},{9,15},{10,... | collective-permute-start | bytes 393224 | tf_op jit(solution)/shard_map/ppermute | solution.py:264
  129.1 13.4 %collective-permute-start.39 = (bf16[64,1024]{1,0:T(8,128)(2,1)S(1)}, bf16[64,1024]{1,0:T(8,128)(2,1)S(1)}, u32[]{:S(2)}, u32[]{:S(2)}) collective-permute-start(bf16[64,1024]{1,0:T(8,128)(2,1)S(1)} %add_convert_fusion.3), channel_id=1, source_target_pairs={{0,0},{4,1},{8,2},{12,3},{16,4},{20,5},{24,6},{28,7},{1,8},{5,9},{... | collective-permute-start | bytes 393224 | tf_op jit(solution)/shard_map/ppermute | solution.py:531

commit v3 on v2

--- a/solution.py
+++ b/solution.py
@@ -11,12 +11,12 @@
 MAXREL = 16
 NB = 33
 LANG_ROWS = 16
-OPT = dict(enc="213", mem="213", ffn="213", p3=("enc",), p1=(), dec="early", norm2=True, p3tie=("enc", "mem", "ffn"), straight=False, pieces=1, home="w", dtie=False, w="all", ls=2)
+OPT = dict(enc="213", mem="213", ffn="213", p3=("enc",), p1=(), dec="early", norm2=True, p3tie=("enc", "mem", "ffn"), straight=False, pieces=1, home="w", dtie=True, w="all", ls=2)
 EPSILON = 1e-06
 NEG_FILL = -1e30
 FFN_STEP = 512
 OUT_STEP = 256
-VMEM_LIMIT = 16 * 1024 * 1024
+VMEM_LIMIT = 10 * 1024 * 1024
 
 IN_VMEM = pl.BlockSpec(memory_space=pltpu.VMEM)
 IN_HBM = pl.BlockSpec(memory_space=pltpu.HBM)

time: 143 us -> 143 us (level)
  no operation moved by 1% of the time
where the time goes in v3:
time: 143 us
  waiting for transfers between devices  51.7 us (36%)
  Pallas kernels  51 us (36%)
  starting transfers between devices  37.3 us (26%)
  between operations  1.76 us (1%)
    ppermute x38, waiting for transfers between devices, swap(): return lax.ppermute(value, 'tensor', [(i, i ^ bits) for i in range(size)])  43.8 us
    ppermute x38, starting transfers between devices, swap(): return lax.ppermute(value, 'tensor', [(i, i ^ bits) for i in range(size)])  30.3 us
    pallas_call x4, Pallas kernels, cross_attention(): pl.pallas_call(functools.partial(cross_body, slot, lax.axis_size('tensor'...  15.6 us
    pallas_call x4, Pallas kernels, self_attention(): pl.pallas_call(functools.partial(self_body, parts, first_slot, lax.axis_s...  14.9 us
    pallas_call x4, Pallas kernels, ffn(): pl.pallas_call(functools.partial(ffn_body, parts), in_specs=[IN_VMEM] * (...  9.97 us
    ppermute x1, waiting for transfers between devices, on_device(): lax.ppermute(bf16_sum(hidden, *ffn_terms), ('dp', 'tensor'), to_home)  7.99 us
    ppermute x1, starting transfers between devices, on_device(): lax.ppermute(bf16_sum(hidden, *ffn_terms), ('dp', 'tensor'), to_home)  4.69 us
    pallas_call x1, Pallas kernels, load(): pl.pallas_call(functools.partial(load_body, count), in_specs=[IN_HBM] * (...  3.55 us
  transfers between devices with their start and end apart: 40, of which 13 were waited for; matrix products, arithmetic and copies ran while one was open for 0% of the time, Pallas kernels for 35%

profile of v3, /device:TPU:4, one launch (start us, length us, event | category | flops | bytes accessed | tf_op | source)
XLA Modules:
  0.0 143.1 jit_solution(8672082370246076525)
XLA Ops:
  0.6 0.1 collective-permute-start
  0.7 2.7 %collective-permute-start.3 = (bf16[128,1024]{1,0:T(8,128)(2,1)}, bf16[128,1024]{1,0:T(8,128)(2,1)S(1)}, u32[]{:S(2)}, u32[]{:S(2)}) collective-permute-start(bf16[128,1024]{1,0:T(8,128)(2,1)} %bitcast.13), channel_id=1, source_target_pairs={{0,4},{1,5},{2,6},{3,7},{4,0},{5,1},{6,2},{7,3},{8,12},{9,13},{10,... | collective-permute-start | bytes 786440 | tf_op jit(solution)/shard_map/ppermute | solution.py:264
  3.4 1.6 %collective-permute-start.2 = (bf16[128,1024]{1,0:T(8,128)(2,1)}, bf16[128,1024]{1,0:T(8,128)(2,1)S(1)}, u32[]{:S(2)}, u32[]{:S(2)}) collective-permute-start(bf16[128,1024]{1,0:T(8,128)(2,1)} %bitcast.14), channel_id=1, source_target_pairs={{0,2},{1,3},{2,0},{3,1},{4,6},{5,7},{6,4},{7,5},{8,10},{9,11},{10,... | collective-permute-start | bytes 786440 | tf_op jit(solution)/shard_map/ppermute | solution.py:264
  4.9 0.7 copy-done.6
  5.6 1.5 %decoder_rows.1 = bf16[80,1024]{1,0:T(8,128)(2,1)S(1)} custom-call(s32[8]{0:T(128)S(1)} %copy-done.6, bf16[64,1024]{1,0:T(8,128)(2,1)} %bitcast.24, bf16[8,1024]{1,0:T(8,128)(2,1)} %table.1), custom_call_target="tpu_custom_call" | custom-call | tf_op jit(solution)/shard_map/decoder_rows/pallas_call | solution.py:362
  7.1 3.5 %load.1 = (bf16[1024,1024]{1,0:T(8,128)(2,1)S(1)}, bf16[1024,1024]{1,0:T(8,128)(2,1)S(1)}, bf16[1024,1024]{1,0:T(8,128)(2,1)S(1)}, bf16[1024,1024]{1,0:T(8,128)(2,1)S(1)}, f32[8,128,128]{2,1,0:T(8,128)S(1)}) custom-call(bf16[1024,1024]{1,0:T(8,128)(2,1)} %refs_0_.6, bf16[1024,1024]{1,0:T(8,128)(2,1)} %refs_1_.2, bf16[1024,1024]{1,0:T(8,128)(2,1)} %refs_2_.6, ...), custom_call_target="tpu_custom_call" | custom-call | bytes 16777216 | tf_op jit(solution)/shard_map/load/pallas_call | solution.py:69
  10.7 2.3 %collective-permute-start.4 = (bf16[80,1024]{1,0:T(8,128)(2,1)S(1)}, bf16[80,1024]{1,0:T(8,128)(2,1)S(1)}, u32[]{:S(2)}, u32[]{:S(2)}) collective-permute-start(bf16[80,1024]{1,0:T(8,128)(2,1)S(1)} %decoder_rows.1), channel_id=1, source_target_pairs={{0,0},{1,4},{2,8},{3,12},{4,16},{5,20},{6,24},{7,28},{8,1},{9,5},{... | collective-permute-start | bytes 491528 | tf_op jit(solution)/shard_map/ppermute | solution.py:471
  13.0 3.7 %self_attention.4 = (bf16[128,1024]{1,0:T(8,128)(2,1)S(1)}, bf16[128,1024]{1,0:T(8,128)(2,1)S(1)}) custom-call(s32[32]{0:T(128)S(1)} %copy-done.2, bf16[128,1024]{1,0:T(8,128)(2,1)S(1)} %bitcast.15, bf16[128,1024]{1,0:T(8,128)(2,1)S(1)} %collective-permute-done.refs_2_, bf16[1024,1024]{1,0:T(8,128)(2,1)S(1)} %get-tuple-element.44.refs_3_, ...), custom_call_target="tpu_custom_call" | custom-call | flops 2281701376 | bytes 1048576 | tf_op jit(solution)/shard_map/self_attention/pallas_call | solution.py:169
  16.9 3.5 %load_stack.1.refs_0_ = bf16[4,1024,1024]{2,1,0:T(8,128)(2,1)S(1)} custom-call(bf16[1024,1024]{1,0:T(8,128)(2,1)} %refs_0_.8, bf16[1024,1024]{1,0:T(8,128)(2,1)} %refs_1_.3, bf16[1024,1024]{1,0:T(8,128)(2,1)} %refs_2_.7, bf16[1024,1024]{1,0:T(8,128)(2,1)} %refs_3_.7), custom_call_target="tpu_custom_call" | custom-call | tf_op jit(solution)/shard_map/load_stack/pallas_call | solution.py:98
  20.4 1.6 %collective-permute-start.7 = (bf16[128,1024]{1,0:T(8,128)(2,1)S(1)}, bf16[128,1024]{1,0:T(8,128)(2,1)S(1)}, u32[]{:S(2)}, u32[]{:S(2)}) collective-permute-start(bf16[128,1024]{1,0:T(8,128)(2,1)S(1)} %collective-permute-done.3.refs_1_), channel_id=1, source_target_pairs={{0,2},{1,3},{2,0},{3,1},{4,6},{5,7},{6,4},{7,5},{8,10},{9,11},{10,... | collective-permute-start | bytes 786440 | tf_op jit(solution)/shard_map/ppermute | solution.py:264
  21.9 0.2 collective-permute-start.8
  22.2 0.1 sum_norm.3
  22.4 0.6 collective-permute-start.6
  23.0 3.7 %self_attention.5 = (bf16[128,1024]{1,0:T(8,128)(2,1)S(1)}, bf16[128,1024]{1,0:T(8,128)(2,1)S(1)}) custom-call(s32[32]{0:T(128)S(1)} %copy-done.2, bf16[128,1024]{1,0:T(8,128)(2,1)S(1)} %collective-permute-done.3.refs_1_, bf16[128,1024]{1,0:T(8,128)(2,1)S(1)} %collective-permute-done.5.refs_2_, bf16[1024,1024]{1,0:T(8,128)(2,1)S(1)} %get-tuple-element.44.refs_3_, ...), custom_call_target="tpu_custom_call" | custom-call | flops 2281701376 | bytes 1048576 | tf_op jit(solution)/shard_map/self_attention/pallas_call | solution.py:169
  26.8 3.2 %collective-permute-start.11 = (bf16[64,1024]{1,0:T(8,128)(2,1)S(1)}, bf16[64,1024]{1,0:T(8,128)(2,1)S(1)}, u32[]{:S(2)}, u32[]{:S(2)}) collective-permute-start(bf16[64,1024]{1,0:T(8,128)(2,1)S(1)} %get-tuple-element.56.queries_in), channel_id=1, source_target_pairs={{0,4},{1,5},{2,6},{3,7},{4,0},{5,1},{6,2},{7,3},{8,12},{9,13},{10,... | collective-permute-start | bytes 393224 | tf_op jit(solution)/shard_map/ppermute | solution.py:264
  30.0 4.7 %collective-permute-done.6.queries_in = bf16[64,1024]{1,0:T(8,128)(2,1)S(1)} collective-permute-done((bf16[64,1024]{1,0:T(8,128)(2,1)S(1)}, bf16[64,1024]{1,0:T(8,128)(2,1)S(1)}, u32[]{:S(2)}, u32[]{:S(2)}) %collective-permute-start.6) | collective-permute-done | bytes 131104 | tf_op jit(solution)/shard_map/ppermute | solution.py:264
  34.7 3.7 %self_attention.6 = (bf16[128,1024]{1,0:T(8,128)(2,1)S(1)}, bf16[128,1024]{1,0:T(8,128)(2,1)S(1)}) custom-call(s32[32]{0:T(128)S(1)} %copy-done.2, bf16[128,1024]{1,0:T(8,128)(2,1)S(1)} %collective-permute-done.2.refs_1_, bf16[128,1024]{1,0:T(8,128)(2,1)S(1)} %collective-permute-done.8.refs_2_, bf16[1024,1024]{1,0:T(8,128)(2,1)S(1)} %get-tuple-element.44.refs_3_, ...), custom_call_target="tpu_custom_call" | custom-call | flops 2281701376 | bytes 1048576 | tf_op jit(solution)/shard_map/self_attention/pallas_call | solution.py:169
  38.5 0.5 collective-permute-start.9
  39.2 0.9 collective-permute-done.12.refs_2_
  40.0 3.7 %self_attention.7 = (bf16[128,1024]{1,0:T(8,128)(2,1)S(1)}, bf16[128,1024]{1,0:T(8,128)(2,1)S(1)}) custom-call(s32[32]{0:T(128)S(1)} %copy-done.2, bf16[128,1024]{1,0:T(8,128)(2,1)S(1)} %collective-permute-done.7.refs_1_, bf16[128,1024]{1,0:T(8,128)(2,1)S(1)} %collective-permute-done.12.refs_2_, bf16[1024,1024]{1,0:T(8,128)(2,1)S(1)} %get-tuple-element.44.refs_3_, ...), custom_call_target="tpu_custom_call" | custom-call | flops 2281701376 | bytes 1048576 | tf_op jit(solution)/shard_map/self_attention/pallas_call | solution.py:169
  43.8 0.2 collective-permute-start.13
  44.0 0.4 collective-permute-start.1
  44.4 3.0 %collective-permute-done.15 = bf16[128,1024]{1,0:T(8,128)(2,1)S(1)} collective-permute-done((bf16[128,1024]{1,0:T(8,128)(2,1)S(1)}, bf16[128,1024]{1,0:T(8,128)(2,1)S(1)}, u32[]{:S(2)}, u32[]{:S(2)}) %collective-permute-start.15) | collective-permute-done | bytes 262176 | tf_op jit(solution)/shard_map/ppermute | solution.py:264
  47.5 0.1 add_convert_fusion
  47.7 0.4 collective-permute-start.10
  48.0 1.8 %collective-permute-start.16 = (bf16[128,1024]{1,0:T(8,128)(2,1)S(1)}, bf16[128,1024]{1,0:T(8,128)(2,1)S(1)}, u32[]{:S(2)}, u32[]{:S(2)}) collective-permute-start(bf16[128,1024]{1,0:T(8,128)(2,1)S(1)} %add_convert_fusion), channel_id=1, source_target_pairs={{0,6},{1,7},{2,4},{3,5},{4,2},{5,3},{6,0},{7,1},{8,14},{9,15},{10,... | collective-permute-start | bytes 786440 | tf_op jit(solution)/shard_map/ppermute | solution.py:264
  49.8 7.0 %collective-permute-done.10.refs_3_ = bf16[128,1024]{1,0:T(8,128)(2,1)S(1)} collective-permute-done((bf16[128,1024]{1,0:T(8,128)(2,1)S(1)}, bf16[128,1024]{1,0:T(8,128)(2,1)S(1)}, u32[]{:S(2)}, u32[]{:S(2)}) %collective-permute-start.10) | collective-permute-done | bytes 262176 | tf_op jit(solution)/shard_map/ppermute | solution.py:264
  56.8 5.4 %collective-permute-done.16.refs_4_ = bf16[128,1024]{1,0:T(8,128)(2,1)S(1)} collective-permute-done((bf16[128,1024]{1,0:T(8,128)(2,1)S(1)}, bf16[128,1024]{1,0:T(8,128)(2,1)S(1)}, u32[]{:S(2)}, u32[]{:S(2)}) %collective-permute-start.16) | collective-permute-done | bytes 262176 | tf_op jit(solution)/shard_map/ppermute | solution.py:264
  62.2 1.0 sum_norm.4
  63.2 1.9 %collective-permute-start.19 = (bf16[128,1024]{1,0:T(8,128)(2,1)S(1)}, bf16[128,1024]{1,0:T(8,128)(2,1)S(1)}, u32[]{:S(2)}, u32[]{:S(2)}) collective-permute-start(bf16[128,1024]{1,0:T(8,128)(2,1)S(1)} %get-tuple-element.66.keys_in), channel_id=1, source_target_pairs={{0,4},{1,5},{2,6},{3,7},{4,0},{5,1},{6,2},{7,3},{8,12},{9,13},{10,... | collective-permute-start | bytes 786440 | tf_op jit(solution)/shard_map/ppermute | solution.py:264
  65.1 0.7 collective-permute-start.22
  65.8 1.4 collective-permute-start.18
  67.1 4.0 %cross_attention.4.refs_1_ = bf16[64,1024]{1,0:T(8,128)(2,1)S(1)} custom-call(s32[32]{0:T(128)S(1)} %copy-done.2, bf16[128,1024]{1,0:T(8,128)(2,1)S(1)} %get-tuple-element.66.keys_in, bf16[64,1024]{1,0:T(8,128)(2,1)S(1)} %get-tuple-element.56.queries_in, bf16[4,1024,1024]{2,1,0:T(8,128)(2,1)S(1)} %load_stack.1.refs_0_, ...), custom_call_target="tpu_custom_call" | custom-call | flops 1677721600 | bytes 786432 | tf_op jit(solution)/shard_map/cross_attention/pallas_call | solution.py:207
  71.2 6.4 %collective-permute-done.19.keys_in = bf16[128,1024]{1,0:T(8,128)(2,1)S(1)} collective-permute-done((bf16[128,1024]{1,0:T(8,128)(2,1)S(1)}, bf16[128,1024]{1,0:T(8,128)(2,1)S(1)}, u32[]{:S(2)}, u32[]{:S(2)}) %collective-permute-start.19) | collective-permute-done | bytes 262176 | tf_op jit(solution)/shard_map/ppermute | solution.py:264
  77.6 3.9 %cross_attention.5 = bf16[64,1024]{1,0:T(8,128)(2,1)S(1)} custom-call(s32[32]{0:T(128)S(1)} %copy-done.2, bf16[128,1024]{1,0:T(8,128)(2,1)S(1)} %collective-permute-done.19.keys_in, bf16[64,1024]{1,0:T(8,128)(2,1)S(1)} %collective-permute-done.11.queries_in, bf16[4,1024,1024]{2,1,0:T(8,128)(2,1)S(1)} %load_stack.1.refs_0_, ...), custom_call_target="tpu_custom_call" | custom-call | flops 1677721600 | bytes 786432 | tf_op jit(solution)/shard_map/cross_attention/pallas_call | solution.py:207
  81.5 2.1 %collective-permute-start.23 = (bf16[64,1024]{1,0:T(8,128)(2,1)S(1)}, bf16[64,1024]{1,0:T(8,128)(2,1)S(1)}, u32[]{:S(2)}, u32[]{:S(2)}) collective-permute-start(bf16[64,1024]{1,0:T(8,128)(2,1)S(1)} %cross_attention.5), channel_id=1, source_target_pairs={{0,2},{1,3},{2,0},{3,1},{4,6},{5,7},{6,4},{7,5},{8,10},{9,11},{10,... | collective-permute-start | bytes 393224 | tf_op jit(solution)/shard_map/ppermute | solution.py:264
  83.6 3.9 %cross_attention.6 = bf16[64,1024]{1,0:T(8,128)(2,1)S(1)} custom-call(s32[32]{0:T(128)S(1)} %copy-done.2, bf16[128,1024]{1,0:T(8,128)(2,1)S(1)} %collective-permute-done.18.keys_in, bf16[64,1024]{1,0:T(8,128)(2,1)S(1)} %collective-permute-done.6.queries_in, bf16[4,1024,1024]{2,1,0:T(8,128)(2,1)S(1)} %load_stack.1.refs_0_, ...), custom_call_target="tpu_custom_call" | custom-call | flops 1677721600 | bytes 786432 | tf_op jit(solution)/shard_map/cross_attention/pallas_call | solution.py:207
  87.5 0.1 collective-permute-start.20
  87.6 3.9 %cross_attention.7 = bf16[64,1024]{1,0:T(8,128)(2,1)S(1)} custom-call(s32[32]{0:T(128)S(1)} %copy-done.2, bf16[128,1024]{1,0:T(8,128)(2,1)S(1)} %collective-permute-done.21.keys_in, bf16[64,1024]{1,0:T(8,128)(2,1)S(1)} %collective-permute-done.22.queries_in, bf16[4,1024,1024]{2,1,0:T(8,128)(2,1)S(1)} %load_stack.1.refs_0_, ...), custom_call_target="tpu_custom_call" | custom-call | flops 1677721600 | bytes 786432 | tf_op jit(solution)/shard_map/cross_attention/pallas_call | solution.py:207
  91.5 2.1 %collective-permute-start.24 = (bf16[64,1024]{1,0:T(8,128)(2,1)S(1)}, bf16[64,1024]{1,0:T(8,128)(2,1)S(1)}, u32[]{:S(2)}, u32[]{:S(2)}) collective-permute-start(bf16[64,1024]{1,0:T(8,128)(2,1)S(1)} %add_convert_fusion.7), channel_id=1, source_target_pairs={{0,6},{1,7},{2,4},{3,5},{4,2},{5,3},{6,0},{7,1},{8,14},{9,15},{10,... | collective-permute-start | bytes 393224 | tf_op jit(solution)/shard_map/ppermute | solution.py:264
  93.6 4.8 %collective-permute-done.24.refs_3_ = bf16[64,1024]{1,0:T(8,128)(2,1)S(1)} collective-permute-done((bf16[64,1024]{1,0:T(8,128)(2,1)S(1)}, bf16[64,1024]{1,0:T(8,128)(2,1)S(1)}, u32[]{:S(2)}, u32[]{:S(2)}) %collective-permute-start.24) | collective-permute-done | bytes 131104 | tf_op jit(solution)/shard_map/ppermute | solution.py:264
  98.5 0.2 sum_norm.5
  98.7 2.5 %collective-permute-start.28 = (bf16[64,1024]{1,0:T(8,128)(2,1)S(1)}, bf16[64,1024]{1,0:T(8,128)(2,1)S(1)}, u32[]{:S(2)}, u32[]{:S(2)}) collective-permute-start(bf16[64,1024]{1,0:T(8,128)(2,1)S(1)} %get-tuple-element.73.refs_0_), channel_id=1, source_target_pairs={{0,4},{1,5},{2,6},{3,7},{4,0},{5,1},{6,2},{7,3},{8,12},{9,13},{10,... | collective-permute-start | bytes 393224 | tf_op jit(solution)/shard_map/ppermute | solution.py:264
  101.2 0.2 collective-permute-start.27
  101.4 2.7 %feed_forward.4 = (bf16[64,1024]{1,0:T(8,128)(2,1)S(1)}, bf16[64,1024]{1,0:T(8,128)(2,1)S(1)}) custom-call(bf16[64,1024]{1,0:T(8,128)(2,1)S(1)} %get-tuple-element.73.refs_0_, bf16[64,1024]{1,0:T(8,128)(2,1)S(1)} %collective-permute-done.25.refs_1_, bf16[1024,4096]{1,0:T(8,128)(2,1)S(1)} %bitcast.9, bf16[4096,1024]{1,0:T(8,128)(2,1)S(1)} %bitcast.11), custom_call_target="tpu_custom_call" | custom-call | flops 2147483648 | bytes 524288 | tf_op jit(solution)/shard_map/feed_forward/pallas_call | solution.py:246
  104.1 4.3 %collective-permute-done.28.refs_0_ = bf16[64,1024]{1,0:T(8,128)(2,1)S(1)} collective-permute-done((bf16[64,1024]{1,0:T(8,128)(2,1)S(1)}, bf16[64,1024]{1,0:T(8,128)(2,1)S(1)}, u32[]{:S(2)}, u32[]{:S(2)}) %collective-permute-start.28) | collective-permute-done | bytes 131104 | tf_op jit(solution)/shard_map/ppermute | solution.py:264
  108.4 0.5 collective-permute-start.26
  109.0 0.8 collective-permute-done.29.refs_1_
  109.8 2.4 %feed_forward.5 = (bf16[64,1024]{1,0:T(8,128)(2,1)S(1)}, bf16[64,1024]{1,0:T(8,128)(2,1)S(1)}) custom-call(bf16[64,1024]{1,0:T(8,128)(2,1)S(1)} %collective-permute-done.28.refs_0_, bf16[64,1024]{1,0:T(8,128)(2,1)S(1)} %collective-permute-done.29.refs_1_, bf16[1024,4096]{1,0:T(8,128)(2,1)S(1)} %bitcast.9, bf16[4096,1024]{1,0:T(8,128)(2,1)S(1)} %bitcast.11), custom_call_target="tpu_custom_call" | custom-call | flops 2147483648 | bytes 524288 | tf_op jit(solution)/shard_map/feed_forward/pallas_call | solution.py:246
  112.2 0.2 collective-permute-start.36
  112.4 2.4 %feed_forward.6 = (bf16[64,1024]{1,0:T(8,128)(2,1)S(1)}, bf16[64,1024]{1,0:T(8,128)(2,1)S(1)}) custom-call(bf16[64,1024]{1,0:T(8,128)(2,1)S(1)} %collective-permute-done.27.refs_0_, bf16[64,1024]{1,0:T(8,128)(2,1)S(1)} %collective-permute-done.30.refs_1_, bf16[1024,4096]{1,0:T(8,128)(2,1)S(1)} %bitcast.9, bf16[4096,1024]{1,0:T(8,128)(2,1)S(1)} %bitcast.11), custom_call_target="tpu_custom_call" | custom-call | flops 2147483648 | bytes 524288 | tf_op jit(solution)/shard_map/feed_forward/pallas_call | solution.py:246
  114.9 0.4 collective-permute-start.34
  115.3 0.2 collective-permute-start.31
  115.5 1.3 collective-permute-start.37
  116.8 2.4 %feed_forward.7 = (bf16[64,1024]{1,0:T(8,128)(2,1)S(1)}, bf16[64,1024]{1,0:T(8,128)(2,1)S(1)}) custom-call(bf16[64,1024]{1,0:T(8,128)(2,1)S(1)} %collective-permute-done.33.refs_0_, bf16[64,1024]{1,0:T(8,128)(2,1)S(1)} %collective-permute-done.34.refs_1_, bf16[1024,4096]{1,0:T(8,128)(2,1)S(1)} %bitcast.9, bf16[4096,1024]{1,0:T(8,128)(2,1)S(1)} %bitcast.11), custom_call_target="tpu_custom_call" | custom-call | flops 2147483648 | bytes 524288 | tf_op jit(solution)/shard_map/feed_forward/pallas_call | solution.py:246
  119.4 1.1 collective-permute-start.32
  120.5 0.9 collective-permute-done.37
  121.4 2.0 %collective-permute-start.38 = (bf16[64,1024]{1,0:T(8,128)(2,1)S(1)}, bf16[64,1024]{1,0:T(8,128)(2,1)S(1)}, u32[]{:S(2)}, u32[]{:S(2)}) collective-permute-start(bf16[64,1024]{1,0:T(8,128)(2,1)S(1)} %add_convert_fusion.4), channel_id=1, source_target_pairs={{0,6},{1,7},{2,4},{3,5},{4,2},{5,3},{6,0},{7,1},{8,14},{9,15},{10,... | collective-permute-start | bytes 393224 | tf_op jit(solution)/shard_map/ppermute | solution.py:264
  123.4 1.9 %collective-permute-done.32 = bf16[64,1024]{1,0:T(8,128)(2,1)S(1)} collective-permute-done((bf16[64,1024]{1,0:T(8,128)(2,1)S(1)}, bf16[64,1024]{1,0:T(8,128)(2,1)S(1)}, u32[]{:S(2)}, u32[]{:S(2)}) %collective-permute-start.32) | collective-permute-done | bytes 131104 | tf_op jit(solution)/shard_map/ppermute | solution.py:264
  125.4 3.6 %collective-permute-done.38 = bf16[64,1024]{1,0:T(8,128)(2,1)S(1)} collective-permute-done((bf16[64,1024]{1,0:T(8,128)(2,1)S(1)}, bf16[64,1024]{1,0:T(8,128)(2,1)S(1)}, u32[]{:S(2)}, u32[]{:S(2)}) %collective-permute-start.38) | collective-permute-done | bytes 131104 | tf_op jit(solution)/shard_map/ppermute | solution.py:264
  129.0 0.1 add_convert_fusion.3
  129.0 4.7 %collective-permute-start.39 = (bf16[64,1024]{1,0:T(8,128)(2,1)S(1)}, bf16[64,1024]{1,0:T(8,128)(2,1)S(1)}, u32[]{:S(2)}, u32[]{:S(2)}) collective-permute-start(bf16[64,1024]{1,0:T(8,128)(2,1)S(1)} %add_convert_fusion.3), channel_id=1, source_target_pairs={{0,0},{4,1},{8,2},{12,3},{16,4},{20,5},{24,6},{28,7},{1,8},{5,9},{... | collective-permute-start | bytes 393224 | tf_op jit(solution)/shard_map/ppermute | solution.py:531
  134.4 8.0 %collective-permute-done.39.refs_0_ = bf16[64,1024]{1,0:T(8,128)(2,1)S(1)} collective-permute-done((bf16[64,1024]{1,0:T(8,128)(2,1)S(1)}, bf16[64,1024]{1,0:T(8,128)(2,1)S(1)}, u32[]{:S(2)}, u32[]{:S(2)}) %collective-permute-start.39) | collective-permute-done | bytes 131104 | tf_op jit(solution)/shard_map/ppermute | solution.py:531
  142.4 0.7 masked.1
  (70 shorter events, 1.0 us)
Async XLA Ops:
  0.6 12.4 %collective-permute-start = (bf16[128,1024]{1,0:T(8,128)(2,1)}, bf16[128,1024]{1,0:T(8,128)(2,1)S(1)}, u32[]{:S(2)}, u32[]{:S(2)}) collective-permute-start(bf16[128,1024]{1,0:T(8,128)(2,1)} %bitcast.12), channel_id=1, source_target_pairs={{0,1},{1,0},{2,3},{3,2},{4,5},{5,4},{6,7},{7,6},{8,9},{9,8},{10,11... | collective-permute-start | bytes 786440 | tf_op jit(solution)/shard_map/ppermute | solution.py:264
  0.7 16.0 %collective-permute-start.3 = (bf16[128,1024]{1,0:T(8,128)(2,1)}, bf16[128,1024]{1,0:T(8,128)(2,1)S(1)}, u32[]{:S(2)}, u32[]{:S(2)}) collective-permute-start(bf16[128,1024]{1,0:T(8,128)(2,1)} %bitcast.13), channel_id=1, source_target_pairs={{0,4},{1,5},{2,6},{3,7},{4,0},{5,1},{6,2},{7,3},{8,12},{9,13},{10,... | collective-permute-start | bytes 786440 | tf_op jit(solution)/shard_map/ppermute | solution.py:264
  3.4 18.6 %collective-permute-start.2 = (bf16[128,1024]{1,0:T(8,128)(2,1)}, bf16[128,1024]{1,0:T(8,128)(2,1)S(1)}, u32[]{:S(2)}, u32[]{:S(2)}) collective-permute-start(bf16[128,1024]{1,0:T(8,128)(2,1)} %bitcast.14), channel_id=1, source_target_pairs={{0,2},{1,3},{2,0},{3,1},{4,6},{5,7},{6,4},{7,5},{8,10},{9,11},{10,... | collective-permute-start | bytes 786440 | tf_op jit(solution)/shard_map/ppermute | solution.py:264
  4.9 0.7 copy-start.6
  7.1 5.9 %copy-start = (bf16[1,128,1024]{2,1,0:T(8,128)(2,1)S(1)}, bf16[1,128,1024]{2,1,0:T(8,128)(2,1)}, u32[]{:S(2)}) copy-start(bf16[1,128,1024]{2,1,0:T(8,128)(2,1)} %param.21) | copy-start | bytes 786436
  7.1 5.9 %copy-start.1 = (f32[1024]{0:T(1024)S(1)}, f32[1024]{0:T(1024)}, u32[]{:S(2)}) copy-start(f32[1024]{0:T(1024)} %param.23) | copy-start | bytes 12292
  7.1 5.9 %copy-start.2 = (s32[32]{0:T(128)S(1)}, s32[32]{0:T(128)}, u32[]{:S(2)}) copy-start(s32[32]{0:T(128)} %lengths.7) | copy-start | bytes 388
  10.7 11.5 %collective-permute-start.4 = (bf16[80,1024]{1,0:T(8,128)(2,1)S(1)}, bf16[80,1024]{1,0:T(8,128)(2,1)S(1)}, u32[]{:S(2)}, u32[]{:S(2)}) collective-permute-start(bf16[80,1024]{1,0:T(8,128)(2,1)S(1)} %decoder_rows.1), channel_id=1, source_target_pairs={{0,0},{1,4},{2,8},{3,12},{4,16},{5,20},{6,24},{7,28},{8,1},{9,5},{... | collective-permute-start | bytes 491528 | tf_op jit(solution)/shard_map/ppermute | solution.py:471
  16.8 5.4 %copy-start.3 = (f32[1024]{0:T(1024)S(1)}, f32[1024]{0:T(1024)}, u32[]{:S(2)}) copy-start(f32[1024]{0:T(1024)} %param.34) | copy-start | bytes 12292
  16.8 6.2 %collective-permute-start.5 = (bf16[128,1024]{1,0:T(8,128)(2,1)S(1)}, bf16[128,1024]{1,0:T(8,128)(2,1)S(1)}, u32[]{:S(2)}, u32[]{:S(2)}) collective-permute-start(bf16[128,1024]{1,0:T(8,128)(2,1)S(1)} %collective-permute-done.3.refs_1_), channel_id=1, source_target_pairs={{0,1},{1,0},{2,3},{3,2},{4,5},{5,4},{6,7},{7,6},{8,9},{9,8},{10,11... | collective-permute-start | bytes 786440 | tf_op jit(solution)/shard_map/ppermute | solution.py:264
  20.4 14.3 %collective-permute-start.7 = (bf16[128,1024]{1,0:T(8,128)(2,1)S(1)}, bf16[128,1024]{1,0:T(8,128)(2,1)S(1)}, u32[]{:S(2)}, u32[]{:S(2)}) collective-permute-start(bf16[128,1024]{1,0:T(8,128)(2,1)S(1)} %collective-permute-done.3.refs_1_), channel_id=1, source_target_pairs={{0,2},{1,3},{2,0},{3,1},{4,6},{5,7},{6,4},{7,5},{8,10},{9,11},{10,... | collective-permute-start | bytes 786440 | tf_op jit(solution)/shard_map/ppermute | solution.py:264
  21.9 12.8 %collective-permute-start.8 = (bf16[128,1024]{1,0:T(8,128)(2,1)S(1)}, bf16[128,1024]{1,0:T(8,128)(2,1)S(1)}, u32[]{:S(2)}, u32[]{:S(2)}) collective-permute-start(bf16[128,1024]{1,0:T(8,128)(2,1)S(1)} %collective-permute-done.2.refs_1_), channel_id=1, source_target_pairs={{0,1},{1,0},{2,3},{3,2},{4,5},{5,4},{6,7},{7,6},{8,9},{9,8},{10,11... | collective-permute-start | bytes 786440 | tf_op jit(solution)/shard_map/ppermute | solution.py:264
  22.4 12.3 %collective-permute-start.6 = (bf16[64,1024]{1,0:T(8,128)(2,1)S(1)}, bf16[64,1024]{1,0:T(8,128)(2,1)S(1)}, u32[]{:S(2)}, u32[]{:S(2)}) collective-permute-start(bf16[64,1024]{1,0:T(8,128)(2,1)S(1)} %get-tuple-element.56.queries_in), channel_id=1, source_target_pairs={{0,2},{1,3},{2,0},{3,1},{4,6},{5,7},{6,4},{7,5},{8,10},{9,11},{10,... | collective-permute-start | bytes 393224 | tf_op jit(solution)/shard_map/ppermute | solution.py:264
  26.7 12.3 %collective-permute-start.14 = (bf16[128,1024]{1,0:T(8,128)(2,1)S(1)}, bf16[128,1024]{1,0:T(8,128)(2,1)S(1)}, u32[]{:S(2)}, u32[]{:S(2)}) collective-permute-start(bf16[128,1024]{1,0:T(8,128)(2,1)S(1)} %get-tuple-element.63), channel_id=1, source_target_pairs={{0,1},{1,0},{2,3},{3,2},{4,5},{5,4},{6,7},{7,6},{8,9},{9,8},{10,11... | collective-permute-start | bytes 786440 | tf_op jit(solution)/shard_map/ppermute | solution.py:264
  26.8 11.7 %collective-permute-start.11 = (bf16[64,1024]{1,0:T(8,128)(2,1)S(1)}, bf16[64,1024]{1,0:T(8,128)(2,1)S(1)}, u32[]{:S(2)}, u32[]{:S(2)}) collective-permute-start(bf16[64,1024]{1,0:T(8,128)(2,1)S(1)} %get-tuple-element.56.queries_in), channel_id=1, source_target_pairs={{0,4},{1,5},{2,6},{3,7},{4,0},{5,1},{6,2},{7,3},{8,12},{9,13},{10,... | collective-permute-start | bytes 393224 | tf_op jit(solution)/shard_map/ppermute | solution.py:264
  38.4 1.6 %collective-permute-start.12 = (bf16[128,1024]{1,0:T(8,128)(2,1)S(1)}, bf16[128,1024]{1,0:T(8,128)(2,1)S(1)}, u32[]{:S(2)}, u32[]{:S(2)}) collective-permute-start(bf16[128,1024]{1,0:T(8,128)(2,1)S(1)} %collective-permute-done.7.refs_1_), channel_id=1, source_target_pairs={{0,1},{1,0},{2,3},{3,2},{4,5},{5,4},{6,7},{7,6},{8,9},{9,8},{10,11... | collective-permute-start | bytes 786440 | tf_op jit(solution)/shard_map/ppermute | solution.py:264
  38.5 5.8 %collective-permute-start.9 = (bf16[128,1024]{1,0:T(8,128)(2,1)S(1)}, bf16[128,1024]{1,0:T(8,128)(2,1)S(1)}, u32[]{:S(2)}, u32[]{:S(2)}) collective-permute-start(bf16[128,1024]{1,0:T(8,128)(2,1)S(1)} %get-tuple-element.59), channel_id=1, source_target_pairs={{0,1},{1,0},{2,3},{3,2},{4,5},{5,4},{6,7},{7,6},{8,9},{9,8},{10,11... | collective-permute-start | bytes 786440 | tf_op jit(solution)/shard_map/ppermute | solution.py:264
  39.1 23.1 %copy-start.4 = (f32[1024]{0:T(1024)S(1)}, f32[1024]{0:T(1024)}, u32[]{:S(2)}) copy-start(f32[1024]{0:T(1024)} %param.29) | copy-start | bytes 12292
  39.1 8.4 %collective-permute-start.15 = (bf16[128,1024]{1,0:T(8,128)(2,1)S(1)}, bf16[128,1024]{1,0:T(8,128)(2,1)S(1)}, u32[]{:S(2)}, u32[]{:S(2)}) collective-permute-start(bf16[128,1024]{1,0:T(8,128)(2,1)S(1)} %add_convert_fusion.1), channel_id=1, source_target_pairs={{0,2},{1,3},{2,0},{3,1},{4,6},{5,7},{6,4},{7,5},{8,10},{9,11},{10,... | collective-permute-start | bytes 786440 | tf_op jit(solution)/shard_map/ppermute | solution.py:264
  43.8 3.7 %collective-permute-start.13 = (bf16[128,1024]{1,0:T(8,128)(2,1)S(1)}, bf16[128,1024]{1,0:T(8,128)(2,1)S(1)}, u32[]{:S(2)}, u32[]{:S(2)}) collective-permute-start(bf16[128,1024]{1,0:T(8,128)(2,1)S(1)} %get-tuple-element.62), channel_id=1, source_target_pairs={{0,1},{1,0},{2,3},{3,2},{4,5},{5,4},{6,7},{7,6},{8,9},{9,8},{10,11... | collective-permute-start | bytes 786440 | tf_op jit(solution)/shard_map/ppermute | solution.py:264
  44.0 3.6 %collective-permute-start.1 = (bf16[128,1024]{1,0:T(8,128)(2,1)S(1)}, bf16[128,1024]{1,0:T(8,128)(2,1)S(1)}, u32[]{:S(2)}, u32[]{:S(2)}) collective-permute-start(bf16[128,1024]{1,0:T(8,128)(2,1)S(1)} %get-tuple-element.50), channel_id=1, source_target_pairs={{0,1},{1,0},{2,3},{3,2},{4,5},{5,4},{6,7},{7,6},{8,9},{9,8},{10,11... | collective-permute-start | bytes 786440 | tf_op jit(solution)/shard_map/ppermute | solution.py:264
  47.6 19.5 %collective-permute-start.17 = (bf16[4,1024,1024]{2,1,0:T(8,128)(2,1)S(1)}, bf16[4,1024,1024]{2,1,0:T(8,128)(2,1)S(1)}, u32[]{:S(2)}, u32[]{:S(2)}) collective-permute-start(bf16[4,1024,1024]{2,1,0:T(8,128)(2,1)S(1)} %load_stack.1.refs_0_), channel_id=1, source_target_pairs={{0,1},{1,0},{2,3},{3,2},{4,5},{5,4},{6,7},{7,6},{8,9},{9,8},{10,11... | collective-permute-start | bytes 25165832 | tf_op jit(solution)/shard_map/ppermute | solution.py:264
  47.7 9.1 %collective-permute-start.10 = (bf16[128,1024]{1,0:T(8,128)(2,1)S(1)}, bf16[128,1024]{1,0:T(8,128)(2,1)S(1)}, u32[]{:S(2)}, u32[]{:S(2)}) collective-permute-start(bf16[128,1024]{1,0:T(8,128)(2,1)S(1)} %add_convert_fusion.2), channel_id=1, source_target_pairs={{0,2},{1,3},{2,0},{3,1},{4,6},{5,7},{6,4},{7,5},{8,10},{9,11},{10,... | collective-permute-start | bytes 786440 | tf_op jit(solution)/shard_map/ppermute | solution.py:264
  48.0 14.2 %collective-permute-start.16 = (bf16[128,1024]{1,0:T(8,128)(2,1)S(1)}, bf16[128,1024]{1,0:T(8,128)(2,1)S(1)}, u32[]{:S(2)}, u32[]{:S(2)}) collective-permute-start(bf16[128,1024]{1,0:T(8,128)(2,1)S(1)} %add_convert_fusion), channel_id=1, source_target_pairs={{0,6},{1,7},{2,4},{3,5},{4,2},{5,3},{6,0},{7,1},{8,14},{9,15},{10,... | collective-permute-start | bytes 786440 | tf_op jit(solution)/shard_map/ppermute | solution.py:264
  63.2 14.4 %collective-permute-start.19 = (bf16[128,1024]{1,0:T(8,128)(2,1)S(1)}, bf16[128,1024]{1,0:T(8,128)(2,1)S(1)}, u32[]{:S(2)}, u32[]{:S(2)}) collective-permute-start(bf16[128,1024]{1,0:T(8,128)(2,1)S(1)} %get-tuple-element.66.keys_in), channel_id=1, source_target_pairs={{0,4},{1,5},{2,6},{3,7},{4,0},{5,1},{6,2},{7,3},{8,12},{9,13},{10,... | collective-permute-start | bytes 786440 | tf_op jit(solution)/shard_map/ppermute | solution.py:264
  65.1 22.5 %collective-permute-start.22 = (bf16[64,1024]{1,0:T(8,128)(2,1)S(1)}, bf16[64,1024]{1,0:T(8,128)(2,1)S(1)}, u32[]{:S(2)}, u32[]{:S(2)}) collective-permute-start(bf16[64,1024]{1,0:T(8,128)(2,1)S(1)} %collective-permute-done.11.queries_in), channel_id=1, source_target_pairs={{0,2},{1,3},{2,0},{3,1},{4,6},{5,7},{6,4},{7,5},{8,10},{9,11},{10,... | collective-permute-start | bytes 393224 | tf_op jit(solution)/shard_map/ppermute | solution.py:264
  65.8 17.8 %collective-permute-start.18 = (bf16[128,1024]{1,0:T(8,128)(2,1)S(1)}, bf16[128,1024]{1,0:T(8,128)(2,1)S(1)}, u32[]{:S(2)}, u32[]{:S(2)}) collective-permute-start(bf16[128,1024]{1,0:T(8,128)(2,1)S(1)} %get-tuple-element.66.keys_in), channel_id=1, source_target_pairs={{0,2},{1,3},{2,0},{3,1},{4,6},{5,7},{6,4},{7,5},{8,10},{9,11},{10,... | collective-permute-start | bytes 786440 | tf_op jit(solution)/shard_map/ppermute | solution.py:264
  77.6 10.0 %collective-permute-start.21 = (bf16[128,1024]{1,0:T(8,128)(2,1)S(1)}, bf16[128,1024]{1,0:T(8,128)(2,1)S(1)}, u32[]{:S(2)}, u32[]{:S(2)}) collective-permute-start(bf16[128,1024]{1,0:T(8,128)(2,1)S(1)} %collective-permute-done.19.keys_in), channel_id=1, source_target_pairs={{0,2},{1,3},{2,0},{3,1},{4,6},{5,7},{6,4},{7,5},{8,10},{9,11},{10,... | collective-permute-start | bytes 786440 | tf_op jit(solution)/shard_map/ppermute | solution.py:264
  81.5 10.0 %collective-permute-start.23 = (bf16[64,1024]{1,0:T(8,128)(2,1)S(1)}, bf16[64,1024]{1,0:T(8,128)(2,1)S(1)}, u32[]{:S(2)}, u32[]{:S(2)}) collective-permute-start(bf16[64,1024]{1,0:T(8,128)(2,1)S(1)} %cross_attention.5), channel_id=1, source_target_pairs={{0,2},{1,3},{2,0},{3,1},{4,6},{5,7},{6,4},{7,5},{8,10},{9,11},{10,... | collective-permute-start | bytes 393224 | tf_op jit(solution)/shard_map/ppermute | solution.py:264
  83.6 17.8 %slice-start = ((s8[8388608]{0:T(1024)(128)(4,1)}), s8[4194304]{0:T(1024)(128)(4,1)S(1)}, s32[]{:S(2)}) async-start(s8[8388608]{0:T(1024)(128)(4,1)} %bitcast.8), calls=%async_computation | async-start | bytes 8388608
  83.6 17.8 %slice-start.2 = ((s8[8388608]{0:T(1024)(128)(4,1)}), s8[4194304]{0:T(1024)(128)(4,1)S(1)}, s32[]{:S(2)}) async-start(s8[8388608]{0:T(1024)(128)(4,1)} %bitcast.10), calls=%async_computation.2 | async-start | bytes 8388608
  87.4 11.0 %copy-start.5 = (f32[1024]{0:T(1024)S(1)}, f32[1024]{0:T(1024)}, u32[]{:S(2)}) copy-start(f32[1024]{0:T(1024)} %param.39) | copy-start | bytes 12292
  87.5 13.9 %slice-start.1 = ((s8[8388608]{0:T(1024)(128)(4,1)}), s8[4194304]{0:T(1024)(128)(4,1)S(1)}, s32[]{:S(2)}) async-start(s8[8388608]{0:T(1024)(128)(4,1)} %bitcast.8), calls=%async_computation.1 | async-start | bytes 8388608
  87.5 13.9 %slice-start.3 = ((s8[8388608]{0:T(1024)(128)(4,1)}), s8[4194304]{0:T(1024)(128)(4,1)S(1)}, s32[]{:S(2)}) async-start(s8[8388608]{0:T(1024)(128)(4,1)} %bitcast.10), calls=%async_computation.3 | async-start | bytes 8388608
  87.5 6.1 %collective-permute-start.20 = (bf16[64,1024]{1,0:T(8,128)(2,1)S(1)}, bf16[64,1024]{1,0:T(8,128)(2,1)S(1)}, u32[]{:S(2)}, u32[]{:S(2)}) collective-permute-start(bf16[64,1024]{1,0:T(8,128)(2,1)S(1)} %cross_attention.6), channel_id=1, source_target_pairs={{0,2},{1,3},{2,0},{3,1},{4,6},{5,7},{6,4},{7,5},{8,10},{9,11},{10,... | collective-permute-start | bytes 393224 | tf_op jit(solution)/shard_map/ppermute | solution.py:264
  91.5 6.9 %collective-permute-start.24 = (bf16[64,1024]{1,0:T(8,128)(2,1)S(1)}, bf16[64,1024]{1,0:T(8,128)(2,1)S(1)}, u32[]{:S(2)}, u32[]{:S(2)}) collective-permute-start(bf16[64,1024]{1,0:T(8,128)(2,1)S(1)} %add_convert_fusion.7), channel_id=1, source_target_pairs={{0,6},{1,7},{2,4},{3,5},{4,2},{5,3},{6,0},{7,1},{8,14},{9,15},{10,... | collective-permute-start | bytes 393224 | tf_op jit(solution)/shard_map/ppermute | solution.py:264
  98.6 2.7 %collective-permute-start.25 = (bf16[64,1024]{1,0:T(8,128)(2,1)S(1)}, bf16[64,1024]{1,0:T(8,128)(2,1)S(1)}, u32[]{:S(2)}, u32[]{:S(2)}) collective-permute-start(bf16[64,1024]{1,0:T(8,128)(2,1)S(1)} %get-tuple-element.73.refs_0_), channel_id=1, source_target_pairs={{0,1},{1,0},{2,3},{3,2},{4,5},{5,4},{6,7},{7,6},{8,9},{9,8},{10,11... | collective-permute-start | bytes 393224 | tf_op jit(solution)/shard_map/ppermute | solution.py:264
  98.7 9.7 %collective-permute-start.28 = (bf16[64,1024]{1,0:T(8,128)(2,1)S(1)}, bf16[64,1024]{1,0:T(8,128)(2,1)S(1)}, u32[]{:S(2)}, u32[]{:S(2)}) collective-permute-start(bf16[64,1024]{1,0:T(8,128)(2,1)S(1)} %get-tuple-element.73.refs_0_), channel_id=1, source_target_pairs={{0,4},{1,5},{2,6},{3,7},{4,0},{5,1},{6,2},{7,3},{8,12},{9,13},{10,... | collective-permute-start | bytes 393224 | tf_op jit(solution)/shard_map/ppermute | solution.py:264
  101.2 7.7 %collective-permute-start.27 = (bf16[64,1024]{1,0:T(8,128)(2,1)S(1)}, bf16[64,1024]{1,0:T(8,128)(2,1)S(1)}, u32[]{:S(2)}, u32[]{:S(2)}) collective-permute-start(bf16[64,1024]{1,0:T(8,128)(2,1)S(1)} %get-tuple-element.73.refs_0_), channel_id=1, source_target_pairs={{0,2},{1,3},{2,0},{3,1},{4,6},{5,7},{6,4},{7,5},{8,10},{9,11},{10,... | collective-permute-start | bytes 393224 | tf_op jit(solution)/shard_map/ppermute | solution.py:264
  108.4 1.3 collective-permute-start.29
  108.4 6.5 %collective-permute-start.33 = (bf16[64,1024]{1,0:T(8,128)(2,1)S(1)}, bf16[64,1024]{1,0:T(8,128)(2,1)S(1)}, u32[]{:S(2)}, u32[]{:S(2)}) collective-permute-start(bf16[64,1024]{1,0:T(8,128)(2,1)S(1)} %collective-permute-done.28.refs_0_), channel_id=1, source_target_pairs={{0,2},{1,3},{2,0},{3,1},{4,6},{5,7},{6,4},{7,5},{8,10},{9,11},{10,... | collective-permute-start | bytes 393224 | tf_op jit(solution)/shard_map/ppermute | solution.py:264
  108.4 15.0 %collective-permute-start.26 = (bf16[64,1024]{1,0:T(8,128)(2,1)S(1)}, bf16[64,1024]{1,0:T(8,128)(2,1)S(1)}, u32[]{:S(2)}, u32[]{:S(2)}) collective-permute-start(bf16[64,1024]{1,0:T(8,128)(2,1)S(1)} %get-tuple-element.75), channel_id=1, source_target_pairs={{0,1},{1,0},{2,3},{3,2},{4,5},{5,4},{6,7},{7,6},{8,9},{9,8},{10,11... | collective-permute-start | bytes 393224 | tf_op jit(solution)/shard_map/ppermute | solution.py:264
  108.9 3.5 %collective-permute-start.30 = (bf16[64,1024]{1,0:T(8,128)(2,1)S(1)}, bf16[64,1024]{1,0:T(8,128)(2,1)S(1)}, u32[]{:S(2)}, u32[]{:S(2)}) collective-permute-start(bf16[64,1024]{1,0:T(8,128)(2,1)S(1)} %collective-permute-done.27.refs_0_), channel_id=1, source_target_pairs={{0,1},{1,0},{2,3},{3,2},{4,5},{5,4},{6,7},{7,6},{8,9},{9,8},{10,11... | collective-permute-start | bytes 393224 | tf_op jit(solution)/shard_map/ppermute | solution.py:264
  112.2 3.3 %collective-permute-start.36 = (bf16[64,1024]{1,0:T(8,128)(2,1)S(1)}, bf16[64,1024]{1,0:T(8,128)(2,1)S(1)}, u32[]{:S(2)}, u32[]{:S(2)}) collective-permute-start(bf16[64,1024]{1,0:T(8,128)(2,1)S(1)} %get-tuple-element.85), channel_id=1, source_target_pairs={{0,1},{1,0},{2,3},{3,2},{4,5},{5,4},{6,7},{7,6},{8,9},{9,8},{10,11... | collective-permute-start | bytes 393224 | tf_op jit(solution)/shard_map/ppermute | solution.py:264
  114.9 2.0 %collective-permute-start.34 = (bf16[64,1024]{1,0:T(8,128)(2,1)S(1)}, bf16[64,1024]{1,0:T(8,128)(2,1)S(1)}, u32[]{:S(2)}, u32[]{:S(2)}) collective-permute-start(bf16[64,1024]{1,0:T(8,128)(2,1)S(1)} %collective-permute-done.33.refs_0_), channel_id=1, source_target_pairs={{0,1},{1,0},{2,3},{3,2},{4,5},{5,4},{6,7},{7,6},{8,9},{9,8},{10,11... | collective-permute-start | bytes 393224 | tf_op jit(solution)/shard_map/ppermute | solution.py:264
  115.3 4.0 %collective-permute-start.31 = (bf16[64,1024]{1,0:T(8,128)(2,1)S(1)}, bf16[64,1024]{1,0:T(8,128)(2,1)S(1)}, u32[]{:S(2)}, u32[]{:S(2)}) collective-permute-start(bf16[64,1024]{1,0:T(8,128)(2,1)S(1)} %get-tuple-element.81), channel_id=1, source_target_pairs={{0,1},{1,0},{2,3},{3,2},{4,5},{5,4},{6,7},{7,6},{8,9},{9,8},{10,11... | collective-permute-start | bytes 393224 | tf_op jit(solution)/shard_map/ppermute | solution.py:264
  115.5 5.8 %collective-permute-start.37 = (bf16[64,1024]{1,0:T(8,128)(2,1)S(1)}, bf16[64,1024]{1,0:T(8,128)(2,1)S(1)}, u32[]{:S(2)}, u32[]{:S(2)}) collective-permute-start(bf16[64,1024]{1,0:T(8,128)(2,1)S(1)} %add_convert_fusion.5), channel_id=1, source_target_pairs={{0,2},{1,3},{2,0},{3,1},{4,6},{5,7},{6,4},{7,5},{8,10},{9,11},{10,... | collective-permute-start | bytes 393224 | tf_op jit(solution)/shard_map/ppermute | solution.py:264
  119.3 2.1 %collective-permute-start.35 = (bf16[64,1024]{1,0:T(8,128)(2,1)S(1)}, bf16[64,1024]{1,0:T(8,128)(2,1)S(1)}, u32[]{:S(2)}, u32[]{:S(2)}) collective-permute-start(bf16[64,1024]{1,0:T(8,128)(2,1)S(1)} %get-tuple-element.84), channel_id=1, source_target_pairs={{0,1},{1,0},{2,3},{3,2},{4,5},{5,4},{6,7},{7,6},{8,9},{9,8},{10,11... | collective-permute-start | bytes 393224 | tf_op jit(solution)/shard_map/ppermute | solution.py:264
  119.4 6.0 %collective-permute-start.32 = (bf16[64,1024]{1,0:T(8,128)(2,1)S(1)}, bf16[64,1024]{1,0:T(8,128)(2,1)S(1)}, u32[]{:S(2)}, u32[]{:S(2)}) collective-permute-start(bf16[64,1024]{1,0:T(8,128)(2,1)S(1)} %add_convert_fusion.6), channel_id=1, source_target_pairs={{0,2},{1,3},{2,0},{3,1},{4,6},{5,7},{6,4},{7,5},{8,10},{9,11},{10,... | collective-permute-start | bytes 393224 | tf_op jit(solution)/shard_map/ppermute | solution.py:264
  121.4 7.6 %collective-permute-start.38 = (bf16[64,1024]{1,0:T(8,128)(2,1)S(1)}, bf16[64,1024]{1,0:T(8,128)(2,1)S(1)}, u32[]{:S(2)}, u32[]{:S(2)}) collective-permute-start(bf16[64,1024]{1,0:T(8,128)(2,1)S(1)} %add_convert_fusion.4), channel_id=1, source_target_pairs={{0,6},{1,7},{2,4},{3,5},{4,2},{5,3},{6,0},{7,1},{8,14},{9,15},{10,... | collective-permute-start | bytes 393224 | tf_op jit(solution)/shard_map/ppermute | solution.py:264
  129.0 13.3 %collective-permute-start.39 = (bf16[64,1024]{1,0:T(8,128)(2,1)S(1)}, bf16[64,1024]{1,0:T(8,128)(2,1)S(1)}, u32[]{:S(2)}, u32[]{:S(2)}) collective-permute-start(bf16[64,1024]{1,0:T(8,128)(2,1)S(1)} %add_convert_fusion.3), channel_id=1, source_target_pairs={{0,0},{4,1},{8,2},{12,3},{16,4},{20,5},{24,6},{28,7},{1,8},{5,9},{... | collective-permute-start | bytes 393224 | tf_op jit(solution)/shard_map/ppermute | solution.py:531
